TPU v7x, 32 devices: a whole 2x2x4 slice. The times are simulated.
32 devices in a mesh: seq: 4 (over z), guid: 2 (over core), tp: 4 (over y, x).
Axes of the slice: x: 2, y: 2, z: 4, core: 2. Of those that a mesh axis runs over, the one named last changes fastest.
Arguments:
- hidden_states: bfloat16 [2, 1536, 3072], P('guid', 'seq'), may hold values from -6 to 6
- modulation: float32 [2, 3, 3072], P('guid')
- w_query: bfloat16 [3072, 3072], P(None, 'tp'), may hold values from -0.109375 to 0.109375
- w_key: bfloat16 [3072, 3072], P(None, 'tp'), may hold values from -0.109375 to 0.109375
- w_value: bfloat16 [3072, 3072], P(None, 'tp'), may hold values from -0.109375 to 0.109375
- w_out: bfloat16 [3072, 3072], P('tp'), may hold values from -0.109375 to 0.109375
- block_ids: int32 [12, 7], P('seq'), may hold values from 0 to 11, as said below
- block_count: int32 [12], P('seq'), may hold values from 1 to 7, as said below
- guidance: float32 [1], replicated, may hold values from 4 to 8
Outputs:
- guided: bfloat16 [1536, 3072], P('seq', ('guid', 'tp'))
Inputs may be any that keep to these rules, and one draw needn't show every extreme that they name: `block_ids`: entry 0 of each list is the query tile itself; the first block_count entries are distinct tiles within 3 tiles of the query tile; later entries repeat the query tile. `block_count`: some query tile lists 7 tiles.
All inputs are finite; a program needn't handle non-finite values.
Results may differ from a plain program's by a relative error of at most 0.02.
The roundings to bfloat16 on the way count: a program that leaves them out, or rounds other values in their place, can miss the bound.
Values may be sent and summed in bfloat16 or wider, within the bound.
No kernel may reach another device: no remote copies, remote signals or barrier semaphores. Data moves between devices by JAX's collectives and lax.ppermute only.
A program may use at most 192 MiB of HBM per device.

v0:
```python
import jax
import jax.numpy as jnp
from jax import lax
from jax.sharding import PartitionSpec as P

HD = 64


def shifted(block, axis, distance):
    devices = range(lax.axis_size(axis))
    route = [(i - distance, i) for i in devices if i - distance in devices]
    return lax.ppermute(block, axis, route)


def swapped(value, axis, distance):
    return lax.ppermute(value, axis, [(i, i ^ 1 << distance) for i in range(lax.axis_size(axis))])


def tile_mask(block_ids, block_count, first_tile, tiles_here):
    key_tiles = first_tile + jnp.arange(tiles_here, dtype=jnp.int32)
    live = jnp.arange(block_ids.shape[1], dtype=jnp.int32)[None, :] < block_count[:, None]
    hit = (block_ids[:, :, None] == key_tiles[None, None, :]) & live[:, :, None]
    return jnp.any(hit, axis=1)


def shards(
    hidden_states, modulation, w_query, w_key, w_value, w_out, block_ids, block_count, guidance
):
    states = hidden_states[0]
    modul = modulation[0]
    ntok = states.shape[0]
    tiles_here = block_ids.shape[0]
    tile_len = ntok // tiles_here
    width = w_query.shape[1]
    heads_here = width // HD
    xf = states.astype(jnp.float32)
    mean = jnp.mean(xf, axis=1, keepdims=True)
    var = jnp.mean((xf - mean) ** 2, axis=1, keepdims=True)
    normed = (xf - mean) / jnp.sqrt(var + 1e-05)
    h = (normed * (1.0 + modul[1]) + modul[0]).astype(jnp.bfloat16)
    query = (
        jnp.dot(h, w_query, preferred_element_type=jnp.float32)
        .astype(jnp.bfloat16)
        .reshape(ntok, heads_here, HD)
    )
    keys = jnp.dot(h, w_key, preferred_element_type=jnp.float32).astype(jnp.bfloat16)
    values = jnp.dot(h, w_value, preferred_element_type=jnp.float32).astype(jnp.bfloat16)
    key_value = jnp.stack([keys, values])
    seq_count = lax.axis_size("seq")
    seq_here = lax.axis_index("seq")
    reach_dev = min(4, (seq_count - 1) // 2)

    def attend(carry, piece, mask):
        run_max, run_sum, run_acc = carry
        near_k = piece[0].reshape(ntok, heads_here, HD)
        near_v = piece[1].reshape(ntok, heads_here, HD)
        scores = (
            jnp.einsum("qhd,khd->hqk", query, near_k, preferred_element_type=jnp.float32) * 0.125
        )
        scores = jnp.where(mask[None], scores, -1e30)
        new_max = jnp.maximum(run_max, jnp.max(scores, axis=2))
        expo = jnp.where(mask[None], jnp.exp(scores - new_max[:, :, None]), 0.0)
        factor = jnp.exp(run_max - new_max)
        new_sum = run_sum * factor + jnp.sum(expo, axis=2)
        added = jnp.einsum(
            "hqk,khd->hqd", expo.astype(jnp.bfloat16), near_v, preferred_element_type=jnp.float32
        )
        return (new_max, new_sum, run_acc * factor[:, :, None] + added)

    def visit(carry, piece, owner):
        tiles_ok = tile_mask(block_ids, block_count, owner * tiles_here, tiles_here)
        mask = jnp.repeat(jnp.repeat(tiles_ok, tile_len, axis=0), tile_len, axis=1)
        return attend(carry, piece, mask)

    carry = (
        jnp.full((heads_here, ntok), -1e30, jnp.float32),
        jnp.zeros((heads_here, ntok), jnp.float32),
        jnp.zeros((heads_here, ntok, HD), jnp.float32),
    )
    carry = visit(carry, key_value, seq_here)
    offsets = []
    for distance in range(1, reach_dev + 1):
        offsets.append(distance)
        offsets.append(-distance)
    for offset in offsets:
        piece = shifted(key_value, "seq", offset)
        carry = visit(carry, piece, seq_here - offset)
    attn = (carry[2] / carry[1][:, :, None]).astype(jnp.bfloat16)
    attn = jnp.transpose(attn, (1, 0, 2)).reshape(ntok, width)
    proj = jnp.dot(attn, w_out, preferred_element_type=jnp.float32)
    scale_now = guidance[0]
    branch = lax.axis_index("guid")
    tp_count = lax.axis_size("tp")
    tp_here = lax.axis_index("tp")
    model_width = states.shape[1]
    half = model_width // (2 * tp_count)

    def regroup(array):
        count = array.shape[0]
        return jnp.transpose(array.reshape(count, 2, tp_count, half), (0, 2, 1, 3)).reshape(
            count, model_width
        )

    shares = lax.psum_scatter(
        regroup(proj).astype(jnp.bfloat16), "tp", scatter_dimension=1, tiled=True
    ).astype(jnp.float32)
    x_part = lax.dynamic_slice_in_dim(regroup(xf), tp_here * 2 * half, 2 * half, 1)
    gate_part = lax.dynamic_slice_in_dim(
        regroup(modul[2][None, :]), tp_here * 2 * half, 2 * half, 1
    )
    block = (x_part + gate_part * shares).reshape(ntok, 2, half)
    own = lax.dynamic_slice_in_dim(block, branch, 1, 1)[:, 0]
    outgoing = lax.dynamic_slice_in_dim(block, 1 - branch, 1, 1)[:, 0]
    other = swapped(outgoing.astype(jnp.bfloat16), "guid", 0).astype(outgoing.dtype)
    cond = jnp.where(branch == 0, own, other)
    uncond = jnp.where(branch == 0, other, own)
    return (uncond + scale_now * (cond - uncond)).astype(jnp.bfloat16)


def solution(mesh):
    in_specs = (
        P("guid", "seq", None),
        P("guid", None, None),
        P(None, "tp"),
        P(None, "tp"),
        P(None, "tp"),
        P("tp", None),
        P("seq", None),
        P("seq"),
        P(),
    )
    out_specs = P("seq", ("guid", "tp"))
    return jax.shard_map(shards, mesh=mesh, in_specs=in_specs, out_specs=out_specs, check_vma=False)
```

profile of v0, /device:TPU:0, one launch (start us, length us, event | category | flops | bytes accessed | tf_op | source)
XLA Modules:
  0.0 126.0 jit_solution(9352463198692702545)
XLA Ops:
  6.5 3.0 %copy.56 = bf16[1,384,3072]{1,2,0:T(8,128)(2,1)S(1)} copy(bf16[1,384,3072]{2,1,0:T(8,128)(2,1)} %param.9) | data formatting | bytes 4718592 | tf_op args[0]
  11.1 3.7 %add_convert_fusion = bf16[384,3072]{0,1:T(8,128)(2,1)S(1)} fusion(bf16[1,384,3072]{1,2,0:T(8,128)(2,1)} %copy-done, f32[3072]{0:T(1024)S(1)} %bitcast.177, f32[3072]{0:T(1024)S(1)} %bitcast.178, f32[384]{0:T(512)S(1)} %add_sqrt_fusion, f32[384]{0:T(512)S(1)} %broadcast_multiply_fusion), kind=kLoop, calls=%fused_computation.16 | loop fusion | flops 7077888 | bytes 4746240 | tf_op jit(solution)/shard_map/convert_element_type | solution.py:40
  14.8 2.1 %convolution_convert_fusion.1 = bf16[384,768]{1,0:T(8,128)(2,1)S(1)} fusion(bf16[384,3072]{0,1:T(8,128)(2,1)S(1)} %add_convert_fusion, bf16[3072,768]{1,0:T(8,128)(2,1)S(1)} %copy-done.2), kind=kOutput, calls=%fused_computation.35 | convolution fusion | flops 1812234240 | bytes 7667712 | tf_op jit(solution)/shard_map/dot_general | solution.py:46
  16.9 2.1 %convolution_convert_fusion = bf16[384,768]{1,0:T(8,128)(2,1)S(1)} fusion(bf16[384,3072]{0,1:T(8,128)(2,1)S(1)} %add_convert_fusion, bf16[3072,768]{1,0:T(8,128)(2,1)S(1)} %bitcast.147), kind=kOutput, calls=%fused_computation.34 | convolution fusion | flops 1812234240 | bytes 7667712 | tf_op jit(solution)/shard_map/dot_general | solution.py:47
  20.2 6.0 %collective-permute-start = (bf16[2,384,768]{2,1,0:T(8,128)(2,1)}, bf16[2,384,768]{2,1,0:T(8,128)(2,1)}, u32[]{:S(2)}, u32[]{:S(2)}) collective-permute-start(bf16[2,384,768]{2,1,0:T(8,128)(2,1)} %pad_maximum_fusion), channel_id=1, source_target_pairs={{0,8},{8,16},{16,24},{1,9},{9,17},{17,25},{2,10},{10,18},{18,26},{... | collective-permute-start | bytes 3538952 | tf_op jit(solution)/shard_map/ppermute | solution.py:12
  27.5 5.2 %convolution_convert_fusion.2 = bf16[384,768]{1,0:T(8,128)(2,1)} fusion(bf16[384,3072]{0,1:T(8,128)(2,1)S(1)} %add_convert_fusion, bf16[3072,768]{1,0:T(8,128)(2,1)} %param.11), kind=kOutput, calls=%fused_computation.36 | convolution fusion | flops 1812234240 | bytes 7667712 | tf_op jit(solution)/shard_map/dot_general | solution.py:42
  34.6 1.4 %copy.60 = bf16[384,768]{0,1:T(8,128)(2,1)S(1)} copy(bf16[384,768]{1,0:T(8,128)(2,1)} %convolution_convert_fusion.2) | data formatting | bytes 1179648 | tf_op jit(solution)/shard_map/convert_element_type | solution.py:43
  37.0 6.7 %copy.81 = bf16[3072,768]{1,0:T(8,128)(2,1)} copy(bf16[3072,768]{0,1:T(8,128)(2,1)} %bitcast.155) | data formatting | bytes 9437184 | tf_op jit(solution)/shard_map/dot_general | solution.py:90
  43.8 4.7 %fusion = (f32[12,384]{1,0:T(8,128)}, f32[12,384,384]{1,2,0:T(8,128)}) fusion(pred[384,384]{0,1:T(8,128)(4,1)S(1)} %bitcast.164, bf16[384,12,64]{0,2,1:T(8,128)(2,1)S(1)} %bitcast.148, bf16[384,12,64]{0,2,1:T(8,128)(2,1)S(1)} %bitcast.161), kind=kOutput, calls=%fused_computation.6 | convolution fusion | flops 231796224 | bytes 8423424 | tf_op jit(solution)/shard_map/qhd,khd->hqk/dot_general | solution.py:58
  48.5 2.1 %collective-permute-done = bf16[2,384,768]{2,1,0:T(8,128)(2,1)} collective-permute-done((bf16[2,384,768]{2,1,0:T(8,128)(2,1)}, bf16[2,384,768]{2,1,0:T(8,128)(2,1)}, u32[]{:S(2)}, u32[]{:S(2)}) %collective-permute-start) | collective-permute-done | bytes 1179680 | tf_op jit(solution)/shard_map/ppermute | solution.py:12
  52.3 3.5 %collective-permute-done.1 = bf16[2,384,768]{2,1,0:T(8,128)(2,1)} collective-permute-done((bf16[2,384,768]{2,1,0:T(8,128)(2,1)}, bf16[2,384,768]{2,1,0:T(8,128)(2,1)}, u32[]{:S(2)}, u32[]{:S(2)}) %collective-permute-start.1) | collective-permute-done | bytes 1179680 | tf_op jit(solution)/shard_map/ppermute | solution.py:12
  55.8 1.3 %fusion.68 = (bf16[1,384,768]{2,1,0:T(8,128)(2,1)S(1)}, bf16[1,384,768]{2,1,0:T(8,128)(2,1)S(1)}) fusion(bf16[2,384,768]{2,1,0:T(8,128)(2,1)} %collective-permute-done.1), kind=kLoop, calls=%fused_computation.92 | loop fusion | bytes 2359296 | tf_op jit(solution)/shard_map/slice | solution.py:56
  61.4 1.7 %fusion.3 = f32[12,384]{1,0:T(8,128)S(1)} fusion(f32[12,384,384]{1,2,0:T(8,128)S(1)} %bitcast.144, f32[12,384]{1,0:T(8,128)S(1)} %get-tuple-element.21, pred[384,384]{0,1:T(8,128)(4,1)S(1)} %bitcast.165), kind=kLoop, calls=%fused_computation.9 | loop fusion | flops 8842752 | bytes 7262208 | tf_op jit(solution)/shard_map/reduce_sum | solution.py:64
  63.1 1.7 %fusion.5 = f32[12,384]{1,0:T(8,128)S(1)} fusion(f32[12,384,384]{1,2,0:T(8,128)S(1)} %get-tuple-element.25, f32[12,384]{1,0:T(8,128)S(1)} %get-tuple-element.11, pred[384,384]{0,1:T(8,128)(4,1)S(1)} %bitcast.171), kind=kLoop, calls=%fused_computation.11 | loop fusion | flops 8842752 | bytes 7262208 | tf_op jit(solution)/shard_map/reduce_sum | solution.py:64
  64.8 1.7 %fusion.7 = f32[12,384]{1,0:T(8,128)S(1)} fusion(f32[12,384,384]{1,2,0:T(8,128)S(1)} %get-tuple-element.23, f32[12,384]{1,0:T(8,128)S(1)} %get-tuple-element.10, pred[384,384]{0,1:T(8,128)(4,1)S(1)} %bitcast.168), kind=kLoop, calls=%fused_computation.13 | loop fusion | flops 8842752 | bytes 7262208 | tf_op jit(solution)/shard_map/reduce_sum | solution.py:64
  66.5 2.4 %fusion.36 = f32[384,12,64]{0,2,1:T(8,128)S(1)} fusion(bf16[384,12,64]{0,2,1:T(8,128)(2,1)S(1)} %bitcast.173, f32[12,384,384]{1,2,0:T(8,128)S(1)} %bitcast.144, f32[12,384]{1,0:T(8,128)S(1)} %get-tuple-element.21, pred[384,384]{0,1:T(8,128)(4,1)S(1)} %bitcast.166, f32[384,12]{0,1:T(8,128)S(1)} %get-tuple-element.16, f32[384,12]{0,1:T(8,128)S(1)} %get-tuple-element.20), kind=kOutput, calls=%fused_computation.32 | convolution fusion | flops 235929600 | bytes 9050112 | tf_op jit(solution)/shard_map/hqk,khd->hqd/dot_general | solution.py:65
  69.0 2.2 %fusion.39 = f32[384,12,64]{0,2,1:T(8,128)S(1)} fusion(f32[384,12,64]{0,2,1:T(8,128)S(1)} %fusion.36, bf16[384,12,64]{0,2,1:T(8,128)(2,1)S(1)} %bitcast.175, f32[12,384,384]{1,2,0:T(8,128)S(1)} %get-tuple-element.25, f32[12,384]{1,0:T(8,128)S(1)} %get-tuple-element.11, pred[384,384]{0,1:T(8,128)(4,1)S(1)} %bitcast.172, f32[384,12]{0,1:T(8,128)S(1)} %get-tuple-element.9), kind=kOutput, calls=%fused_computation.33 | convolution fusion | flops 235929600 | bytes 10211328 | tf_op jit(solution)/shard_map/hqk,khd->hqd/dot_general | solution.py:65
  71.2 2.3 %divide_convert_fusion = bf16[384,12,64]{0,2,1:T(8,128)(2,1)S(1)} fusion(f32[384,12,64]{0,2,1:T(8,128)S(1)} %fusion.39, bf16[384,12,64]{0,2,1:T(8,128)(2,1)S(1)} %bitcast.174, f32[12,384,384]{1,2,0:T(8,128)S(1)} %get-tuple-element.23, f32[12,384]{1,0:T(8,128)S(1)} %get-tuple-element.10, pred[384,384]{0,1:T(8,128)(4,1)S(1)} %bitcast.169, ...), kind=kOutput, calls=%fused_computation.39 | convolution fusion | flops 236224512 | bytes 9621504 | tf_op jit(solution)/shard_map/hqk,khd->hqd/dot_general | solution.py:65
  73.5 2.8 %convert_bitcast_fusion = bf16[384,4,2,384]{0,3,1,2:T(8,128)(2,1)S(1)} fusion(bf16[384,768,1,1]{0,1,3,2:T(8,128)(2,1)S(1)} %bitcast.182, bf16[2,4,384,768]{3,2,1,0:T(8,128)(2,1)S(1)} %bitcast.158), kind=kOutput, calls=%fused_computation.25 | convolution fusion | flops 1813118976 | bytes 7667712 | tf_op jit(solution)/shard_map/dot_general | solution.py:90
  76.4 1.6 %copy.74 = bf16[384,4,2,384]{0,3,2,1:T(8,128)(2,1)} copy(bf16[384,4,2,384]{0,3,1,2:T(8,128)(2,1)S(1)} %convert_bitcast_fusion) | data formatting | bytes 4718592 | tf_op jit(solution)/shard_map/convert_element_type | solution.py:105
  78.9 2.5 %reshape.162 = f32[1,384,3072]{1,2,0:T(8,128)} convert(bf16[1,384,3072]{1,2,0:T(8,128)(2,1)S(1)} %copy-done.1) | non-fusion elementwise | flops 1179648 | bytes 7077888 | tf_op jit(solution)/shard_map/reshape | solution.py:100
  81.4 4.8 %copy.57 = f32[384,4,2,384]{0,3,2,1:T(8,128)} copy(f32[384,4,2,384]{0,3,1,2:T(8,128)} %bitcast.145) | data formatting | bytes 9437184 | tf_op jit(solution)/shard_map/reshape | solution.py:100
  86.2 28.6 %reduce-scatter.2.cloned.1.call-done = bf16[384,768]{0,1:T(8,128)(2,1)} async-done(((bf16[384,3072]{0,1:T(8,128)(2,1)}), bf16[384,768]{0,1:T(8,128)(2,1)}) %reduce-scatter.2.cloned.1.call-update) | async-done | bytes 589840 | tf_op jit(solution)/shard_map/reduce_scatter | solution.py:104
  114.8 1.7 %multiply_add_fusion = f32[384,768]{0,1:T(8,128)S(1)} fusion(bf16[384,768]{0,1:T(8,128)(2,1)} %reduce-scatter.2.cloned.1.call-done, f32[384,3072]{0,1:T(8,128)} %bitcast.152, s32[]{:T(128)S(6)} %select_n.42, f32[768]{0:T(1024)S(1)} %dynamic-slice_reduce_fusion), kind=kLoop, calls=%fused_computation.38 | loop fusion | flops 884736 | bytes 2952196 | tf_op jit(solution)/shard_map/add | solution.py:111
  (82 shorter events, 15.8 us)
Async XLA Ops:
  6.5 4.2 %copy-start.7 = (f32[1,3,3072]{2,0,1:T(1,128)S(1)}, f32[1,3,3072]{2,0,1:T(1,128)}, u32[]{:S(2)}) copy-start(f32[1,3,3072]{2,0,1:T(1,128)} %param.10) | copy-start | bytes 110596
  6.5 108.2 %reduce-scatter.2.cloned.1.call-start = ((), (), s32[]{:S(2)}) async-start(), calls=%async_computation.1 | async-start | bytes 2949120 | tf_op jit(solution)/shard_map/reduce_scatter | solution.py:104
  9.6 1.5 %copy-start = (bf16[1,384,3072]{1,2,0:T(8,128)(2,1)}, bf16[1,384,3072]{1,2,0:T(8,128)(2,1)S(1)}, u32[]{:S(2)}) copy-start(bf16[1,384,3072]{1,2,0:T(8,128)(2,1)S(1)} %copy.56) | copy-start | bytes 7077892
  9.6 5.2 %copy-start.2 = (bf16[3072,768]{1,0:T(8,128)(2,1)S(1)}, bf16[3072,768]{1,0:T(8,128)(2,1)}, u32[]{:S(2)}) copy-start(bf16[3072,768]{1,0:T(8,128)(2,1)} %param.12) | copy-start | bytes 14155780
  11.1 5.8 %slice-start.2 = ((s8[4718592]{0:T(1024)(128)(4,1)}), s8[4194304]{0:T(1024)(128)(4,1)S(1)}, s32[]{:S(2)}) async-start(s8[4718592]{0:T(1024)(128)(4,1)} %bitcast.146), calls=%async_computation.4 | async-start | bytes 8388608
  14.8 2.1 %slice-start.3 = ((s8[4718592]{0:T(1024)(128)(4,1)}), s8[524288]{0:T(1024)(128)(4,1)S(1)}, s32[]{:S(2)}) async-start(s8[4718592]{0:T(1024)(128)(4,1)} %bitcast.146), calls=%async_computation.5 | async-start | bytes 1048576
  16.9 10.5 %copy-start.10 = (s32[3]{0:T(128)S(1)}, s32[3]{0:T(128)}, u32[]{:S(2)}) copy-start(s32[3]{0:T(128)} %param.16) | copy-start | bytes 40
  20.2 30.4 %collective-permute-start = (bf16[2,384,768]{2,1,0:T(8,128)(2,1)}, bf16[2,384,768]{2,1,0:T(8,128)(2,1)}, u32[]{:S(2)}, u32[]{:S(2)}) collective-permute-start(bf16[2,384,768]{2,1,0:T(8,128)(2,1)} %pad_maximum_fusion), channel_id=1, source_target_pairs={{0,8},{8,16},{16,24},{1,9},{9,17},{17,25},{2,10},{10,18},{18,26},{... | collective-permute-start | bytes 3538952 | tf_op jit(solution)/shard_map/ppermute | solution.py:12
  26.1 29.6 %collective-permute-start.1 = (bf16[2,384,768]{2,1,0:T(8,128)(2,1)}, bf16[2,384,768]{2,1,0:T(8,128)(2,1)}, u32[]{:S(2)}, u32[]{:S(2)}) collective-permute-start(bf16[2,384,768]{2,1,0:T(8,128)(2,1)} %pad_maximum_fusion), channel_id=1, source_target_pairs={{8,0},{16,8},{24,16},{9,1},{17,9},{25,17},{10,2},{18,10},{26,18},{... | collective-permute-start | bytes 3538952 | tf_op jit(solution)/shard_map/ppermute | solution.py:12
  27.5 5.2 %copy-start.9 = (s32[3,7]{1,0:T(4,128)S(1)}, s32[3,7]{1,0:T(4,128)}, u32[]{:S(2)}) copy-start(s32[3,7]{1,0:T(4,128)} %param.15) | copy-start | bytes 256
  43.7 8.2 %copy-start.3 = (pred[384,3,128]{0,2,1:T(8,128)(4,1)}, pred[384,3,128]{0,2,1:T(8,128)(4,1)S(1)}, u32[]{:S(2)}) copy-start(pred[384,3,128]{0,2,1:T(8,128)(4,1)S(1)} %broadcast_in_dim.98) | copy-start | bytes 442372
  58.0 1.3 %copy-start.8 = (pred[1,3,3,128]{3,1,2,0:T(4,128)(4,1)S(1)}, pred[1,3,3,128]{3,1,2,0:T(4,128)(4,1)}, u32[]{:S(2)}) copy-start(pred[1,3,3,128]{3,1,2,0:T(4,128)(4,1)} %copy.90) | copy-start | bytes 3460
  58.1 2.6 %slice-start = ((s8[7077888]{0:T(1024)(128)(4,1)}), s8[4194304]{0:T(1024)(128)(4,1)S(1)}, s32[]{:S(2)}) async-start(s8[7077888]{0:T(1024)(128)(4,1)} %bitcast.143), calls=%async_computation.2 | async-start | bytes 8388608
  59.3 1.3 %copy-start.6 = (f32[12,384]{1,0:T(8,128)S(1)}, f32[12,384]{1,0:T(8,128)}, u32[]{:S(2)}) copy-start(f32[12,384]{1,0:T(8,128)} %get-tuple-element.26) | copy-start | bytes 55300
  59.3 1.4 %copy-start.4 = (pred[384,3,128]{0,2,1:T(8,128)(4,1)S(1)}, pred[384,3,128]{0,2,1:T(8,128)(4,1)}, u32[]{:S(2)}) copy-start(pred[384,3,128]{0,2,1:T(8,128)(4,1)} %copy-done.3) | copy-start | bytes 442372
  59.4 2.0 %slice-start.1 = ((s8[7077888]{0:T(1024)(128)(4,1)}), s8[2883584]{0:T(1024)(128)(4,1)S(1)}, s32[]{:S(2)}) async-start(s8[7077888]{0:T(1024)(128)(4,1)} %bitcast.143), calls=%async_computation.3 | async-start | bytes 5767168
  64.8 1.7 %copy-start.5 = (bf16[384,768]{0,1:T(8,128)(2,1)S(1)}, bf16[384,768]{0,1:T(8,128)(2,1)}, u32[]{:S(2)}) copy-start(bf16[384,768]{0,1:T(8,128)(2,1)} %copy.62) | copy-start | bytes 1769476
  69.0 4.5 %slice-start.4 = ((s8[4718592]{0:T(1024)(128)(4,1)}), s8[4194304]{0:T(1024)(128)(4,1)S(1)}, s32[]{:S(2)}) async-start(s8[4718592]{0:T(1024)(128)(4,1)} %bitcast.156), calls=%async_computation.6 | async-start | bytes 8388608
  71.2 2.3 %slice-start.5 = ((s8[4718592]{0:T(1024)(128)(4,1)}), s8[524288]{0:T(1024)(128)(4,1)S(1)}, s32[]{:S(2)}) async-start(s8[4718592]{0:T(1024)(128)(4,1)} %bitcast.156), calls=%async_computation.7 | async-start | bytes 1048576
  76.3 2.5 %copy-start.1 = (bf16[1,384,3072]{1,2,0:T(8,128)(2,1)S(1)}, bf16[1,384,3072]{1,2,0:T(8,128)(2,1)}, u32[]{:S(2)}) copy-start(bf16[1,384,3072]{1,2,0:T(8,128)(2,1)} %copy-done) | copy-start | bytes 7077892
  116.5 1.6 %collective-permute-start.2 = (bf16[384,384]{0,1:T(8,128)(2,1)S(1)}, bf16[384,384]{0,1:T(8,128)(2,1)S(1)}, u32[]{:S(2)}, u32[]{:S(2)}) collective-permute-start(bf16[384,384]{0,1:T(8,128)(2,1)S(1)} %fusion.48), channel_id=1, source_target_pairs={{0,4},{4,0},{1,5},{5,1},{2,6},{6,2},{3,7},{7,3},{8,12},{12,8},{9,1... | collective-permute-start | bytes 884744 | tf_op jit(solution)/shard_map/ppermute | solution.py:16
Sparse Core Ops, SparseCore 0:
  78.1 36.5 reduce-scatter.1
where the time goes:
time: 127 us; the launch traced here: 126 us
  waiting for transfers between devices  35.1 us (28%)
  local copies, waits for them, and re-layouts  27 us (21%)
  matrix products  26.3 us (21%)
  other arithmetic  15.8 us (12%)
  between operations  14.5 us (11%)
  starting transfers between devices  7.31 us (6%)
    reduce_scatter x1, waiting for transfers between devices, shards(): lax.psum_scatter(regroup(proj).astype(jnp.bfloat16), 'tp', scatter_dimens...  28.6 us
    ppermute x2, starting transfers between devices, shifted(): return lax.ppermute(block, axis, route)  7.24 us
    dot_general x3, matrix products, attend(): jnp.einsum('qhd,khd->hqk', query, near_k, preferred_element_type=jnp.floa...  7.21 us
    dot_general x3, matrix products, attend(): jnp.einsum('hqk,khd->hqd', expo.astype(jnp.bfloat16), near_v, preferred_e...  6.92 us
    dot_general x1, local copies, waits for them, and re-layouts, shards(): proj = jnp.dot(attn, w_out, preferred_element_type=jnp.float32)  6.72 us
    unnamed x41, local copies, waits for them, and re-layouts  5.78 us
    ppermute x2, waiting for transfers between devices, shifted(): return lax.ppermute(block, axis, route)  5.62 us
    dot_general x1, matrix products, shards(): jnp.dot(h, w_query, preferred_element_type=jnp.float32).astype(jnp.bfloat16)  5.19 us
  transfers between devices with their start and end apart: 4, of which 4 were waited for; matrix products, arithmetic and copies ran while one was open for 24% of the time, Pallas kernels for 0%

commit v1 on v0

v1 whole, which is shorter than its diff:
```python
import functools

import jax
import jax.numpy as jnp
from jax import lax
from jax.experimental import pallas as pl
from jax.experimental.pallas import tpu as pltpu
from jax.sharding import PartitionSpec as P

HD = 64
PAIR = 2 * HD
CUTS = (2, 6, 4)
VMEM_LIMIT = 56 * 1024 * 1024


def whole(count):
    return [pl.BlockSpec(memory_space=pltpu.VMEM)] * count


def params():
    return pltpu.CompilerParams(vmem_limit_bytes=VMEM_LIMIT)


def norm_kernel(x_ref, mod_ref, h_ref):
    rows = 16
    shift = mod_ref[0:1, :]
    scale = 1.0 + mod_ref[1:2, :]

    def body(step, _):
        at = pl.ds(pl.multiple_of(step * rows, rows), rows)
        xf = x_ref[at, :].astype(jnp.float32)
        mean = jnp.mean(xf, axis=1, keepdims=True)
        cent = xf - mean
        var = jnp.mean(cent * cent, axis=1, keepdims=True)
        normed = cent / jnp.sqrt(var + 1e-05)
        h_ref[at, :] = (normed * scale + shift).astype(jnp.bfloat16)
        return 0

    lax.fori_loop(0, x_ref.shape[0] // rows, body, 0)


def norm(states, modul):
    ntok, width = states.shape
    block = 128
    return pl.pallas_call(
        norm_kernel,
        grid=(ntok // block,),
        in_specs=[
            pl.BlockSpec((block, width), lambda i: (i, 0)),
            pl.BlockSpec((3, width), lambda i: (0, 0)),
        ],
        out_specs=pl.BlockSpec((block, width), lambda i: (i, 0)),
        out_shape=jax.ShapeDtypeStruct((ntok, width), jnp.bfloat16),
        compiler_params=params(),
        cost_estimate=pl.CostEstimate(
            flops=10 * ntok * width, bytes_accessed=4 * ntok * width, transcendentals=ntok
        ),
        name="norm",
    )(states, modul)


def attend_kernel(tiles, tile_len, kmax, col, trimmed, ids_ref, own_ref, place_ref, q_ref, *refs):
    pieces, o_ref = refs[:-1], refs[-1]
    width = o_ref.shape[1]
    later = place_ref[0]

    def windows(which):
        if not trimmed:
            return which, [(0, tiles)] * len(pieces)
        last = tiles - 1
        if which == 0:
            return last * later, [(0, tiles), (0, tiles), (last * later, 1)]
        if which == last:
            return last * (1 - later), [(0, tiles), (last * (1 - later), 1), (0, tiles)]
        before, after = tiles - which, which + 1
        if before == after:
            return which, [(0, tiles), (which * (1 - later), after), (which * later, after)]
        return which, [(0, tiles)] * 3

    def row(which, slot, first, count):
        shape = (1, count * tile_len)
        lane = lax.broadcasted_iota(jnp.int32, shape, 1)
        tile = lax.div(lane, tile_len) + (own_ref[slot] + first)
        hit = tile == ids_ref[which * kmax]
        for c in range(1, kmax):
            hit = hit | (tile == ids_ref[which * kmax + c])
        return jnp.where(hit, 0.0, -1e30).astype(jnp.float32)

    lane = lax.broadcasted_iota(jnp.int32, (tile_len, PAIR), 1)
    for position in range(tiles):
        which, spans = windows(position)
        rows = pl.ds(pl.multiple_of(which * tile_len, tile_len), tile_len)
        biases = [row(which, s, f, n) for s, (f, n) in enumerate(spans)]
        keys = [pl.ds(pl.multiple_of(f * tile_len, tile_len), n * tile_len) for f, n in spans]
        for pair in range(width // PAIR):
            cols = slice(pair * PAIR, (pair + 1) * PAIR)
            vals = slice(width + pair * PAIR, width + (pair + 1) * PAIR)
            q = q_ref[rows, col + pair * PAIR : col + (pair + 1) * PAIR]
            zero = jnp.zeros_like(q)
            q2 = jnp.concatenate([jnp.where(lane < HD, q, zero), jnp.where(lane < HD, zero, q)], 0)
            scores = [
                lax.dot_general(
                    q2,
                    piece[at, cols],
                    (((1,), (1,)), ((), ())),
                    preferred_element_type=jnp.float32,
                )
                * 0.125
                + bias
                for piece, at, bias in zip(pieces, keys, biases)
            ]
            top = functools.reduce(
                jnp.maximum, [jnp.max(s, axis=1, keepdims=True) for s in scores]
            )
            expo = [jnp.exp(s - top) for s in scores]
            total = sum(jnp.sum(e, axis=1, keepdims=True) for e in expo)
            acc = sum(
                jnp.dot(e.astype(jnp.bfloat16), piece[at, vals], preferred_element_type=jnp.float32)
                for e, piece, at in zip(expo, pieces, keys)
            )
            out = acc / total
            out = jnp.where(lane < HD, out[:tile_len], out[tile_len:])
            o_ref[rows, cols] = out.astype(jnp.bfloat16)


def attend(ids, owners, place, query, pieces, col, tiles, trimmed):
    ntok = query.shape[0]
    width = pieces[0].shape[1] // 2
    kmax = ids.shape[0] // tiles
    heads = width // HD
    span = (2 * tiles + 1) * (ntok // tiles) if trimmed else len(pieces) * ntok
    smem = pl.BlockSpec(memory_space=pltpu.SMEM)
    return pl.pallas_call(
        functools.partial(attend_kernel, tiles, ntok // tiles, kmax, col, trimmed),
        in_specs=[smem] * 3 + whole(1 + len(pieces)),
        out_specs=whole(1)[0],
        out_shape=jax.ShapeDtypeStruct((ntok, width), jnp.bfloat16),
        compiler_params=params(),
        cost_estimate=pl.CostEstimate(
            flops=16 * ntok * span * heads * HD,
            bytes_accessed=4 * ntok * width * (len(pieces) + 1),
            transcendentals=ntok * span * heads,
        ),
        name="attend",
    )(ids, owners, place, query, *pieces)


def close_kernel(early_ref, own_ref, oth_ref, w_ref, c_ref, keep_a, keep_b, send_a, send_b):
    half = early_ref.shape[0] // 2
    part = early_ref.shape[1] // 4
    for p in range(4):
        cols = slice(p * part, (p + 1) * part)
        y = early_ref[:, cols]
        y += c_ref[0:1, cols] * jnp.dot(
            own_ref[...], w_ref[:, cols], preferred_element_type=jnp.float32
        )
        y += c_ref[1:2, cols] * jnp.dot(
            oth_ref[...], w_ref[:, cols], preferred_element_type=jnp.float32
        )
        a, b = y[:half], y[half:]
        at = slice((p // 2) * part, (p // 2 + 1) * part)
        if p % 2:
            send_a[:, at] = a.astype(jnp.bfloat16)
        else:
            keep_a[:, at] = a
        at = slice((p % 2) * part, (p % 2 + 1) * part)
        if p // 2:
            send_b[:, at] = b.astype(jnp.bfloat16)
        else:
            keep_b[:, at] = b


def close(early, own, oth, w_last, coef):
    ntok, width = early.shape
    keep = jax.ShapeDtypeStruct((ntok // 2, width // 2), jnp.float32)
    send = jax.ShapeDtypeStruct((ntok // 2, width // 2), jnp.bfloat16)
    return pl.pallas_call(
        close_kernel,
        in_specs=whole(5),
        out_specs=whole(4),
        out_shape=[keep, keep, send, send],
        compiler_params=params(),
        cost_estimate=pl.CostEstimate(
            flops=4 * ntok * width * own.shape[1], bytes_accessed=8 * ntok * width, transcendentals=0
        ),
        name="close",
    )(early, own, oth, w_last, coef)


def neighbours(value, distance):
    count = lax.axis_size("seq")
    firsts = [i for i in range(count - distance) if (i // distance) % 2 == 0]
    seconds = [i for i in range(count - distance) if (i // distance) % 2 == 1]
    out = []
    for lows in (firsts, seconds):
        route = [(i, i + distance) for i in lows] + [(i + distance, i) for i in lows]
        out.append(lax.ppermute(value, "seq", route))
    return out


def crossed(value, axis, bit):
    return lax.ppermute(value, axis, [(i, i ^ bit) for i in range(lax.axis_size(axis))])


def shards(
    hidden_states, modulation, w_query, w_key, w_value, w_out, block_ids, block_count, guidance
):
    states = hidden_states[0]
    modul = modulation[0]
    ntok, model = states.shape
    tiles, kmax = block_ids.shape
    heads = w_query.shape[1] // HD
    branch = lax.axis_index("guid")
    tp_here = lax.axis_index("tp")
    seq_here = lax.axis_index("seq")
    seq_count = lax.axis_size("seq")
    reach_dev = min(4, (seq_count - 1) // 2)
    part = model // (2 * lax.axis_size("tp"))
    cuts = [c * heads // sum(CUTS) for c in CUTS]
    starts = [sum(cuts[:i]) for i in range(len(cuts))]

    live = jnp.arange(kmax, dtype=jnp.int32)[None, :] < block_count[:, None]
    ids = jnp.where(live, block_ids, -(1 << 20)).reshape(-1)
    owners = [seq_here]
    for distance in range(1, reach_dev + 1):
        ahead = (seq_here // distance) % 2 == 0
        owners += [
            jnp.where(ahead, seq_here + distance, seq_here - distance),
            jnp.where(ahead, seq_here - distance, seq_here + distance),
        ]
    place = (seq_here % 2 == 0).astype(jnp.int32).reshape(1)
    owners = jnp.stack(owners).astype(jnp.int32) * tiles

    h = norm(states, modul)

    def project(weight):
        return jnp.dot(h, weight, preferred_element_type=jnp.float32).astype(jnp.bfloat16)

    slots = []
    for first, count in zip(starts, cuts):
        cols = slice(first * HD, (first + count) * HD)
        piece = jnp.concatenate([project(w_key[:, cols]), project(w_value[:, cols])], axis=1)
        near = [piece]
        for distance in range(1, reach_dev + 1):
            near += neighbours(piece, distance)
        slots.append(near)
    query = project(w_query)

    scale = guidance[0]
    mine = jnp.where(branch == 0, scale, 1.0 - scale)
    others = jnp.where(branch == 0, 1.0 - scale, scale)
    here = branch * (model // 2)
    there = (1 - branch) * (model // 2)
    x_there = lax.dynamic_slice(states, (0, there + tp_here * part), (ntok, part))
    x_here = lax.dynamic_slice(states, (0, here + tp_here * part), (ntok, part))
    x_other = crossed(x_there, "guid", 1)
    gate_other = crossed(lax.dynamic_slice(modul, (2, there), (1, model // 2)), "guid", 1)
    gate_own = lax.dynamic_slice(modul, (2, here), (1, model // 2))
    coef = jnp.concatenate([mine * gate_own, others * gate_other], axis=0)
    base = mine * x_here.astype(jnp.float32) + others * x_other.astype(jnp.float32)

    def by_partner(array, offset):
        return jnp.concatenate(
            [
                lax.dynamic_slice(
                    array, (0, offset + (tp_here ^ p) * part), (array.shape[0], part)
                )
                for p in range(4)
            ],
            axis=1,
        )

    w_here = by_partner(w_out, here)
    coef = by_partner(coef, 0)

    own, other = [], []
    for first, near in zip(starts, slots):
        out = attend(ids, owners, place, query, near, first * HD, tiles, reach_dev == 1)
        own.append(out)
        other.append(crossed(out, "guid", 1))

    last = starts[-1] * HD
    early = coef[0:1] * jnp.dot(
        jnp.concatenate(own[:-1], axis=1), w_here[:last], preferred_element_type=jnp.float32
    ) + coef[1:2] * jnp.dot(
        jnp.concatenate(other[:-1], axis=1), w_here[:last], preferred_element_type=jnp.float32
    )
    keep_a, keep_b, send_a, send_b = close(early, own[-1], other[-1], w_here[last:], coef)
    got_a = crossed(send_a, "tp", 1)
    got_b = crossed(send_b, "tp", 2)
    sum_a = keep_a + got_a.astype(jnp.float32)
    sum_b = keep_b + got_b.astype(jnp.float32)
    last_a = crossed(sum_a[:, part:].astype(jnp.bfloat16), "tp", 2)
    last_b = crossed(sum_b[:, part:].astype(jnp.bfloat16), "tp", 1)
    total = jnp.concatenate(
        [
            sum_a[:, :part] + last_a.astype(jnp.float32),
            sum_b[:, :part] + last_b.astype(jnp.float32),
        ],
        axis=0,
    )
    return (base + total).astype(jnp.bfloat16)


def solution(mesh):
    in_specs = (
        P("guid", "seq", None),
        P("guid", None, None),
        P(None, "tp"),
        P(None, "tp"),
        P(None, "tp"),
        P("tp", None),
        P("seq", None),
        P("seq"),
        P(),
    )
    out_specs = P("seq", ("guid", "tp"))
    return jax.shard_map(shards, mesh=mesh, in_specs=in_specs, out_specs=out_specs, check_vma=False)
```

time: 127 us -> 94.5 us (0.74)
  Pallas kernels: 0 us -> 27.5 us
  waiting for transfers between devices: 35.1 us -> 9.03 us
  local copies, waits for them, and re-layouts: 27 us -> 8.69 us
  between operations: 14.5 us -> 0.97 us
  starting transfers between devices: 7.31 us -> 19.6 us
  other arithmetic: 15.8 us -> 7.08 us
  matrix products: 26.3 us -> 21 us
    reduce_scatter x1 -> x0, waiting for transfers between devices: 28.6 us -> none  [shards(): lax.psum_scatter(regroup(proj).astype(jnp.bfloat16), 'tp', scatter_dimens...]
    pallas_call x0 -> x5, Pallas kernels: none -> 27.5 us  [the longest x3 15.3 us: attend(): pl.pallas_call(functools.partial(attend_kernel, tiles, ntok // tiles, kma...]
    ppermute x3 -> x15, starting transfers between devices: 7.31 us -> 19.6 us  [the longest x6 12.9 us: neighbours(): out.append(lax.ppermute(value, 'seq', route))]
    dot_general x1 -> x0, local copies, waits for them, and re-layouts: 6.72 us -> none  [shards(): proj = jnp.dot(attn, w_out, preferred_element_type=jnp.float32)]
    reduce_sum x5 -> x0, other arithmetic: 6.18 us -> none  [the longest x3 5.04 us: attend(): new_sum = run_sum * factor + jnp.sum(expo, axis=2)]
    convert_element_type x6 -> x0, local copies, waits for them, and re-layouts: 5.33 us -> none  [the longest x1 1.64 us: shards(): regroup(proj).astype(jnp.bfloat16)]
    dot_general x10 -> x9, matrix products: 26.3 us -> 21 us  [the longest x7 18 us: project(): jnp.dot(h, weight, preferred_element_type=jnp.float32).astype(jnp.bfloat16)]
    reshape x2 -> x1, local copies, waits for them, and re-layouts: 4.83 us -> 0.67 us  [shards(): ids = jnp.where(live, block_ids, -(1 << 20)).reshape(-1)]
  transfers between devices with their start and end apart: 4 -> 15, of which waited for: 4 -> 3; matrix products, arithmetic and copies ran while one was open for 24% -> 27% of each run, Pallas kernels for 0% -> 16%
where the time goes in v1:
time: 94.5 us; the launch traced here: 93.9 us
  Pallas kernels  27.5 us (29%)
  matrix products  21 us (22%)
  starting transfers between devices  19.6 us (21%)
  waiting for transfers between devices  9.03 us (10%)
  local copies, waits for them, and re-layouts  8.69 us (9%)
  other arithmetic  7.08 us (7%)
  between operations  0.97 us (1%)
    dot_general x7, matrix products, project(): jnp.dot(h, weight, preferred_element_type=jnp.float32).astype(jnp.bfloat16)  18 us
    pallas_call x3, Pallas kernels, attend(): pl.pallas_call(functools.partial(attend_kernel, tiles, ntok // tiles, kma...  15.3 us
    ppermute x6, starting transfers between devices, neighbours(): out.append(lax.ppermute(value, 'seq', route))  12.9 us
    ppermute x9, waiting for transfers between devices, crossed(): lax.ppermute(value, axis, [(i, i ^ bit) for i in range(lax.axis_size(axis...  9.02 us
    pallas_call x1, Pallas kernels, norm(): pl.pallas_call(norm_kernel, grid=(ntok // block,), in_specs=[pl.BlockSpec...  8.34 us
    ppermute x9, starting transfers between devices, crossed(): lax.ppermute(value, axis, [(i, i ^ bit) for i in range(lax.axis_size(axis...  6.73 us
    unnamed x39, local copies, waits for them, and re-layouts  5.1 us
    pallas_call x1, Pallas kernels, close(): pl.pallas_call(close_kernel, in_specs=whole(5), out_specs=whole(4), out_s...  3.81 us
  transfers between devices with their start and end apart: 15, of which 3 were waited for; matrix products, arithmetic and copies ran while one was open for 27% of the time, Pallas kernels for 16%

profile of v1, /device:TPU:0, one launch (start us, length us, event | category | flops | bytes accessed | tf_op | source)
XLA Modules:
  0.0 93.9 jit_solution(12503644426001415444)
XLA Ops:
  1.4 8.3 %norm.1 = bf16[384,3072]{1,0:T(8,128)(2,1)} custom-call(bf16[384,3072]{1,0:T(8,128)(2,1)} %bitcast.30, f32[3,3072]{1,0:T(4,128)} %bitcast.31), custom_call_target="tpu_custom_call" | custom-call | flops 11796480 | bytes 4718592 | tf_op jit(solution)/shard_map/norm/pallas_call | solution.py:45
  9.7 2.6 %fusion.20 = bf16[384,256]{1,0:T(8,128)(2,1)S(1)} fusion(bf16[384,3072]{1,0:T(8,128)(2,1)} %norm.1, bf16[3072,768]{1,0:T(8,128)(2,1)S(1)} %copy-done.14), kind=kOutput, calls=%fused_computation.18 | convolution fusion | flops 604078080 | bytes 4128768 | tf_op jit(solution)/shard_map/dot_general | solution.py:237
  12.4 2.3 %fusion.17 = bf16[384,256]{1,0:T(8,128)(2,1)S(1)} fusion(bf16[384,3072]{1,0:T(8,128)(2,1)S(1)} %copy-done, bf16[3072,768]{1,0:T(8,128)(2,1)} %param.12), kind=kOutput, calls=%fused_computation.17 | convolution fusion | flops 604078080 | bytes 4128768 | tf_op jit(solution)/shard_map/dot_general | solution.py:237
  14.8 1.6 %collective-permute-start.9 = (bf16[384,512]{1,0:T(8,128)(2,1)S(1)}, bf16[384,512]{1,0:T(8,128)(2,1)}, u32[]{:S(2)}, u32[]{:S(2)}) collective-permute-start(bf16[384,512]{1,0:T(8,128)(2,1)S(1)} %pad_maximum_fusion.3.refs_0_), channel_id=1, source_target_pairs={{8,16},{16,8},{9,17},{17,9},{10,18},{18,10},{11,19},{19,11},{12,20... | collective-permute-start | bytes 1179656 | tf_op jit(solution)/shard_map/ppermute | solution.py:197
  16.3 5.1 %collective-permute-start.8 = (bf16[384,512]{1,0:T(8,128)(2,1)S(1)}, bf16[384,512]{1,0:T(8,128)(2,1)}, u32[]{:S(2)}, u32[]{:S(2)}) collective-permute-start(bf16[384,512]{1,0:T(8,128)(2,1)S(1)} %pad_maximum_fusion.3.refs_0_), channel_id=1, source_target_pairs={{0,8},{16,24},{8,0},{24,16},{1,9},{17,25},{9,1},{25,17},{2,10},{18... | collective-permute-start | bytes 1179656 | tf_op jit(solution)/shard_map/ppermute | solution.py:197
  24.4 1.5 %collective-permute-start.5 = (bf16[384,768]{1,0:T(8,128)(2,1)S(1)}, bf16[384,768]{1,0:T(8,128)(2,1)}, u32[]{:S(2)}, u32[]{:S(2)}) collective-permute-start(bf16[384,768]{1,0:T(8,128)(2,1)S(1)} %pad_maximum_fusion.2.refs_0_), channel_id=1, source_target_pairs={{8,16},{16,8},{9,17},{17,9},{10,18},{18,10},{11,19},{19,11},{12,20... | collective-permute-start | bytes 1769480 | tf_op jit(solution)/shard_map/ppermute | solution.py:197
  25.9 1.5 %collective-permute-start.4 = (bf16[384,768]{1,0:T(8,128)(2,1)S(1)}, bf16[384,768]{1,0:T(8,128)(2,1)}, u32[]{:S(2)}, u32[]{:S(2)}) collective-permute-start(bf16[384,768]{1,0:T(8,128)(2,1)S(1)} %pad_maximum_fusion.2.refs_0_), channel_id=1, source_target_pairs={{0,8},{16,24},{8,0},{24,16},{1,9},{17,25},{9,1},{25,17},{2,10},{18... | collective-permute-start | bytes 1769480 | tf_op jit(solution)/shard_map/ppermute | solution.py:197
  29.4 2.5 %convolution_convert_fusion.1 = bf16[384,128]{1,0:T(8,128)(2,1)} fusion(bf16[384,3072]{1,0:T(8,128)(2,1)S(1)} %copy-done, bf16[3072,768]{1,0:T(8,128)(2,1)} %param.13), kind=kOutput, calls=%fused_computation.19 | convolution fusion | flops 302039040 | bytes 3244032 | tf_op jit(solution)/shard_map/dot_general | solution.py:237
  31.9 2.5 %convolution_convert_fusion.2 = bf16[384,128]{1,0:T(8,128)(2,1)} fusion(bf16[384,3072]{1,0:T(8,128)(2,1)S(1)} %copy-done, bf16[3072,768]{1,0:T(8,128)(2,1)} %param.12), kind=kOutput, calls=%fused_computation.20 | convolution fusion | flops 302039040 | bytes 3244032 | tf_op jit(solution)/shard_map/dot_general | solution.py:237
  34.5 1.9 %constant_dynamic-slice_fusion.3 = (bf16[768,384]{1,0:T(8,128)(2,1)S(1)}, bf16[768,384]{1,0:T(8,128)(2,1)S(1)}, bf16[768,384]{1,0:T(8,128)(2,1)S(1)}, bf16[768,384]{1,0:T(8,128)(2,1)S(1)}) fusion(bf16[768,3072]{1,0:T(8,128)(2,1)} %param.14, s32[]{:T(128)S(6)} %select_n.63, s32[]{:T(128)S(6)} %select_n.76, s32[]{:T(128)S(6)} %select_n.78, s32[]{:T(128)S(6)} %select_n.77), kind=kLoop, calls=%fused_computation.60 | loop fusion | bytes 4718608 | tf_op jit(solution)/shard_map/dynamic_slice | solution.py:265
  38.9 5.2 %convolution_convert_fusion.q_ref = bf16[384,768]{1,0:T(8,128)(2,1)} fusion(bf16[384,3072]{1,0:T(8,128)(2,1)S(1)} %copy-done.1, bf16[3072,768]{1,0:T(8,128)(2,1)} %param.11), kind=kOutput, calls=%fused_computation.14 | convolution fusion | flops 1812234240 | bytes 7667712 | tf_op jit(solution)/shard_map/dot_general | solution.py:237
  47.2 2.3 %collective-permute-start.2 = (bf16[384,256]{1,0:T(8,128)(2,1)S(1)}, bf16[384,256]{1,0:T(8,128)(2,1)S(1)}, u32[]{:S(2)}, u32[]{:S(2)}) collective-permute-start(bf16[384,256]{1,0:T(8,128)(2,1)S(1)} %pad_maximum_fusion.4.refs_0_), channel_id=1, source_target_pairs={{0,8},{16,24},{8,0},{24,16},{1,9},{17,25},{9,1},{25,17},{2,10},{18... | collective-permute-start | bytes 589832 | tf_op jit(solution)/shard_map/ppermute | solution.py:197
  49.6 6.7 %attend.4 = bf16[384,384]{1,0:T(8,128)(2,1)} custom-call(s32[21]{0:T(128)} %reshape.30.ids_ref, s32[3]{0:T(128)} %add_multiply_fusion.own_ref, s32[1]{0:T(128)} %bitcast.8.place_ref, bf16[384,768]{1,0:T(8,128)(2,1)} %convolution_convert_fusion.q_ref, bf16[384,768]{1,0:T(8,128)(2,1)} %copy-done.2, bf16[384,768]{1,0:T(8,128)(2,1)} %collective-permute-done.4.refs_1_, ...), custom_call_target="tpu_custom_call" | custom-call | flops 2113929216 | bytes 2359296 | tf_op jit(solution)/shard_map/attend/pallas_call | solution.py:133
  57.7 3.5 %attend.3 = bf16[384,128]{1,0:T(8,128)(2,1)} custom-call(s32[21]{0:T(128)} %reshape.30.ids_ref, s32[3]{0:T(128)} %add_multiply_fusion.own_ref, s32[1]{0:T(128)} %bitcast.8.place_ref, bf16[384,768]{1,0:T(8,128)(2,1)} %convolution_convert_fusion.q_ref, bf16[384,256]{1,0:T(8,128)(2,1)} %copy-done.6, bf16[384,256]{1,0:T(8,128)(2,1)} %copy-done.16, ...), custom_call_target="tpu_custom_call" | custom-call | flops 704643072 | bytes 786432 | tf_op jit(solution)/shard_map/attend/pallas_call | solution.py:133
  61.7 5.1 %attend.5.own_ref = bf16[384,256]{1,0:T(8,128)(2,1)} custom-call(s32[21]{0:T(128)} %reshape.30.ids_ref, s32[3]{0:T(128)} %add_multiply_fusion.own_ref, s32[1]{0:T(128)} %bitcast.8.place_ref, bf16[384,768]{1,0:T(8,128)(2,1)} %convolution_convert_fusion.q_ref, bf16[384,512]{1,0:T(8,128)(2,1)} %copy-done.4, bf16[384,512]{1,0:T(8,128)(2,1)} %collective-permute-done.8.refs_1_, ...), custom_call_target="tpu_custom_call" | custom-call | flops 1409286144 | bytes 1572864 | tf_op jit(solution)/shard_map/attend/pallas_call | solution.py:133
  67.8 2.2 %fusion.early_ref = f32[384,1536]{1,0:T(8,128)} fusion(f32[384,1536]{1,0:T(8,128)S(1)} %convolution_multiply_fusion, bf16[768,1536]{1,0:T(8,128)(2,1)S(1)} %pad_maximum_fusion, f32[1536]{0:T(1024)S(1)} %get-tuple-element.13, bf16[384,384]{1,0:T(8,128)(2,1)S(1)} %copy-done.5, bf16[384,128]{1,0:T(8,128)(2,1)S(1)} %copy-done.11), kind=kOutput, calls=%fused_computation.2 | convolution fusion | flops 605945856 | bytes 6692864 | tf_op jit(solution)/shard_map/dot_general | solution.py:283
  70.7 3.8 %close.1 = (f32[192,768]{1,0:T(8,128)}, f32[192,768]{1,0:T(8,128)}, bf16[192,768]{1,0:T(8,128)(2,1)}, bf16[192,768]{1,0:T(8,128)(2,1)}) custom-call(f32[384,1536]{1,0:T(8,128)} %fusion.early_ref, bf16[384,256]{1,0:T(8,128)(2,1)} %attend.5.own_ref, bf16[384,256]{1,0:T(8,128)(2,1)} %copy-done.7, bf16[256,1536]{1,0:T(8,128)(2,1)} %pad_maximum_fusion.1.w_ref, ...), custom_call_target="tpu_custom_call" | custom-call | flops 603979776 | bytes 4718592 | tf_op jit(solution)/shard_map/close/pallas_call | solution.py:177
  74.5 1.5 %collective-permute-start.11 = (bf16[192,768]{1,0:T(8,128)(2,1)}, bf16[192,768]{1,0:T(8,128)(2,1)S(1)}, u32[]{:S(2)}, u32[]{:S(2)}) collective-permute-start(bf16[192,768]{1,0:T(8,128)(2,1)} %get-tuple-element.10), channel_id=1, source_target_pairs={{0,1},{1,0},{2,3},{3,2},{4,5},{5,4},{6,7},{7,6},{8,9},{9,8},{10,11... | collective-permute-start | bytes 884744 | tf_op jit(solution)/shard_map/ppermute | solution.py:202
  76.0 1.5 %collective-permute-start.13 = (bf16[192,768]{1,0:T(8,128)(2,1)}, bf16[192,768]{1,0:T(8,128)(2,1)S(1)}, u32[]{:S(2)}, u32[]{:S(2)}) collective-permute-start(bf16[192,768]{1,0:T(8,128)(2,1)} %get-tuple-element.12), channel_id=1, source_target_pairs={{0,2},{1,3},{2,0},{3,1},{4,6},{5,7},{6,4},{7,5},{8,10},{9,11},{10,... | collective-permute-start | bytes 884744 | tf_op jit(solution)/shard_map/ppermute | solution.py:202
  78.6 5.4 %collective-permute-done.11 = bf16[192,768]{1,0:T(8,128)(2,1)S(1)} collective-permute-done((bf16[192,768]{1,0:T(8,128)(2,1)}, bf16[192,768]{1,0:T(8,128)(2,1)S(1)}, u32[]{:S(2)}, u32[]{:S(2)}) %collective-permute-start.11) | collective-permute-done | bytes 294944 | tf_op jit(solution)/shard_map/ppermute | solution.py:202
  85.1 1.6 %collective-permute-start.12 = (bf16[192,384]{1,0:T(8,128)(2,1)S(1)}, bf16[192,384]{1,0:T(8,128)(2,1)S(1)}, u32[]{:S(2)}, u32[]{:S(2)}) collective-permute-start(bf16[192,384]{1,0:T(8,128)(2,1)S(1)} %slice.97), channel_id=1, source_target_pairs={{0,2},{1,3},{2,0},{3,1},{4,6},{5,7},{6,4},{7,5},{8,10},{9,11},{10,... | collective-permute-start | bytes 442376 | tf_op jit(solution)/shard_map/ppermute | solution.py:202
  86.8 1.6 %collective-permute-start.14 = (bf16[192,384]{1,0:T(8,128)(2,1)S(1)}, bf16[192,384]{1,0:T(8,128)(2,1)S(1)}, u32[]{:S(2)}, u32[]{:S(2)}) collective-permute-start(bf16[192,384]{1,0:T(8,128)(2,1)S(1)} %slice.96), channel_id=1, source_target_pairs={{0,1},{1,0},{2,3},{3,2},{4,5},{5,4},{6,7},{7,6},{8,9},{9,8},{10,11... | collective-permute-start | bytes 442376 | tf_op jit(solution)/shard_map/ppermute | solution.py:202
  88.3 2.1 %collective-permute-done.12 = bf16[192,384]{1,0:T(8,128)(2,1)S(1)} collective-permute-done((bf16[192,384]{1,0:T(8,128)(2,1)S(1)}, bf16[192,384]{1,0:T(8,128)(2,1)S(1)}, u32[]{:S(2)}, u32[]{:S(2)}) %collective-permute-start.12) | collective-permute-done | bytes 147488 | tf_op jit(solution)/shard_map/ppermute | solution.py:202
  92.0 1.8 %fusion.25 = bf16[384,384]{1,0:T(8,128)(2,1)} fusion(f32[192,384]{1,0:T(8,128)S(1)} %slice_add_fusion, f32[192,384]{1,0:T(8,128)S(1)} %slice_add_fusion.1, bf16[384,384]{1,0:T(8,128)(2,1)S(1)} %collective-permute-done, f32[]{:T(128)S(6)} %select_n.64, bf16[1,384,3072]{2,1,0:T(8,128)(2,1)} %param.9, s32[]{:T(128)S(6)} %select_n.63, f32[]{:T(128)S(6)} %select_n.62), kind=kLoop, calls=%fused_computation.26 | loop fusion | flops 1179648 | bytes 1474572 | tf_op jit(solution)/shard_map/convert_element_type | solution.py:302
  (82 shorter events, 18.6 us)
Async XLA Ops:
  1.4 8.3 %copy-start.14 = (bf16[3072,768]{1,0:T(8,128)(2,1)S(1)}, bf16[3072,768]{1,0:T(8,128)(2,1)}, u32[]{:S(2)}) copy-start(bf16[3072,768]{1,0:T(8,128)(2,1)} %param.13) | copy-start | bytes 14155780
  12.4 10.5 %slice-start = ((s8[4718592]{0:T(1024)(128)(4,1)}), s8[4194304]{0:T(1024)(128)(4,1)S(1)}, s32[]{:S(2)}) async-start(s8[4718592]{0:T(1024)(128)(4,1)} %bitcast.32), calls=%async_computation | async-start | bytes 8388608
  14.7 8.2 %slice-start.1 = ((s8[4718592]{0:T(1024)(128)(4,1)}), s8[524288]{0:T(1024)(128)(4,1)S(1)}, s32[]{:S(2)}) async-start(s8[4718592]{0:T(1024)(128)(4,1)} %bitcast.32), calls=%async_computation.1 | async-start | bytes 1048576
  14.8 8.1 %copy-start.4 = (bf16[384,512]{1,0:T(8,128)(2,1)}, bf16[384,512]{1,0:T(8,128)(2,1)S(1)}, u32[]{:S(2)}) copy-start(bf16[384,512]{1,0:T(8,128)(2,1)S(1)} %pad_maximum_fusion.3.refs_0_) | copy-start | bytes 1179652
  14.8 47.0 %collective-permute-start.9 = (bf16[384,512]{1,0:T(8,128)(2,1)S(1)}, bf16[384,512]{1,0:T(8,128)(2,1)}, u32[]{:S(2)}, u32[]{:S(2)}) collective-permute-start(bf16[384,512]{1,0:T(8,128)(2,1)S(1)} %pad_maximum_fusion.3.refs_0_), channel_id=1, source_target_pairs={{8,16},{16,8},{9,17},{17,9},{10,18},{18,10},{11,19},{19,11},{12,20... | collective-permute-start | bytes 1179656 | tf_op jit(solution)/shard_map/ppermute | solution.py:197
  16.3 45.4 %collective-permute-start.8 = (bf16[384,512]{1,0:T(8,128)(2,1)S(1)}, bf16[384,512]{1,0:T(8,128)(2,1)}, u32[]{:S(2)}, u32[]{:S(2)}) collective-permute-start(bf16[384,512]{1,0:T(8,128)(2,1)S(1)} %pad_maximum_fusion.3.refs_0_), channel_id=1, source_target_pairs={{0,8},{16,24},{8,0},{24,16},{1,9},{17,25},{9,1},{25,17},{2,10},{18... | collective-permute-start | bytes 1179656 | tf_op jit(solution)/shard_map/ppermute | solution.py:197
  24.4 10.1 %copy-start.2 = (bf16[384,768]{1,0:T(8,128)(2,1)}, bf16[384,768]{1,0:T(8,128)(2,1)S(1)}, u32[]{:S(2)}) copy-start(bf16[384,768]{1,0:T(8,128)(2,1)S(1)} %pad_maximum_fusion.2.refs_0_) | copy-start | bytes 1769476
  24.4 22.8 %collective-permute-start.5 = (bf16[384,768]{1,0:T(8,128)(2,1)S(1)}, bf16[384,768]{1,0:T(8,128)(2,1)}, u32[]{:S(2)}, u32[]{:S(2)}) collective-permute-start(bf16[384,768]{1,0:T(8,128)(2,1)S(1)} %pad_maximum_fusion.2.refs_0_), channel_id=1, source_target_pairs={{8,16},{16,8},{9,17},{17,9},{10,18},{18,10},{11,19},{19,11},{12,20... | collective-permute-start | bytes 1769480 | tf_op jit(solution)/shard_map/ppermute | solution.py:197
  25.9 23.7 %collective-permute-start.4 = (bf16[384,768]{1,0:T(8,128)(2,1)S(1)}, bf16[384,768]{1,0:T(8,128)(2,1)}, u32[]{:S(2)}, u32[]{:S(2)}) collective-permute-start(bf16[384,768]{1,0:T(8,128)(2,1)S(1)} %pad_maximum_fusion.2.refs_0_), channel_id=1, source_target_pairs={{0,8},{16,24},{8,0},{24,16},{1,9},{17,25},{9,1},{25,17},{2,10},{18... | collective-permute-start | bytes 1769480 | tf_op jit(solution)/shard_map/ppermute | solution.py:197
  29.4 16.2 %collective-permute-start.1 = (f32[1,1536]{1,0:T(1,128)}, f32[1,1536]{1,0:T(1,128)}, u32[]{:S(2)}, u32[]{:S(2)}) collective-permute-start(f32[1,1536]{1,0:T(1,128)} %get-tuple-element.19), channel_id=1, source_target_pairs={{0,4},{4,0},{1,5},{5,1},{2,6},{6,2},{3,7},{7,3},{8,12},{12,8},{9,1... | collective-permute-start | bytes 18440 | tf_op jit(solution)/shard_map/ppermute | solution.py:202
  38.9 5.3 %copy-start.10 = (bf16[384,128]{1,0:T(8,128)(2,1)S(1)}, bf16[384,128]{1,0:T(8,128)(2,1)}, u32[]{:S(2)}) copy-start(bf16[384,128]{1,0:T(8,128)(2,1)} %convolution_convert_fusion.2) | copy-start | bytes 294916
  44.2 12.0 %copy-start.6 = (bf16[384,256]{1,0:T(8,128)(2,1)}, bf16[384,256]{1,0:T(8,128)(2,1)S(1)}, u32[]{:S(2)}) copy-start(bf16[384,256]{1,0:T(8,128)(2,1)S(1)} %pad_maximum_fusion.4.refs_0_) | copy-start | bytes 589828
  45.5 10.8 %collective-permute-start.3 = (bf16[384,256]{1,0:T(8,128)(2,1)S(1)}, bf16[384,256]{1,0:T(8,128)(2,1)S(1)}, u32[]{:S(2)}, u32[]{:S(2)}) collective-permute-start(bf16[384,256]{1,0:T(8,128)(2,1)S(1)} %pad_maximum_fusion.4.refs_0_), channel_id=1, source_target_pairs={{8,16},{16,8},{9,17},{17,9},{10,18},{18,10},{11,19},{19,11},{12,20... | collective-permute-start | bytes 589832 | tf_op jit(solution)/shard_map/ppermute | solution.py:197
  47.2 9.1 %copy-start.8 = (f32[2,1536]{1,0:T(2,128)}, f32[2,1536]{1,0:T(2,128)S(1)}, u32[]{:S(2)}) copy-start(f32[2,1536]{1,0:T(2,128)S(1)} %pad_maximum_fusion.5.c_ref) | copy-start | bytes 36868
  47.2 9.1 %collective-permute-start.2 = (bf16[384,256]{1,0:T(8,128)(2,1)S(1)}, bf16[384,256]{1,0:T(8,128)(2,1)S(1)}, u32[]{:S(2)}, u32[]{:S(2)}) collective-permute-start(bf16[384,256]{1,0:T(8,128)(2,1)S(1)} %pad_maximum_fusion.4.refs_0_), channel_id=1, source_target_pairs={{0,8},{16,24},{8,0},{24,16},{1,9},{17,25},{9,1},{25,17},{2,10},{18... | collective-permute-start | bytes 589832 | tf_op jit(solution)/shard_map/ppermute | solution.py:197
  56.3 10.6 %collective-permute-start.7 = (bf16[384,384]{1,0:T(8,128)(2,1)}, bf16[384,384]{1,0:T(8,128)(2,1)S(1)}, u32[]{:S(2)}, u32[]{:S(2)}) collective-permute-start(bf16[384,384]{1,0:T(8,128)(2,1)} %attend.4), channel_id=1, source_target_pairs={{0,4},{4,0},{1,5},{5,1},{2,6},{6,2},{3,7},{7,3},{8,12},{12,8},{9,1... | collective-permute-start | bytes 884744 | tf_op jit(solution)/shard_map/ppermute | solution.py:202
  61.2 5.6 %collective-permute-start.6 = (bf16[384,128]{1,0:T(8,128)(2,1)}, bf16[384,128]{1,0:T(8,128)(2,1)S(1)}, u32[]{:S(2)}, u32[]{:S(2)}) collective-permute-start(bf16[384,128]{1,0:T(8,128)(2,1)} %attend.3), channel_id=1, source_target_pairs={{0,4},{4,0},{1,5},{5,1},{2,6},{6,2},{3,7},{7,3},{8,12},{12,8},{9,1... | collective-permute-start | bytes 294920 | tf_op jit(solution)/shard_map/ppermute | solution.py:202
  66.8 3.2 %collective-permute-start.10 = (bf16[384,256]{1,0:T(8,128)(2,1)}, bf16[384,256]{1,0:T(8,128)(2,1)S(1)}, u32[]{:S(2)}, u32[]{:S(2)}) collective-permute-start(bf16[384,256]{1,0:T(8,128)(2,1)} %attend.5.own_ref), channel_id=1, source_target_pairs={{0,4},{4,0},{1,5},{5,1},{2,6},{6,2},{3,7},{7,3},{8,12},{12,8},{9,1... | collective-permute-start | bytes 589832 | tf_op jit(solution)/shard_map/ppermute | solution.py:202
  74.5 12.2 %copy-start.3 = (f32[192,768]{1,0:T(8,128)S(1)}, f32[192,768]{1,0:T(8,128)}, u32[]{:S(2)}) copy-start(f32[192,768]{1,0:T(8,128)} %get-tuple-element.11) | copy-start | bytes 1769476
  74.5 9.5 %collective-permute-start.11 = (bf16[192,768]{1,0:T(8,128)(2,1)}, bf16[192,768]{1,0:T(8,128)(2,1)S(1)}, u32[]{:S(2)}, u32[]{:S(2)}) collective-permute-start(bf16[192,768]{1,0:T(8,128)(2,1)} %get-tuple-element.10), channel_id=1, source_target_pairs={{0,1},{1,0},{2,3},{3,2},{4,5},{5,4},{6,7},{7,6},{8,9},{9,8},{10,11... | collective-permute-start | bytes 884744 | tf_op jit(solution)/shard_map/ppermute | solution.py:202
  76.0 10.7 %collective-permute-start.13 = (bf16[192,768]{1,0:T(8,128)(2,1)}, bf16[192,768]{1,0:T(8,128)(2,1)S(1)}, u32[]{:S(2)}, u32[]{:S(2)}) collective-permute-start(bf16[192,768]{1,0:T(8,128)(2,1)} %get-tuple-element.12), channel_id=1, source_target_pairs={{0,2},{1,3},{2,0},{3,1},{4,6},{5,7},{6,4},{7,5},{8,10},{9,11},{10,... | collective-permute-start | bytes 884744 | tf_op jit(solution)/shard_map/ppermute | solution.py:202
  78.5 13.5 %collective-permute-start = (bf16[384,384]{1,0:T(8,128)(2,1)S(1)}, bf16[384,384]{1,0:T(8,128)(2,1)S(1)}, u32[]{:S(2)}, u32[]{:S(2)}) collective-permute-start(bf16[384,384]{1,0:T(8,128)(2,1)S(1)} %dynamic-slice_bitcast_fusion), channel_id=1, source_target_pairs={{0,4},{4,0},{1,5},{5,1},{2,6},{6,2},{3,7},{7,3},{8,12},{12,8},{9,1... | collective-permute-start | bytes 884744 | tf_op jit(solution)/shard_map/ppermute | solution.py:202
  85.1 5.4 %collective-permute-start.12 = (bf16[192,384]{1,0:T(8,128)(2,1)S(1)}, bf16[192,384]{1,0:T(8,128)(2,1)S(1)}, u32[]{:S(2)}, u32[]{:S(2)}) collective-permute-start(bf16[192,384]{1,0:T(8,128)(2,1)S(1)} %slice.97), channel_id=1, source_target_pairs={{0,2},{1,3},{2,0},{3,1},{4,6},{5,7},{6,4},{7,5},{8,10},{9,11},{10,... | collective-permute-start | bytes 442376 | tf_op jit(solution)/shard_map/ppermute | solution.py:202
  86.8 5.2 %collective-permute-start.14 = (bf16[192,384]{1,0:T(8,128)(2,1)S(1)}, bf16[192,384]{1,0:T(8,128)(2,1)S(1)}, u32[]{:S(2)}, u32[]{:S(2)}) collective-permute-start(bf16[192,384]{1,0:T(8,128)(2,1)S(1)} %slice.96), channel_id=1, source_target_pairs={{0,1},{1,0},{2,3},{3,2},{4,5},{5,4},{6,7},{7,6},{8,9},{9,8},{10,11... | collective-permute-start | bytes 442376 | tf_op jit(solution)/shard_map/ppermute | solution.py:202
  (10 other events, 23.9 us)

commit v2 on v0

v2 whole, which is shorter than its diff:
```python
import functools

import jax
import jax.numpy as jnp
from jax import lax
from jax.experimental import pallas as pl
from jax.experimental.pallas import tpu as pltpu
from jax.sharding import PartitionSpec as P

HD = 64
PAIR = 2 * HD
FIRST_VALUES = 8 / 12
MIB = 1024 * 1024


def vmem(count):
    return [pl.BlockSpec(memory_space=pltpu.VMEM)] * count


def smem(count):
    return [pl.BlockSpec(memory_space=pltpu.SMEM)] * count


def params(mib):
    return pltpu.CompilerParams(vmem_limit_bytes=mib * MIB)


def cost(flops, nbytes, exps=0):
    return pl.CostEstimate(flops=int(flops), bytes_accessed=int(nbytes), transcendentals=int(exps))


def aligned(start, size):
    return pl.ds(pl.multiple_of(start, 128), size)


def norm_kernel(x_ref, mod_ref, h_ref):
    rows = 64
    shift = mod_ref[0]
    scale = 1.0 + mod_ref[1]
    for step in range(h_ref.shape[0] // rows):
        at = slice(step * rows, (step + 1) * rows)
        xf = x_ref[0, at, :].astype(jnp.float32)
        cent = xf - jnp.mean(xf, axis=1, keepdims=True)
        var = jnp.mean(cent * cent, axis=1, keepdims=True)
        h_ref[at, :] = (cent / jnp.sqrt(var + 1e-05) * scale + shift).astype(jnp.bfloat16)


def norm(states, modul):
    _, ntok, width = states.shape
    block = 128
    return pl.pallas_call(
        norm_kernel,
        grid=(ntok // block,),
        in_specs=[
            pl.BlockSpec((1, block, width), lambda i: (0, i, 0)),
            pl.BlockSpec((3, 1, width), lambda i: (0, 0, 0)),
        ],
        out_specs=pl.BlockSpec((block, width), lambda i: (i, 0)),
        out_shape=jax.ShapeDtypeStruct((ntok, width), jnp.bfloat16),
        compiler_params=params(12),
        cost_estimate=cost(10 * ntok * width, 4 * ntok * width, ntok),
        name="norm",
    )(states, modul)


def ahead_here(distance):
    return 1 - lax.rem(lax.div(lax.axis_index("seq"), distance), 2)


def spans_of(position, tiles, slots, trimmed):
    if not trimmed:
        return position, [(0, tiles)] * slots
    ahead, last = ahead_here(1), tiles - 1
    if position == 0:
        return last * ahead, [(0, tiles), (0, tiles), (last * ahead, 1)]
    if position == last:
        return last * (1 - ahead), [(0, tiles), (last * (1 - ahead), 1), (0, tiles)]
    if tiles - position == position + 1:
        count = position + 1
        return position, [(0, tiles), (position * (1 - ahead), count), (position * ahead, count)]
    return position, [(0, tiles)] * 3


def bias_rows(which, spans, tile_len, ids_ref, count_ref):
    here, tiles = lax.axis_index("seq"), ids_ref.shape[0]
    owners = [here]
    for distance in range(1, (len(spans) - 1) // 2 + 1):
        side = 2 * ahead_here(distance) - 1
        owners += [here + side * distance, here - side * distance]
    kmax = ids_ref.shape[1]
    live = count_ref[which]
    listed = [jnp.where(c < live, ids_ref[which, c], ids_ref[which, 0]) for c in range(kmax)]
    out = []
    for owner, (first, count) in zip(owners, spans):
        lane = lax.broadcasted_iota(jnp.int32, (1, count * tile_len), 1)
        tile = lax.div(lane, tile_len) + (owner * tiles + first)
        hit = functools.reduce(jnp.logical_or, [tile == one for one in listed])
        out.append(jnp.where(hit, 0.0, -1e30).astype(jnp.float32))
    return out


def score(q, keys, biases):
    lane = lax.broadcasted_iota(jnp.int32, q.shape, 1)
    q = q * jnp.asarray(0.125, q.dtype)
    zero = jnp.zeros_like(q)
    both = jnp.concatenate([jnp.where(lane < HD, q, zero), jnp.where(lane < HD, zero, q)], 0)
    return [
        lax.dot_general(both, k, (((1,), (1,)), ((), ())), preferred_element_type=jnp.float32) + b
        for k, b in zip(keys, biases)
    ]


def soften(scores):
    top = functools.reduce(jnp.maximum, [jnp.max(s, axis=1, keepdims=True) for s in scores])
    expo = [jnp.exp(s - top) for s in scores]
    total = sum(jnp.sum(e, axis=1, keepdims=True) for e in expo)
    return [e.astype(jnp.bfloat16) for e in expo], 1.0 / total


def by_head(stacked, width):
    half = stacked.shape[0] // 2
    lane = lax.broadcasted_iota(jnp.int32, (half, width), 1)
    return jnp.where(lane < HD, stacked[:half], stacked[half:])


def plan(tiles, tile_len, slots, trimmed, pairs):
    items = []
    for position in range(tiles):
        which, spans = spans_of(position, tiles, slots, trimmed)
        rows = pl.ds(pl.multiple_of(which * tile_len, tile_len), tile_len)
        keys = [pl.ds(pl.multiple_of(f * tile_len, tile_len), n * tile_len) for f, n in spans]
        items += [(position, which, spans, rows, keys, pair) for pair in range(pairs)]
    return items


def overlapped(items, begin, end):
    current = begin(items[0])
    for i, item in enumerate(items):
        following = begin(items[i + 1]) if i + 1 < len(items) else None
        end(item, current)
        current = following


def columns(pair):
    return slice(pair * PAIR, (pair + 1) * PAIR)


def weigh_kernel(tiles, trimmed, ids_ref, count_ref, q_ref, *refs):
    pieces, p_ref, inv_ref = refs[:-2], refs[-2], refs[-1]
    tile_len = q_ref.shape[0] // tiles
    pairs = q_ref.shape[1] // PAIR
    rows_of = {}

    def begin(item):
        position, which, spans, rows, keys, pair = item
        if position not in rows_of:
            rows_of[position] = bias_rows(which, spans, tile_len, ids_ref, count_ref)
        near = [piece[at, columns(pair)] for piece, at in zip(pieces, keys)]
        return score(q_ref[rows, columns(pair)], near, rows_of[position])

    def end(item, scores):
        position, which, spans, rows, keys, pair = item
        expo, inverse = soften(scores)
        slot, at = position * pairs + pair, 0
        for e in expo:
            p_ref[slot, :, at : at + e.shape[1]] = e
            at += e.shape[1]
        inv_ref[slot] = by_head(inverse, PAIR)

    overlapped(plan(tiles, tile_len, len(pieces), trimmed, pairs), begin, end)


def weigh(block_ids, block_count, query, pieces, span):
    ntok, width = query.shape
    tiles = block_ids.shape[0]
    items = tiles * width // PAIR
    tile_len = ntok // tiles
    return pl.pallas_call(
        functools.partial(weigh_kernel, tiles, True),
        in_specs=smem(2) + vmem(1 + len(pieces)),
        out_specs=vmem(2),
        out_shape=[
            jax.ShapeDtypeStruct((items, 2 * tile_len, span), jnp.bfloat16),
            jax.ShapeDtypeStruct((items, tile_len, PAIR), jnp.float32),
        ],
        compiler_params=params(24),
        cost_estimate=cost(4 * ntok * span * width, 2 * ntok * span * width / HD, ntok * span * width / HD),
        name="weigh",
    )(block_ids, block_count, query, *pieces)


def gather_kernel(tiles, first_pair, p_ref, inv_ref, *refs):
    pieces, o_ref = refs[:-1], refs[-1]
    tile_len = o_ref.shape[0] // tiles
    pairs = o_ref.shape[1] // PAIR
    all_pairs = p_ref.shape[0] // tiles
    for position, which, spans, rows, keys, pair in plan(tiles, tile_len, len(pieces), True, pairs):
        slot, start, acc = position * all_pairs + first_pair + pair, 0, 0.0
        for piece, at, (_, count) in zip(pieces, keys, spans):
            part = p_ref[slot, :, start : start + count * tile_len]
            acc += jnp.dot(part, piece[at, columns(pair)], preferred_element_type=jnp.float32)
            start += count * tile_len
        o_ref[rows, columns(pair)] = (by_head(acc, PAIR) * inv_ref[slot]).astype(jnp.bfloat16)


def gather(p, inv, pieces, first_pair, tiles):
    ntok, width = pieces[0].shape
    return pl.pallas_call(
        functools.partial(gather_kernel, tiles, first_pair),
        in_specs=vmem(2 + len(pieces)),
        out_specs=vmem(1)[0],
        out_shape=jax.ShapeDtypeStruct((ntok, width), jnp.bfloat16),
        compiler_params=params(24),
        cost_estimate=cost(4 * ntok * p.shape[2] * width, 2 * ntok * p.shape[2] * width / HD),
        name="gather",
    )(p, inv, *pieces)


def attend_kernel(tiles, slots, ids_ref, count_ref, q_ref, *refs):
    keys_refs, values, o_ref = refs[:slots], refs[slots : 2 * slots], refs[-1]
    tile_len = q_ref.shape[0] // tiles
    for position, which, spans, rows, keys, pair in plan(
        tiles, tile_len, slots, False, o_ref.shape[1] // PAIR
    ):
        biases = bias_rows(which, spans, tile_len, ids_ref, count_ref)
        near = [piece[at, columns(pair)] for piece, at in zip(keys_refs, keys)]
        expo, inverse = soften(score(q_ref[rows, columns(pair)], near, biases))
        acc = sum(
            jnp.dot(e, piece[at, columns(pair)], preferred_element_type=jnp.float32)
            for e, piece, at in zip(expo, values, keys)
        )
        o_ref[rows, columns(pair)] = by_head(acc * inverse, PAIR).astype(jnp.bfloat16)


def attend(block_ids, block_count, query, keys, values):
    ntok, width = query.shape
    span = ntok * len(keys)
    return pl.pallas_call(
        functools.partial(attend_kernel, block_ids.shape[0], len(keys)),
        in_specs=smem(2) + vmem(1 + 2 * len(keys)),
        out_specs=vmem(1)[0],
        out_shape=jax.ShapeDtypeStruct((ntok, width), jnp.bfloat16),
        compiler_params=params(40),
        cost_estimate=cost(8 * ntok * span * width, 4 * span * width, ntok * span * width / HD),
        name="attend",
    )(block_ids, block_count, query, *keys, *values)


def early_kernel(own_ref, oth_ref, w_hbm, x_hbm, xo_ref, mod_ref, gate_ref, scale_ref, *refs):
    y_ref, wl_ref, c_ref, wb, xb, sems = refs
    part = xb.shape[1]
    model = x_hbm.shape[2]
    done = own_ref.shape[1]
    branch, here = lax.axis_index("guid"), lax.axis_index("tp")
    starts = [branch * (model // 2) + lax.bitwise_xor(here, p) * part for p in range(4)]
    spots = [slice(p * part, (p + 1) * part) for p in range(4)]
    copies = [
        pltpu.make_async_copy(x_hbm.at[0, :, aligned(starts[0], part)], xb, sems.at[8])
    ]
    for p in range(4):
        src = w_hbm.at[pl.ds(0, done), aligned(starts[p], part)]
        copies.append(pltpu.make_async_copy(src, wb.at[:, spots[p]], sems.at[p]))
    for p in range(4):
        src = w_hbm.at[pl.ds(done, wl_ref.shape[0]), aligned(starts[p], part)]
        copies.append(pltpu.make_async_copy(src, wl_ref.at[:, spots[p]], sems.at[4 + p]))
    for copy in copies:
        copy.start()
    scale = scale_ref[0]
    mine = jnp.where(branch == 0, scale, 1.0 - scale)
    others = jnp.where(branch == 0, 1.0 - scale, scale)
    copies[0].wait()
    base = mine * xb[...].astype(jnp.float32) + others * xo_ref[...].astype(jnp.float32)
    for p in range(4):
        at = aligned(starts[p], part)
        own_gate = mine * mod_ref[2, :, at]
        oth_gate = others * gate_ref[0, :, at]
        c_ref[0:1, spots[p]] = own_gate
        c_ref[1:2, spots[p]] = oth_gate
        copies[1 + p].wait()
        weight = wb[:, spots[p]]
        y = own_gate * jnp.dot(own_ref[...], weight, preferred_element_type=jnp.float32)
        y += oth_gate * jnp.dot(oth_ref[...], weight, preferred_element_type=jnp.float32)
        y_ref[:, spots[p]] = y + base if p == 0 else y
    for copy in copies[5:]:
        copy.wait()


def early(own, oth, w_out, states, x_other, modul, gate_other, scale):
    ntok, done = own.shape
    width, model = w_out.shape
    part = x_other.shape[1]
    hbm = [pl.BlockSpec(memory_space=pl.ANY)]
    return pl.pallas_call(
        early_kernel,
        in_specs=vmem(2) + hbm * 2 + vmem(3) + smem(1),
        out_specs=vmem(3),
        out_shape=[
            jax.ShapeDtypeStruct((ntok, model // 2), jnp.float32),
            jax.ShapeDtypeStruct((width - done, model // 2), jnp.bfloat16),
            jax.ShapeDtypeStruct((2, model // 2), jnp.float32),
        ],
        scratch_shapes=[
            pltpu.VMEM((done, model // 2), jnp.bfloat16),
            pltpu.VMEM((ntok, part), jnp.bfloat16),
            pltpu.SemaphoreType.DMA((9,)),
        ],
        compiler_params=params(16),
        cost_estimate=cost(2 * ntok * model * done, width * model + 4 * ntok * model),
        name="early",
    )(own, oth, w_out, states, x_other, modul, gate_other, scale)


def close_kernel(early_ref, own_ref, oth_ref, w_ref, c_ref, keep_a, keep_b, send_a, send_b):
    half = early_ref.shape[0] // 2
    part = early_ref.shape[1] // 4
    for p in (3, 1, 2, 0):
        cols = slice(p * part, (p + 1) * part)
        y = early_ref[:, cols]
        y += c_ref[0:1, cols] * jnp.dot(
            own_ref[...], w_ref[:, cols], preferred_element_type=jnp.float32
        )
        y += c_ref[1:2, cols] * jnp.dot(
            oth_ref[...], w_ref[:, cols], preferred_element_type=jnp.float32
        )
        a, b = y[:half], y[half:]
        at = slice((p // 2) * part, (p // 2 + 1) * part)
        if p % 2:
            send_a[:, at] = a.astype(jnp.bfloat16)
        else:
            keep_a[:, at] = a
        at = slice((p % 2) * part, (p % 2 + 1) * part)
        if p // 2:
            send_b[:, at] = b.astype(jnp.bfloat16)
        else:
            keep_b[:, at] = b


def close(sofar, own, oth, w_last, coef):
    ntok, width = sofar.shape
    keep = jax.ShapeDtypeStruct((ntok // 2, width // 2), jnp.float32)
    send = jax.ShapeDtypeStruct((ntok // 2, width // 2), jnp.bfloat16)
    return pl.pallas_call(
        close_kernel,
        in_specs=vmem(5),
        out_specs=vmem(4),
        out_shape=[keep, keep, send, send],
        compiler_params=params(16),
        cost_estimate=cost(4 * ntok * width * own.shape[1], 8 * ntok * width),
        name="close",
    )(sofar, own, oth, w_last, coef)


def neighbours(value, distance):
    count = lax.axis_size("seq")
    out = []
    for odd in (0, 1):
        lows = [i for i in range(count - distance) if (i // distance) % 2 == odd]
        route = [(i, i + distance) for i in lows] + [(i + distance, i) for i in lows]
        out.append(lax.ppermute(value, "seq", route))
    return out


def crossed(value, axis, bit):
    return lax.ppermute(value, axis, [(i, i ^ bit) for i in range(lax.axis_size(axis))])


def shards(
    hidden_states, modulation, w_query, w_key, w_value, w_out, block_ids, block_count, guidance
):
    _, ntok, model = hidden_states.shape
    tiles = block_ids.shape[0]
    width = w_query.shape[1]
    branch = lax.axis_index("guid")
    tp_here = lax.axis_index("tp")
    reach_dev = min(4, (lax.axis_size("seq") - 1) // 2)
    part = model // (2 * lax.axis_size("tp"))
    cut = int(width * FIRST_VALUES) // PAIR * PAIR
    modul = jnp.transpose(modulation, (1, 0, 2))

    h = norm(hidden_states, modul)

    def project(weight):
        return jnp.dot(h, weight, preferred_element_type=jnp.float32).astype(jnp.bfloat16)

    def near(value):
        out = [value]
        for distance in range(1, reach_dev + 1):
            out += neighbours(value, distance)
        return out

    keys = near(project(w_key))
    value = project(w_value)
    values = [near(value[:, :cut]), near(value[:, cut:])]
    query = project(w_query)

    there = (1 - branch) * (model // 2) + tp_here * part
    x_other = crossed(lax.dynamic_slice_in_dim(hidden_states[0], there, part, 1), "guid", 1)
    gate_other = crossed(modul[2:3], "guid", 1)

    if reach_dev == 1:
        span = (2 * tiles + 1) * (ntok // tiles)
        p, inv = weigh(block_ids, block_count, query, keys, span)
        own = [gather(p, inv, values[0], 0, tiles), gather(p, inv, values[1], cut // PAIR, tiles)]
    else:
        own = [
            attend(block_ids, block_count, query[:, at], [k[:, at] for k in keys], v)
            for at, v in zip((slice(0, cut), slice(cut, width)), values)
        ]
    other = [crossed(one, "guid", 1) for one in own]

    sofar, w_last, coef = early(
        own[0], other[0], w_out, hidden_states, x_other, modul, gate_other, guidance
    )
    keep_a, keep_b, send_a, send_b = close(sofar, own[1], other[1], w_last, coef)
    got_a = crossed(send_a, "tp", 1)
    got_b = crossed(send_b, "tp", 2)
    sum_a = keep_a + got_a.astype(jnp.float32)
    sum_b = keep_b + got_b.astype(jnp.float32)
    last_a = crossed(sum_a[:, part:].astype(jnp.bfloat16), "tp", 2)
    last_b = crossed(sum_b[:, part:].astype(jnp.bfloat16), "tp", 1)
    return jnp.concatenate(
        [
            (sum_a[:, :part] + last_a.astype(jnp.float32)).astype(jnp.bfloat16),
            (sum_b[:, :part] + last_b.astype(jnp.float32)).astype(jnp.bfloat16),
        ],
        axis=0,
    )


def solution(mesh):
    in_specs = (
        P("guid", "seq", None),
        P("guid", None, None),
        P(None, "tp"),
        P(None, "tp"),
        P(None, "tp"),
        P("tp", None),
        P("seq", None),
        P("seq"),
        P(),
    )
    out_specs = P("seq", ("guid", "tp"))
    return jax.shard_map(shards, mesh=mesh, in_specs=in_specs, out_specs=out_specs, check_vma=False)
```

time: 127 us -> 73.1 us (0.58)
  waiting for transfers between devices: 35.1 us -> 10.5 us
  starting transfers between devices: 7.31 us -> 31.6 us
  local copies, waits for them, and re-layouts: 27 us -> 4.15 us
  matrix products: 26.3 us -> 7.65 us
  Pallas kernels: 0 us -> 17 us
  other arithmetic: 15.8 us -> 0.94 us
  between operations: 14.5 us -> 0.95 us
    reduce_scatter x1 -> x0, waiting for transfers between devices: 28.6 us -> none  [shards(): lax.psum_scatter(regroup(proj).astype(jnp.bfloat16), 'tp', scatter_dimens...]
    ppermute x3 -> x14, starting transfers between devices: 7.31 us -> 31.6 us  [the longest x6 24.2 us: neighbours(): out.append(lax.ppermute(value, 'seq', route))]
    dot_general x10 -> x3, matrix products: 26.3 us -> 7.65 us  [project(): jnp.dot(h, weight, preferred_element_type=jnp.float32).astype(jnp.bfloat16)]
    pallas_call x0 -> x6, Pallas kernels: none -> 17 us  [the longest x1 7.45 us: weigh(): pl.pallas_call(functools.partial(weigh_kernel, tiles, True), in_specs=sme...]
    dot_general x1 -> x0, local copies, waits for them, and re-layouts: 6.72 us -> none  [shards(): proj = jnp.dot(attn, w_out, preferred_element_type=jnp.float32)]
    reduce_sum x5 -> x0, other arithmetic: 6.18 us -> none  [the longest x3 5.04 us: attend(): new_sum = run_sum * factor + jnp.sum(expo, axis=2)]
    convert_element_type x6 -> x0, local copies, waits for them, and re-layouts: 5.33 us -> none  [the longest x1 1.64 us: shards(): regroup(proj).astype(jnp.bfloat16)]
    reshape x2 -> x0, local copies, waits for them, and re-layouts: 4.83 us -> none  [regroup(): jnp.transpose(array.reshape(count, 2, tp_count, half), (0, 2, 1, 3))]
  transfers between devices with their start and end apart: 4 -> 14, of which waited for: 4 -> 4; matrix products, arithmetic and copies ran while one was open for 24% -> 8% of each run, Pallas kernels for 0% -> 19%
where the time goes in v2:
time: 73.1 us; the launch traced here: 72.8 us
  starting transfers between devices  31.6 us (43%)
  Pallas kernels  17 us (23%)
  waiting for transfers between devices  10.5 us (14%)
  matrix products  7.65 us (10%)
  local copies, waits for them, and re-layouts  4.15 us (6%)
  between operations  0.95 us (1%)
  other arithmetic  0.94 us (1%)
    ppermute x6, starting transfers between devices, neighbours(): out.append(lax.ppermute(value, 'seq', route))  24.2 us
    ppermute x8, waiting for transfers between devices, crossed(): lax.ppermute(value, axis, [(i, i ^ bit) for i in range(lax.axis_size(axis...  10.5 us
    dot_general x3, matrix products, project(): jnp.dot(h, weight, preferred_element_type=jnp.float32).astype(jnp.bfloat16)  7.65 us
    pallas_call x1, Pallas kernels, weigh(): pl.pallas_call(functools.partial(weigh_kernel, tiles, True), in_specs=sme...  7.45 us
    ppermute x8, starting transfers between devices, crossed(): lax.ppermute(value, axis, [(i, i ^ bit) for i in range(lax.axis_size(axis...  7.43 us
    unnamed x28, local copies, waits for them, and re-layouts  4.05 us
    pallas_call x2, Pallas kernels, gather(): pl.pallas_call(functools.partial(gather_kernel, tiles, first_pair), in_sp...  3.48 us
    pallas_call x1, Pallas kernels, early(): pl.pallas_call(early_kernel, in_specs=vmem(2) + hbm * 2 + vmem(3) + smem(...  3.17 us
  transfers between devices with their start and end apart: 14, of which 4 were waited for; matrix products, arithmetic and copies ran while one was open for 8% of the time, Pallas kernels for 19%

profile of v2, /device:TPU:0, one launch (start us, length us, event | category | flops | bytes accessed | tf_op | source)
XLA Modules:
  0.0 72.8 jit_solution(7877459967673966720)
XLA Ops:
  0.0 1.7 %copy-done = bf16[1,384,3072]{2,1,0:T(8,128)(2,1)S(1)} copy-done((bf16[1,384,3072]{2,1,0:T(8,128)(2,1)S(1)}, bf16[1,384,3072]{2,1,0:T(8,128)(2,1)}, u32[]{:S(2)}) %copy-start) | copy-done | bytes 2359320
  2.4 1.8 %norm.1 = bf16[384,3072]{1,0:T(8,128)(2,1)S(1)} custom-call(bf16[1,384,3072]{2,1,0:T(8,128)(2,1)S(1)} %copy-done, f32[3,1,3072]{2,1,0:T(1,128)S(1)} %bitcast.13), custom_call_target="tpu_custom_call" | custom-call | flops 11796480 | bytes 4718592 | tf_op jit(solution)/shard_map/norm/pallas_call | solution.py:51
  4.8 2.0 %convolution_convert_fusion = bf16[384,768]{1,0:T(8,128)(2,1)S(1)} fusion(bf16[384,3072]{1,0:T(8,128)(2,1)S(1)} %norm.1, bf16[3072,768]{1,0:T(8,128)(2,1)S(1)} %copy-done.7), kind=kOutput, calls=%fused_computation | convolution fusion | flops 1812234240 | bytes 7667712 | tf_op jit(solution)/shard_map/dot_general | solution.py:383
  6.8 0.8 %collective-permute-start.3 = (bf16[384,512]{1,0:T(8,128)(2,1)S(1)}, bf16[384,512]{1,0:T(8,128)(2,1)S(1)}, u32[]{:S(2)}, u32[]{:S(2)}) collective-permute-start(bf16[384,512]{1,0:T(8,128)(2,1)S(1)} %slice.31.refs_0_), channel_id=1, source_target_pairs={{8,16},{16,8},{9,17},{17,9},{10,18},{18,10},{11,19},{19,11},{12,20... | collective-permute-start | bytes 1179656 | tf_op jit(solution)/shard_map/ppermute | solution.py:359
  7.7 6.0 %collective-permute-start.2 = (bf16[384,512]{1,0:T(8,128)(2,1)S(1)}, bf16[384,512]{1,0:T(8,128)(2,1)}, u32[]{:S(2)}, u32[]{:S(2)}) collective-permute-start(bf16[384,512]{1,0:T(8,128)(2,1)S(1)} %slice.31.refs_0_), channel_id=1, source_target_pairs={{0,8},{16,24},{8,0},{24,16},{1,9},{17,25},{9,1},{25,17},{2,10},{18... | collective-permute-start | bytes 1179656 | tf_op jit(solution)/shard_map/ppermute | solution.py:359
  13.7 2.8 %convolution_convert_fusion.1.refs_0_ = bf16[384,768]{1,0:T(8,128)(2,1)} fusion(bf16[384,3072]{1,0:T(8,128)(2,1)S(1)} %norm.1, bf16[3072,768]{1,0:T(8,128)(2,1)S(1)} %bitcast.16), kind=kOutput, calls=%fused_computation.1 | convolution fusion | flops 1812234240 | bytes 7667712 | tf_op jit(solution)/shard_map/dot_general | solution.py:383
  16.5 1.5 %collective-permute-start.1 = (bf16[384,768]{1,0:T(8,128)(2,1)}, bf16[384,768]{1,0:T(8,128)(2,1)}, u32[]{:S(2)}, u32[]{:S(2)}) collective-permute-start(bf16[384,768]{1,0:T(8,128)(2,1)} %convolution_convert_fusion.1.refs_0_), channel_id=1, source_target_pairs={{8,16},{16,8},{9,17},{17,9},{10,18},{18,10},{11,19},{19,11},{12,20... | collective-permute-start | bytes 1769480 | tf_op jit(solution)/shard_map/ppermute | solution.py:359
  18.0 1.0 %collective-permute-start = (bf16[384,768]{1,0:T(8,128)(2,1)}, bf16[384,768]{1,0:T(8,128)(2,1)}, u32[]{:S(2)}, u32[]{:S(2)}) collective-permute-start(bf16[384,768]{1,0:T(8,128)(2,1)} %convolution_convert_fusion.1.refs_0_), channel_id=1, source_target_pairs={{0,8},{16,24},{8,0},{24,16},{1,9},{17,25},{9,1},{25,17},{2,10},{18... | collective-permute-start | bytes 1769480 | tf_op jit(solution)/shard_map/ppermute | solution.py:359
  19.0 1.0 %collective-permute-start.8 = (bf16[384,256]{1,0:T(8,128)(2,1)S(1)}, bf16[384,256]{1,0:T(8,128)(2,1)S(1)}, u32[]{:S(2)}, u32[]{:S(2)}) collective-permute-start(bf16[384,256]{1,0:T(8,128)(2,1)S(1)} %slice.32.refs_0_), channel_id=1, source_target_pairs={{8,16},{16,8},{9,17},{17,9},{10,18},{18,10},{11,19},{19,11},{12,20... | collective-permute-start | bytes 589832 | tf_op jit(solution)/shard_map/ppermute | solution.py:359
  20.1 2.8 %convolution_convert_fusion.2.q_ref = bf16[384,768]{1,0:T(8,128)(2,1)} fusion(bf16[384,3072]{1,0:T(8,128)(2,1)S(1)} %norm.1, bf16[3072,768]{1,0:T(8,128)(2,1)S(1)} %bitcast.18), kind=kOutput, calls=%fused_computation.2 | convolution fusion | flops 1812234240 | bytes 7667712 | tf_op jit(solution)/shard_map/dot_general | solution.py:383
  22.9 13.9 %collective-permute-start.7 = (bf16[384,256]{1,0:T(8,128)(2,1)S(1)}, bf16[384,256]{1,0:T(8,128)(2,1)S(1)}, u32[]{:S(2)}, u32[]{:S(2)}) collective-permute-start(bf16[384,256]{1,0:T(8,128)(2,1)S(1)} %slice.32.refs_0_), channel_id=1, source_target_pairs={{0,8},{16,24},{8,0},{24,16},{1,9},{17,25},{9,1},{25,17},{2,10},{18... | collective-permute-start | bytes 589832 | tf_op jit(solution)/shard_map/ppermute | solution.py:359
  36.9 1.1 %copy-done.6 = bf16[384,768]{1,0:T(8,128)(2,1)S(1)} copy-done((bf16[384,768]{1,0:T(8,128)(2,1)S(1)}, bf16[384,768]{1,0:T(8,128)(2,1)}, u32[]{:S(2)}) %copy-start.6) | copy-done | bytes 589848
  38.0 7.5 %weigh.1 = (bf16[18,256,896]{2,1,0:T(8,128)(2,1)S(1)}, f32[18,128,128]{2,1,0:T(8,128)S(1)}) custom-call(s32[3,7]{1,0:T(4,128)S(1)} %copy-done.4, s32[3]{0:T(128)S(1)} %copy-done.5, bf16[384,768]{1,0:T(8,128)(2,1)S(1)} %copy-done.6, bf16[384,768]{1,0:T(8,128)(2,1)} %convolution_convert_fusion.1.refs_0_, bf16[384,768]{1,0:T(8,128)(2,1)} %collective-permute-done.refs_1_, ...), custom_call_target="tpu_custom_call" | custom-call | flops 1056964608 | bytes 8257536 | tf_op jit(solution)/shard_map/weigh/pallas_call | solution.py:178
  45.5 0.9 %gather.3.own_ref = bf16[384,256]{1,0:T(8,128)(2,1)S(1)} custom-call(bf16[18,256,896]{2,1,0:T(8,128)(2,1)S(1)} %get-tuple-element.14.p_ref, f32[18,128,128]{2,1,0:T(8,128)S(1)} %get-tuple-element.15.inv_ref, bf16[384,256]{1,0:T(8,128)(2,1)S(1)} %slice.32.refs_0_, bf16[384,256]{1,0:T(8,128)(2,1)S(1)} %collective-permute-done.7.refs_1_, ...), custom_call_target="tpu_custom_call" | custom-call | flops 352321536 | bytes 2752512 | tf_op jit(solution)/shard_map/gather/pallas_call | solution.py:208
  47.0 2.6 %gather.2.own_ref = bf16[384,512]{1,0:T(8,128)(2,1)S(1)} custom-call(bf16[18,256,896]{2,1,0:T(8,128)(2,1)S(1)} %get-tuple-element.14.p_ref, f32[18,128,128]{2,1,0:T(8,128)S(1)} %get-tuple-element.15.inv_ref, bf16[384,512]{1,0:T(8,128)(2,1)S(1)} %slice.31.refs_0_, bf16[384,512]{1,0:T(8,128)(2,1)} %collective-permute-done.2.refs_1_, ...), custom_call_target="tpu_custom_call" | custom-call | flops 704643072 | bytes 5505024 | tf_op jit(solution)/shard_map/gather/pallas_call | solution.py:208
  51.4 3.2 %early.1 = (f32[384,1536]{1,0:T(8,128)S(1)}, bf16[256,1536]{1,0:T(8,128)(2,1)S(1)}, f32[2,1536]{1,0:T(2,128)S(1)}) custom-call(bf16[384,512]{1,0:T(8,128)(2,1)S(1)} %gather.2.own_ref, bf16[384,512]{1,0:T(8,128)(2,1)S(1)} %collective-permute-done.4.oth_ref, bf16[768,3072]{1,0:T(8,128)(2,1)S(1)} %bitcast.12, bf16[1,384,3072]{2,1,0:T(8,128)(2,1)S(1)} %copy-done.1, ...), custom_call_target="tpu_custom_call" | custom-call | flops 1207959552 | bytes 7077888 | tf_op jit(solution)/shard_map/early/pallas_call | solution.py:293
  54.6 1.1 %close.1 = (f32[192,768]{1,0:T(8,128)S(1)}, f32[192,768]{1,0:T(8,128)S(1)}, bf16[192,768]{1,0:T(8,128)(2,1)S(1)}, bf16[192,768]{1,0:T(8,128)(2,1)S(1)}) custom-call(f32[384,1536]{1,0:T(8,128)S(1)} %get-tuple-element.16.early_ref, bf16[384,256]{1,0:T(8,128)(2,1)S(1)} %gather.3.own_ref, bf16[384,256]{1,0:T(8,128)(2,1)S(1)} %collective-permute-done.9.oth_ref, ...), custom_call_target="tpu_custom_call" | custom-call | flops 603979776 | bytes 4718592 | tf_op jit(solution)/shard_map/close/pallas_call | solution.py:342
  55.7 1.6 %collective-permute-start.10 = (bf16[192,768]{1,0:T(8,128)(2,1)S(1)}, bf16[192,768]{1,0:T(8,128)(2,1)S(1)}, u32[]{:S(2)}, u32[]{:S(2)}) collective-permute-start(bf16[192,768]{1,0:T(8,128)(2,1)S(1)} %get-tuple-element.20), channel_id=1, source_target_pairs={{0,1},{1,0},{2,3},{3,2},{4,5},{5,4},{6,7},{7,6},{8,9},{9,8},{10,11... | collective-permute-start | bytes 884744 | tf_op jit(solution)/shard_map/ppermute | solution.py:364
  57.3 1.5 %collective-permute-start.12 = (bf16[192,768]{1,0:T(8,128)(2,1)S(1)}, bf16[192,768]{1,0:T(8,128)(2,1)S(1)}, u32[]{:S(2)}, u32[]{:S(2)}) collective-permute-start(bf16[192,768]{1,0:T(8,128)(2,1)S(1)} %get-tuple-element.22), channel_id=1, source_target_pairs={{0,2},{1,3},{2,0},{3,1},{4,6},{5,7},{6,4},{7,5},{8,10},{9,11},{10,... | collective-permute-start | bytes 884744 | tf_op jit(solution)/shard_map/ppermute | solution.py:364
  58.8 6.3 %collective-permute-done.10 = bf16[192,768]{1,0:T(8,128)(2,1)S(1)} collective-permute-done((bf16[192,768]{1,0:T(8,128)(2,1)S(1)}, bf16[192,768]{1,0:T(8,128)(2,1)S(1)}, u32[]{:S(2)}, u32[]{:S(2)}) %collective-permute-start.10) | collective-permute-done | bytes 294944 | tf_op jit(solution)/shard_map/ppermute | solution.py:364
  65.2 1.6 %collective-permute-start.11 = (bf16[192,384]{1,0:T(8,128)(2,1)S(1)}, bf16[192,384]{1,0:T(8,128)(2,1)S(1)}, u32[]{:S(2)}, u32[]{:S(2)}) collective-permute-start(bf16[192,384]{1,0:T(8,128)(2,1)S(1)} %slice.47), channel_id=1, source_target_pairs={{0,2},{1,3},{2,0},{3,1},{4,6},{5,7},{6,4},{7,5},{8,10},{9,11},{10,... | collective-permute-start | bytes 442376 | tf_op jit(solution)/shard_map/ppermute | solution.py:364
  66.8 1.6 %collective-permute-start.13 = (bf16[192,384]{1,0:T(8,128)(2,1)S(1)}, bf16[192,384]{1,0:T(8,128)(2,1)S(1)}, u32[]{:S(2)}, u32[]{:S(2)}) collective-permute-start(bf16[192,384]{1,0:T(8,128)(2,1)S(1)} %slice.46), channel_id=1, source_target_pairs={{0,1},{1,0},{2,3},{3,2},{4,5},{5,4},{6,7},{7,6},{8,9},{9,8},{10,11... | collective-permute-start | bytes 442376 | tf_op jit(solution)/shard_map/ppermute | solution.py:364
  68.4 2.1 %collective-permute-done.11 = bf16[192,384]{1,0:T(8,128)(2,1)S(1)} collective-permute-done((bf16[192,384]{1,0:T(8,128)(2,1)S(1)}, bf16[192,384]{1,0:T(8,128)(2,1)S(1)}, u32[]{:S(2)}, u32[]{:S(2)}) %collective-permute-start.11) | collective-permute-done | bytes 147488 | tf_op jit(solution)/shard_map/ppermute | solution.py:364
  70.6 1.5 %collective-permute-done.13 = bf16[192,384]{1,0:T(8,128)(2,1)S(1)} collective-permute-done((bf16[192,384]{1,0:T(8,128)(2,1)S(1)}, bf16[192,384]{1,0:T(8,128)(2,1)S(1)}, u32[]{:S(2)}, u32[]{:S(2)}) %collective-permute-start.13) | collective-permute-done | bytes 147488 | tf_op jit(solution)/shard_map/ppermute | solution.py:364
  (55 shorter events, 4.2 us)
Async XLA Ops:
  2.4 11.3 %slice-start.2 = ((s8[4718592]{0:T(1024)(128)(4,1)}), s8[4194304]{0:T(1024)(128)(4,1)S(1)}, s32[]{:S(2)}) async-start(s8[4718592]{0:T(1024)(128)(4,1)} %bitcast.15), calls=%async_computation.2 | async-start | bytes 8388608
  4.8 8.9 %slice-start.3 = ((s8[4718592]{0:T(1024)(128)(4,1)}), s8[524288]{0:T(1024)(128)(4,1)S(1)}, s32[]{:S(2)}) async-start(s8[4718592]{0:T(1024)(128)(4,1)} %bitcast.15), calls=%async_computation.3 | async-start | bytes 1048576
  6.8 13.2 %slice-start.4 = ((s8[4718592]{0:T(1024)(128)(4,1)}), s8[4194304]{0:T(1024)(128)(4,1)S(1)}, s32[]{:S(2)}) async-start(s8[4718592]{0:T(1024)(128)(4,1)} %bitcast.17), calls=%async_computation.4 | async-start | bytes 8388608
  6.8 13.2 %slice-start.5 = ((s8[4718592]{0:T(1024)(128)(4,1)}), s8[524288]{0:T(1024)(128)(4,1)S(1)}, s32[]{:S(2)}) async-start(s8[4718592]{0:T(1024)(128)(4,1)} %bitcast.17), calls=%async_computation.5 | async-start | bytes 1048576
  6.8 40.1 %collective-permute-start.3 = (bf16[384,512]{1,0:T(8,128)(2,1)S(1)}, bf16[384,512]{1,0:T(8,128)(2,1)S(1)}, u32[]{:S(2)}, u32[]{:S(2)}) collective-permute-start(bf16[384,512]{1,0:T(8,128)(2,1)S(1)} %slice.31.refs_0_), channel_id=1, source_target_pairs={{8,16},{16,8},{9,17},{17,9},{10,18},{18,10},{11,19},{19,11},{12,20... | collective-permute-start | bytes 1179656 | tf_op jit(solution)/shard_map/ppermute | solution.py:359
  7.7 39.3 %collective-permute-start.2 = (bf16[384,512]{1,0:T(8,128)(2,1)S(1)}, bf16[384,512]{1,0:T(8,128)(2,1)}, u32[]{:S(2)}, u32[]{:S(2)}) collective-permute-start(bf16[384,512]{1,0:T(8,128)(2,1)S(1)} %slice.31.refs_0_), channel_id=1, source_target_pairs={{0,8},{16,24},{8,0},{24,16},{1,9},{17,25},{9,1},{25,17},{2,10},{18... | collective-permute-start | bytes 1179656 | tf_op jit(solution)/shard_map/ppermute | solution.py:359
  16.5 6.4 %collective-permute-start.1 = (bf16[384,768]{1,0:T(8,128)(2,1)}, bf16[384,768]{1,0:T(8,128)(2,1)}, u32[]{:S(2)}, u32[]{:S(2)}) collective-permute-start(bf16[384,768]{1,0:T(8,128)(2,1)} %convolution_convert_fusion.1.refs_0_), channel_id=1, source_target_pairs={{8,16},{16,8},{9,17},{17,9},{10,18},{18,10},{11,19},{19,11},{12,20... | collective-permute-start | bytes 1769480 | tf_op jit(solution)/shard_map/ppermute | solution.py:359
  18.0 18.8 %collective-permute-start = (bf16[384,768]{1,0:T(8,128)(2,1)}, bf16[384,768]{1,0:T(8,128)(2,1)}, u32[]{:S(2)}, u32[]{:S(2)}) collective-permute-start(bf16[384,768]{1,0:T(8,128)(2,1)} %convolution_convert_fusion.1.refs_0_), channel_id=1, source_target_pairs={{0,8},{16,24},{8,0},{24,16},{1,9},{17,25},{9,1},{25,17},{2,10},{18... | collective-permute-start | bytes 1769480 | tf_op jit(solution)/shard_map/ppermute | solution.py:359
  19.0 17.8 %copy-start.1 = (bf16[1,384,3072]{2,1,0:T(8,128)(2,1)S(1)}, bf16[1,384,3072]{2,1,0:T(8,128)(2,1)}, u32[]{:S(2)}) copy-start(bf16[1,384,3072]{2,1,0:T(8,128)(2,1)} %x_hbm.1) | copy-start | bytes 7077892
  19.0 17.9 %copy-start.4 = (s32[3,7]{1,0:T(4,128)S(1)}, s32[3,7]{1,0:T(4,128)}, u32[]{:S(2)}) copy-start(s32[3,7]{1,0:T(4,128)} %ids_ref.1) | copy-start | bytes 256
  19.0 17.9 %copy-start.5 = (s32[3]{0:T(128)S(1)}, s32[3]{0:T(128)}, u32[]{:S(2)}) copy-start(s32[3]{0:T(128)} %count_ref.1) | copy-start | bytes 40
  19.0 26.4 %collective-permute-start.8 = (bf16[384,256]{1,0:T(8,128)(2,1)S(1)}, bf16[384,256]{1,0:T(8,128)(2,1)S(1)}, u32[]{:S(2)}, u32[]{:S(2)}) collective-permute-start(bf16[384,256]{1,0:T(8,128)(2,1)S(1)} %slice.32.refs_0_), channel_id=1, source_target_pairs={{8,16},{16,8},{9,17},{17,9},{10,18},{18,10},{11,19},{19,11},{12,20... | collective-permute-start | bytes 589832 | tf_op jit(solution)/shard_map/ppermute | solution.py:359
  22.9 22.6 %collective-permute-start.7 = (bf16[384,256]{1,0:T(8,128)(2,1)S(1)}, bf16[384,256]{1,0:T(8,128)(2,1)S(1)}, u32[]{:S(2)}, u32[]{:S(2)}) collective-permute-start(bf16[384,256]{1,0:T(8,128)(2,1)S(1)} %slice.32.refs_0_), channel_id=1, source_target_pairs={{0,8},{16,24},{8,0},{24,16},{1,9},{17,25},{9,1},{25,17},{2,10},{18... | collective-permute-start | bytes 589832 | tf_op jit(solution)/shard_map/ppermute | solution.py:359
  36.8 14.6 %collective-permute-start.5 = (bf16[384,384]{1,0:T(8,128)(2,1)S(1)}, bf16[384,384]{1,0:T(8,128)(2,1)S(1)}, u32[]{:S(2)}, u32[]{:S(2)}) collective-permute-start(bf16[384,384]{1,0:T(8,128)(2,1)S(1)} %dynamic-slice_bitcast_fusion), channel_id=1, source_target_pairs={{0,4},{4,0},{1,5},{5,1},{2,6},{6,2},{3,7},{7,3},{8,12},{12,8},{9,1... | collective-permute-start | bytes 884744 | tf_op jit(solution)/shard_map/ppermute | solution.py:364
  45.5 5.9 %slice-start = ((s8[4718592]{0:T(1024)(128)(4,1)}), s8[4194304]{0:T(1024)(128)(4,1)S(1)}, s32[]{:S(2)}) async-start(s8[4718592]{0:T(1024)(128)(4,1)} %bitcast.11), calls=%async_computation | async-start | bytes 8388608
  46.4 3.7 %copy-start.3 = (f32[1,3,3072]{2,0,1:T(1,128)S(1)}, f32[1,3,3072]{2,0,1:T(1,128)}, u32[]{:S(2)}) copy-start(f32[1,3,3072]{2,0,1:T(1,128)} %param.10) | copy-start | bytes 110596
  46.4 5.0 %slice-start.1 = ((s8[4718592]{0:T(1024)(128)(4,1)}), s8[524288]{0:T(1024)(128)(4,1)S(1)}, s32[]{:S(2)}) async-start(s8[4718592]{0:T(1024)(128)(4,1)} %bitcast.11), calls=%async_computation.1 | async-start | bytes 1048576
  46.4 8.2 %collective-permute-start.9 = (bf16[384,256]{1,0:T(8,128)(2,1)S(1)}, bf16[384,256]{1,0:T(8,128)(2,1)S(1)}, u32[]{:S(2)}, u32[]{:S(2)}) collective-permute-start(bf16[384,256]{1,0:T(8,128)(2,1)S(1)} %gather.3.own_ref), channel_id=1, source_target_pairs={{0,4},{4,0},{1,5},{5,1},{2,6},{6,2},{3,7},{7,3},{8,12},{12,8},{9,1... | collective-permute-start | bytes 589832 | tf_op jit(solution)/shard_map/ppermute | solution.py:364
  49.6 1.9 %collective-permute-start.4 = (bf16[384,512]{1,0:T(8,128)(2,1)S(1)}, bf16[384,512]{1,0:T(8,128)(2,1)S(1)}, u32[]{:S(2)}, u32[]{:S(2)}) collective-permute-start(bf16[384,512]{1,0:T(8,128)(2,1)S(1)} %gather.2.own_ref), channel_id=1, source_target_pairs={{0,4},{4,0},{1,5},{5,1},{2,6},{6,2},{3,7},{7,3},{8,12},{12,8},{9,1... | collective-permute-start | bytes 1179656 | tf_op jit(solution)/shard_map/ppermute | solution.py:364
  50.0 1.4 %collective-permute-start.6 = (f32[1,1,3072]{2,1,0:T(1,128)S(1)}, f32[1,1,3072]{2,1,0:T(1,128)S(1)}, u32[]{:S(2)}, u32[]{:S(2)}) collective-permute-start(f32[1,1,3072]{2,1,0:T(1,128)S(1)} %slice_bitcast_fusion), channel_id=1, source_target_pairs={{0,4},{4,0},{1,5},{5,1},{2,6},{6,2},{3,7},{7,3},{8,12},{12,8},{9,1... | collective-permute-start | bytes 36872 | tf_op jit(solution)/shard_map/ppermute | solution.py:364
  55.7 9.4 %collective-permute-start.10 = (bf16[192,768]{1,0:T(8,128)(2,1)S(1)}, bf16[192,768]{1,0:T(8,128)(2,1)S(1)}, u32[]{:S(2)}, u32[]{:S(2)}) collective-permute-start(bf16[192,768]{1,0:T(8,128)(2,1)S(1)} %get-tuple-element.20), channel_id=1, source_target_pairs={{0,1},{1,0},{2,3},{3,2},{4,5},{5,4},{6,7},{7,6},{8,9},{9,8},{10,11... | collective-permute-start | bytes 884744 | tf_op jit(solution)/shard_map/ppermute | solution.py:364
  57.3 9.5 %collective-permute-start.12 = (bf16[192,768]{1,0:T(8,128)(2,1)S(1)}, bf16[192,768]{1,0:T(8,128)(2,1)S(1)}, u32[]{:S(2)}, u32[]{:S(2)}) collective-permute-start(bf16[192,768]{1,0:T(8,128)(2,1)S(1)} %get-tuple-element.22), channel_id=1, source_target_pairs={{0,2},{1,3},{2,0},{3,1},{4,6},{5,7},{6,4},{7,5},{8,10},{9,11},{10,... | collective-permute-start | bytes 884744 | tf_op jit(solution)/shard_map/ppermute | solution.py:364
  65.2 5.4 %collective-permute-start.11 = (bf16[192,384]{1,0:T(8,128)(2,1)S(1)}, bf16[192,384]{1,0:T(8,128)(2,1)S(1)}, u32[]{:S(2)}, u32[]{:S(2)}) collective-permute-start(bf16[192,384]{1,0:T(8,128)(2,1)S(1)} %slice.47), channel_id=1, source_target_pairs={{0,2},{1,3},{2,0},{3,1},{4,6},{5,7},{6,4},{7,5},{8,10},{9,11},{10,... | collective-permute-start | bytes 442376 | tf_op jit(solution)/shard_map/ppermute | solution.py:364
  66.8 5.2 %collective-permute-start.13 = (bf16[192,384]{1,0:T(8,128)(2,1)S(1)}, bf16[192,384]{1,0:T(8,128)(2,1)S(1)}, u32[]{:S(2)}, u32[]{:S(2)}) collective-permute-start(bf16[192,384]{1,0:T(8,128)(2,1)S(1)} %slice.46), channel_id=1, source_target_pairs={{0,1},{1,0},{2,3},{3,2},{4,5},{5,4},{6,7},{7,6},{8,9},{9,8},{10,11... | collective-permute-start | bytes 442376 | tf_op jit(solution)/shard_map/ppermute | solution.py:364
  (4 other events, 5.8 us)

commit v3 on v2

--- a/solution.py
+++ b/solution.py
@@ -189,7 +189,7 @@
     )(block_ids, block_count, query, *pieces)
 
 
-def gather_kernel(tiles, first_pair, p_ref, inv_ref, *refs):
+def gather_kernel(tiles, first_pair, p_ref, inv_ref, _, *refs):
     pieces, o_ref = refs[:-1], refs[-1]
     tile_len = o_ref.shape[0] // tiles
     pairs = o_ref.shape[1] // PAIR
@@ -203,17 +203,17 @@
         o_ref[rows, columns(pair)] = (by_head(acc, PAIR) * inv_ref[slot]).astype(jnp.bfloat16)
 
 
-def gather(p, inv, pieces, first_pair, tiles):
+def gather(p, inv, after, pieces, first_pair, tiles):
     ntok, width = pieces[0].shape
     return pl.pallas_call(
         functools.partial(gather_kernel, tiles, first_pair),
-        in_specs=vmem(2 + len(pieces)),
+        in_specs=vmem(2) + [pl.BlockSpec(memory_space=pl.ANY)] + vmem(len(pieces)),
         out_specs=vmem(1)[0],
         out_shape=jax.ShapeDtypeStruct((ntok, width), jnp.bfloat16),
         compiler_params=params(24),
-        cost_estimate=cost(4 * ntok * p.shape[2] * width, 2 * ntok * p.shape[2] * width / HD),
+        cost_estimate=cost(2e10, 2 * ntok * p.shape[2] * width / HD),
         name="gather",
-    )(p, inv, *pieces)
+    )(p, inv, after, *pieces)
 
 
 def attend_kernel(tiles, slots, ids_ref, count_ref, q_ref, *refs):
@@ -246,64 +246,51 @@
     )(block_ids, block_count, query, *keys, *values)
 
 
-def early_kernel(own_ref, oth_ref, w_hbm, x_hbm, xo_ref, mod_ref, gate_ref, scale_ref, *refs):
-    y_ref, wl_ref, c_ref, wb, xb, sems = refs
+def partner_starts(model, part):
+    branch, here = lax.axis_index("guid"), lax.axis_index("tp")
+    return [branch * (model // 2) + lax.bitwise_xor(here, p) * part for p in range(4)]
+
+
+def early_kernel(own_ref, oth_ref, w_ref, x_hbm, xo_ref, mod_ref, gate_ref, scale_ref, *refs):
+    y_ref, c_ref, xb, sem = refs
     part = xb.shape[1]
-    model = x_hbm.shape[2]
     done = own_ref.shape[1]
-    branch, here = lax.axis_index("guid"), lax.axis_index("tp")
-    starts = [branch * (model // 2) + lax.bitwise_xor(here, p) * part for p in range(4)]
-    spots = [slice(p * part, (p + 1) * part) for p in range(4)]
-    copies = [
-        pltpu.make_async_copy(x_hbm.at[0, :, aligned(starts[0], part)], xb, sems.at[8])
-    ]
-    for p in range(4):
-        src = w_hbm.at[pl.ds(0, done), aligned(starts[p], part)]
-        copies.append(pltpu.make_async_copy(src, wb.at[:, spots[p]], sems.at[p]))
-    for p in range(4):
-        src = w_hbm.at[pl.ds(done, wl_ref.shape[0]), aligned(starts[p], part)]
-        copies.append(pltpu.make_async_copy(src, wl_ref.at[:, spots[p]], sems.at[4 + p]))
-    for copy in copies:
-        copy.start()
+    starts = partner_starts(x_hbm.shape[2], part)
+    copy = pltpu.make_async_copy(x_hbm.at[0, :, aligned(starts[0], part)], xb, sem)
+    copy.start()
     scale = scale_ref[0]
+    branch = lax.axis_index("guid")
     mine = jnp.where(branch == 0, scale, 1.0 - scale)
     others = jnp.where(branch == 0, 1.0 - scale, scale)
-    copies[0].wait()
-    base = mine * xb[...].astype(jnp.float32) + others * xo_ref[...].astype(jnp.float32)
-    for p in range(4):
+    for p in (3, 2, 1, 0):
         at = aligned(starts[p], part)
+        spot = slice(p * part, (p + 1) * part)
         own_gate = mine * mod_ref[2, :, at]
         oth_gate = others * gate_ref[0, :, at]
-        c_ref[0:1, spots[p]] = own_gate
-        c_ref[1:2, spots[p]] = oth_gate
-        copies[1 + p].wait()
-        weight = wb[:, spots[p]]
+        c_ref[0:1, spot] = own_gate
+        c_ref[1:2, spot] = oth_gate
+        weight = w_ref[0:done, at]
         y = own_gate * jnp.dot(own_ref[...], weight, preferred_element_type=jnp.float32)
         y += oth_gate * jnp.dot(oth_ref[...], weight, preferred_element_type=jnp.float32)
-        y_ref[:, spots[p]] = y + base if p == 0 else y
-    for copy in copies[5:]:
-        copy.wait()
+        if p == 0:
+            copy.wait()
+            y += mine * xb[...].astype(jnp.float32) + others * xo_ref[...].astype(jnp.float32)
+        y_ref[:, spot] = y
 
 
 def early(own, oth, w_out, states, x_other, modul, gate_other, scale):
     ntok, done = own.shape
     width, model = w_out.shape
     part = x_other.shape[1]
-    hbm = [pl.BlockSpec(memory_space=pl.ANY)]
     return pl.pallas_call(
         early_kernel,
-        in_specs=vmem(2) + hbm * 2 + vmem(3) + smem(1),
-        out_specs=vmem(3),
+        in_specs=vmem(3) + [pl.BlockSpec(memory_space=pl.ANY)] + vmem(3) + smem(1),
+        out_specs=vmem(2),
         out_shape=[
             jax.ShapeDtypeStruct((ntok, model // 2), jnp.float32),
-            jax.ShapeDtypeStruct((width - done, model // 2), jnp.bfloat16),
             jax.ShapeDtypeStruct((2, model // 2), jnp.float32),
         ],
-        scratch_shapes=[
-            pltpu.VMEM((done, model // 2), jnp.bfloat16),
-            pltpu.VMEM((ntok, part), jnp.bfloat16),
-            pltpu.SemaphoreType.DMA((9,)),
-        ],
+        scratch_shapes=[pltpu.VMEM((ntok, part), jnp.bfloat16), pltpu.SemaphoreType.DMA],
         compiler_params=params(16),
         cost_estimate=cost(2 * ntok * model * done, width * model + 4 * ntok * model),
         name="early",
@@ -313,15 +300,14 @@
 def close_kernel(early_ref, own_ref, oth_ref, w_ref, c_ref, keep_a, keep_b, send_a, send_b):
     half = early_ref.shape[0] // 2
     part = early_ref.shape[1] // 4
+    first = w_ref.shape[0] - own_ref.shape[1]
+    starts = partner_starts(w_ref.shape[1], part)
     for p in (3, 1, 2, 0):
         cols = slice(p * part, (p + 1) * part)
+        weight = w_ref[first:, aligned(starts[p], part)]
         y = early_ref[:, cols]
-        y += c_ref[0:1, cols] * jnp.dot(
-            own_ref[...], w_ref[:, cols], preferred_element_type=jnp.float32
-        )
-        y += c_ref[1:2, cols] * jnp.dot(
-            oth_ref[...], w_ref[:, cols], preferred_element_type=jnp.float32
-        )
+        y += c_ref[0:1, cols] * jnp.dot(own_ref[...], weight, preferred_element_type=jnp.float32)
+        y += c_ref[1:2, cols] * jnp.dot(oth_ref[...], weight, preferred_element_type=jnp.float32)
         a, b = y[:half], y[half:]
         at = slice((p // 2) * part, (p // 2 + 1) * part)
         if p % 2:
@@ -335,7 +321,7 @@
             keep_b[:, at] = b
 
 
-def close(sofar, own, oth, w_last, coef):
+def close(sofar, own, oth, w_out, coef):
     ntok, width = sofar.shape
     keep = jax.ShapeDtypeStruct((ntok // 2, width // 2), jnp.float32)
     send = jax.ShapeDtypeStruct((ntok // 2, width // 2), jnp.bfloat16)
@@ -347,7 +333,7 @@
         compiler_params=params(16),
         cost_estimate=cost(4 * ntok * width * own.shape[1], 8 * ntok * width),
         name="close",
-    )(sofar, own, oth, w_last, coef)
+    )(sofar, own, oth, w_out, coef)
 
 
 def neighbours(value, distance):
@@ -379,8 +365,8 @@
 
     h = norm(hidden_states, modul)
 
-    def project(weight):
-        return jnp.dot(h, weight, preferred_element_type=jnp.float32).astype(jnp.bfloat16)
+    def project(source, weight):
+        return jnp.dot(source, weight, preferred_element_type=jnp.float32).astype(jnp.bfloat16)
 
     def near(value):
         out = [value]
@@ -388,30 +374,31 @@
             out += neighbours(value, distance)
         return out
 
-    keys = near(project(w_key))
-    value = project(w_value)
+    key, h = lax.optimization_barrier((project(h, w_key), h))
+    keys = near(key)
+    value, h = lax.optimization_barrier((project(h, w_value), h))
     values = [near(value[:, :cut]), near(value[:, cut:])]
-    query = project(w_query)
+    query = project(h, w_query)
 
     there = (1 - branch) * (model // 2) + tp_here * part
     x_other = crossed(lax.dynamic_slice_in_dim(hidden_states[0], there, part, 1), "guid", 1)
     gate_other = crossed(modul[2:3], "guid", 1)
+    query, x_other, gate_other = lax.optimization_barrier((query, x_other, gate_other))
+
+    def finish(at, group, after):
+        if reach_dev == 1:
+            return gather(*weights, after, group, at.start // PAIR, tiles)
+        return attend(block_ids, block_count, query[:, at], [k[:, at] for k in keys], group)
 
     if reach_dev == 1:
         span = (2 * tiles + 1) * (ntok // tiles)
-        p, inv = weigh(block_ids, block_count, query, keys, span)
-        own = [gather(p, inv, values[0], 0, tiles), gather(p, inv, values[1], cut // PAIR, tiles)]
-    else:
-        own = [
-            attend(block_ids, block_count, query[:, at], [k[:, at] for k in keys], v)
-            for at, v in zip((slice(0, cut), slice(cut, width)), values)
-        ]
-    other = [crossed(one, "guid", 1) for one in own]
-
-    sofar, w_last, coef = early(
-        own[0], other[0], w_out, hidden_states, x_other, modul, gate_other, guidance
+        weights = weigh(block_ids, block_count, query, keys, span)
+    first = finish(slice(0, cut), values[0], query)
+    last = finish(slice(cut, width), values[1], first)
+    sofar, coef = early(
+        first, crossed(first, "guid", 1), w_out, hidden_states, x_other, modul, gate_other, guidance
     )
-    keep_a, keep_b, send_a, send_b = close(sofar, own[1], other[1], w_last, coef)
+    keep_a, keep_b, send_a, send_b = close(sofar, last, crossed(last, "guid", 1), w_out, coef)
     got_a = crossed(send_a, "tp", 1)
     got_b = crossed(send_b, "tp", 2)
     sum_a = keep_a + got_a.astype(jnp.float32)

time: 73.1 us -> 60.4 us (0.83)
  starting transfers between devices: 31.6 us -> 18.3 us
  matrix products: 7.65 us -> 9.03 us
  Pallas kernels: 17 us -> 15.9 us
    ppermute x6, starting transfers between devices: 24.2 us -> 11.3 us  [neighbours(): out.append(lax.ppermute(value, 'seq', route))]
    dot_general x3, matrix products: 7.65 us -> 9.03 us  [project(): jnp.dot(source, weight, preferred_element_type=jnp.float32)]
    pallas_call x1, Pallas kernels: 3.17 us -> 2.02 us  [early(): pl.pallas_call(early_kernel, in_specs=vmem(3) + [pl.BlockSpec(memory_spac...]
    unnamed x28 -> x26, local copies, waits for them, and re-layouts: 4.05 us -> 2.98 us
    slice x2, local copies, waits for them, and re-layouts: 0.04 us -> 0.97 us  [shards(): values = [near(value[:, :cut]), near(value[:, cut:])]]
  transfers between devices with their start and end apart: 14 -> 14, of which waited for: 4 -> 4; matrix products, arithmetic and copies ran while one was open for 8% -> 14% of each run, Pallas kernels for 19% -> 22%
where the time goes in v3:
time: 60.4 us; the launch traced here: 59.9 us
  starting transfers between devices  18.3 us (30%)
  Pallas kernels  15.9 us (26%)
  waiting for transfers between devices  10.7 us (18%)
  matrix products  9.03 us (15%)
  local copies, waits for them, and re-layouts  4.03 us (7%)
  between operations  0.96 us (2%)
  other arithmetic  0.92 us (2%)
    ppermute x6, starting transfers between devices, neighbours(): out.append(lax.ppermute(value, 'seq', route))  11.3 us
    ppermute x8, waiting for transfers between devices, crossed(): lax.ppermute(value, axis, [(i, i ^ bit) for i in range(lax.axis_size(axis...  10.7 us
    dot_general x3, matrix products, project(): jnp.dot(source, weight, preferred_element_type=jnp.float32)  9.03 us
    pallas_call x1, Pallas kernels, weigh(): pl.pallas_call(functools.partial(weigh_kernel, tiles, True), in_specs=sme...  7.33 us
    ppermute x8, starting transfers between devices, crossed(): lax.ppermute(value, axis, [(i, i ^ bit) for i in range(lax.axis_size(axis...  7.01 us
    pallas_call x2, Pallas kernels, gather(): pl.pallas_call(functools.partial(gather_kernel, tiles, first_pair), in_sp...  3.69 us
    unnamed x26, local copies, waits for them, and re-layouts  2.98 us
    pallas_call x1, Pallas kernels, early(): pl.pallas_call(early_kernel, in_specs=vmem(3) + [pl.BlockSpec(memory_spac...  2.02 us
  transfers between devices with their start and end apart: 14, of which 4 were waited for; matrix products, arithmetic and copies ran while one was open for 14% of the time, Pallas kernels for 22%

profile of v3, /device:TPU:0, one launch (start us, length us, event | category | flops | bytes accessed | tf_op | source)
XLA Modules:
  0.0 59.9 jit_solution(11208925657309251339)
XLA Ops:
  0.0 1.7 %copy-done = bf16[1,384,3072]{2,1,0:T(8,128)(2,1)S(1)} copy-done((bf16[1,384,3072]{2,1,0:T(8,128)(2,1)S(1)}, bf16[1,384,3072]{2,1,0:T(8,128)(2,1)}, u32[]{:S(2)}) %copy-start) | copy-done | bytes 2359320
  2.4 1.8 %norm.1 = bf16[384,3072]{1,0:T(8,128)(2,1)S(1)} custom-call(bf16[1,384,3072]{2,1,0:T(8,128)(2,1)S(1)} %copy-done, f32[3,1,3072]{2,1,0:T(1,128)S(1)} %bitcast.13), custom_call_target="tpu_custom_call" | custom-call | flops 11796480 | bytes 4718592 | tf_op jit(solution)/shard_map/norm/pallas_call | solution.py:51
  4.8 2.0 %convolution_convert_fusion.2.refs_0_ = bf16[384,768]{1,0:T(8,128)(2,1)S(1)} fusion(bf16[384,3072]{1,0:T(8,128)(2,1)S(1)} %norm.1, bf16[3072,768]{1,0:T(8,128)(2,1)S(1)} %copy-done.8), kind=kOutput, calls=%fused_computation.2 | convolution fusion | flops 1812234240 | bytes 7667712 | tf_op jit(solution)/shard_map/dot_general | solution.py:369
  6.8 3.1 %collective-permute-start.2 = (bf16[384,768]{1,0:T(8,128)(2,1)S(1)}, bf16[384,768]{1,0:T(8,128)(2,1)}, u32[]{:S(2)}, u32[]{:S(2)}) collective-permute-start(bf16[384,768]{1,0:T(8,128)(2,1)S(1)} %convolution_convert_fusion.2.refs_0_), channel_id=1, source_target_pairs={{0,8},{16,24},{8,0},{24,16},{1,9},{17,25},{9,1},{25,17},{2,10},{18... | collective-permute-start | bytes 1769480 | tf_op jit(solution)/shard_map/ppermute | solution.py:345
  9.9 1.5 %collective-permute-start.3 = (bf16[384,768]{1,0:T(8,128)(2,1)S(1)}, bf16[384,768]{1,0:T(8,128)(2,1)}, u32[]{:S(2)}, u32[]{:S(2)}) collective-permute-start(bf16[384,768]{1,0:T(8,128)(2,1)S(1)} %convolution_convert_fusion.2.refs_0_), channel_id=1, source_target_pairs={{8,16},{16,8},{9,17},{17,9},{10,18},{18,10},{11,19},{19,11},{12,20... | collective-permute-start | bytes 1769480 | tf_op jit(solution)/shard_map/ppermute | solution.py:345
  11.4 2.0 %convolution_convert_fusion.1 = bf16[384,768]{1,0:T(8,128)(2,1)S(1)} fusion(bf16[384,3072]{1,0:T(8,128)(2,1)S(1)} %norm.1, bf16[3072,768]{1,0:T(8,128)(2,1)S(1)} %bitcast.16), kind=kOutput, calls=%fused_computation.1 | convolution fusion | flops 1812234240 | bytes 7667712 | tf_op jit(solution)/shard_map/dot_general | solution.py:369
  13.4 3.7 %collective-permute-start.4 = (bf16[384,512]{1,0:T(8,128)(2,1)S(1)}, bf16[384,512]{1,0:T(8,128)(2,1)}, u32[]{:S(2)}, u32[]{:S(2)}) collective-permute-start(bf16[384,512]{1,0:T(8,128)(2,1)S(1)} %slice.25.refs_0_), channel_id=1, source_target_pairs={{0,8},{16,24},{8,0},{24,16},{1,9},{17,25},{9,1},{25,17},{2,10},{18... | collective-permute-start | bytes 1179656 | tf_op jit(solution)/shard_map/ppermute | solution.py:345
  17.1 1.4 %collective-permute-start.5 = (bf16[384,512]{1,0:T(8,128)(2,1)S(1)}, bf16[384,512]{1,0:T(8,128)(2,1)}, u32[]{:S(2)}, u32[]{:S(2)}) collective-permute-start(bf16[384,512]{1,0:T(8,128)(2,1)S(1)} %slice.25.refs_0_), channel_id=1, source_target_pairs={{8,16},{16,8},{9,17},{17,9},{10,18},{18,10},{11,19},{19,11},{12,20... | collective-permute-start | bytes 1179656 | tf_op jit(solution)/shard_map/ppermute | solution.py:345
  18.6 1.1 %collective-permute-done.1.gate_ref = f32[1,1,3072]{2,1,0:T(1,128)S(1)} collective-permute-done((f32[1,1,3072]{2,1,0:T(1,128)S(1)}, f32[1,1,3072]{2,1,0:T(1,128)S(1)}, u32[]{:S(2)}, u32[]{:S(2)}) %collective-permute-start.1) | collective-permute-done | bytes 12320 | tf_op jit(solution)/shard_map/ppermute | solution.py:350
  19.9 5.0 %convolution_convert_fusion.q_ref._ = bf16[384,768]{1,0:T(8,128)(2,1)S(1)} fusion(bf16[384,3072]{1,0:T(8,128)(2,1)} %copy-done.2, bf16[3072,768]{1,0:T(8,128)(2,1)} %param.11), kind=kOutput, calls=%fused_computation | convolution fusion | flops 1812234240 | bytes 7667712 | tf_op jit(solution)/shard_map/dot_general | solution.py:369
  24.9 0.9 %slice.26.refs_0_ = bf16[384,256]{1,0:T(8,128)(2,1)S(1)} slice(bf16[384,768]{1,0:T(8,128)(2,1)} %copy-done.7), slice={[0:384], [512:768]} | slice | bytes 393216 | tf_op jit(solution)/shard_map/slice | solution.py:380
  26.6 0.8 %collective-permute-start.8 = (bf16[384,256]{1,0:T(8,128)(2,1)S(1)}, bf16[384,256]{1,0:T(8,128)(2,1)S(1)}, u32[]{:S(2)}, u32[]{:S(2)}) collective-permute-start(bf16[384,256]{1,0:T(8,128)(2,1)S(1)} %slice.26.refs_0_), channel_id=1, source_target_pairs={{8,16},{16,8},{9,17},{17,9},{10,18},{18,10},{11,19},{19,11},{12,20... | collective-permute-start | bytes 589832 | tf_op jit(solution)/shard_map/ppermute | solution.py:345
  27.5 7.3 %weigh.1 = (bf16[18,256,896]{2,1,0:T(8,128)(2,1)S(1)}, f32[18,128,128]{2,1,0:T(8,128)S(1)}) custom-call(s32[3,7]{1,0:T(4,128)S(1)} %copy-done.5, s32[3]{0:T(128)S(1)} %copy-done.6, bf16[384,768]{1,0:T(8,128)(2,1)S(1)} %convolution_convert_fusion.q_ref._, bf16[384,768]{1,0:T(8,128)(2,1)S(1)} %convolution_convert_fusion.2.refs_0_, ...), custom_call_target="tpu_custom_call" | custom-call | flops 1056964608 | bytes 8257536 | tf_op jit(solution)/shard_map/weigh/pallas_call | solution.py:178
  34.9 2.8 %gather.2.own_ref._ = bf16[384,512]{1,0:T(8,128)(2,1)S(1)} custom-call(bf16[18,256,896]{2,1,0:T(8,128)(2,1)S(1)} %get-tuple-element.24.p_ref, f32[18,128,128]{2,1,0:T(8,128)S(1)} %get-tuple-element.25.inv_ref, bf16[384,768]{1,0:T(8,128)(2,1)S(1)} %convolution_convert_fusion.q_ref._, bf16[384,512]{1,0:T(8,128)(2,1)S(1)} %slice.25.refs_0_, ...), custom_call_target="tpu_custom_call" | custom-call | flops 20000000000 | bytes 5505024 | tf_op jit(solution)/shard_map/gather/pallas_call | solution.py:208
  37.9 0.9 %gather.3.own_ref = bf16[384,256]{1,0:T(8,128)(2,1)S(1)} custom-call(bf16[18,256,896]{2,1,0:T(8,128)(2,1)S(1)} %get-tuple-element.24.p_ref, f32[18,128,128]{2,1,0:T(8,128)S(1)} %get-tuple-element.25.inv_ref, bf16[384,512]{1,0:T(8,128)(2,1)S(1)} %gather.2.own_ref._, bf16[384,256]{1,0:T(8,128)(2,1)S(1)} %slice.26.refs_0_, ...), custom_call_target="tpu_custom_call" | custom-call | flops 20000000000 | bytes 2752512 | tf_op jit(solution)/shard_map/gather/pallas_call | solution.py:208
  40.0 2.0 %early.1 = (f32[384,1536]{1,0:T(8,128)S(1)}, f32[2,1536]{1,0:T(2,128)S(1)}) custom-call(bf16[384,512]{1,0:T(8,128)(2,1)S(1)} %gather.2.own_ref._, bf16[384,512]{1,0:T(8,128)(2,1)S(1)} %collective-permute-done.6.oth_ref, bf16[768,3072]{1,0:T(8,128)(2,1)S(1)} %bitcast.12, bf16[1,384,3072]{2,1,0:T(8,128)(2,1)S(1)} %copy-done.1, ...), custom_call_target="tpu_custom_call" | custom-call | flops 1207959552 | bytes 7077888 | tf_op jit(solution)/shard_map/early/pallas_call | solution.py:285
  42.0 1.1 %close.1 = (f32[192,768]{1,0:T(8,128)S(1)}, f32[192,768]{1,0:T(8,128)S(1)}, bf16[192,768]{1,0:T(8,128)(2,1)S(1)}, bf16[192,768]{1,0:T(8,128)(2,1)S(1)}) custom-call(f32[384,1536]{1,0:T(8,128)S(1)} %get-tuple-element.29.early_ref, bf16[384,256]{1,0:T(8,128)(2,1)S(1)} %gather.3.own_ref, bf16[384,256]{1,0:T(8,128)(2,1)S(1)} %collective-permute-done.9.oth_ref, ...), custom_call_target="tpu_custom_call" | custom-call | flops 603979776 | bytes 4718592 | tf_op jit(solution)/shard_map/close/pallas_call | solution.py:328
  43.1 1.6 %collective-permute-start.10 = (bf16[192,768]{1,0:T(8,128)(2,1)S(1)}, bf16[192,768]{1,0:T(8,128)(2,1)S(1)}, u32[]{:S(2)}, u32[]{:S(2)}) collective-permute-start(bf16[192,768]{1,0:T(8,128)(2,1)S(1)} %get-tuple-element.32), channel_id=1, source_target_pairs={{0,1},{1,0},{2,3},{3,2},{4,5},{5,4},{6,7},{7,6},{8,9},{9,8},{10,11... | collective-permute-start | bytes 884744 | tf_op jit(solution)/shard_map/ppermute | solution.py:350
  44.6 1.5 %collective-permute-start.12 = (bf16[192,768]{1,0:T(8,128)(2,1)S(1)}, bf16[192,768]{1,0:T(8,128)(2,1)S(1)}, u32[]{:S(2)}, u32[]{:S(2)}) collective-permute-start(bf16[192,768]{1,0:T(8,128)(2,1)S(1)} %get-tuple-element.34), channel_id=1, source_target_pairs={{0,2},{1,3},{2,0},{3,1},{4,6},{5,7},{6,4},{7,5},{8,10},{9,11},{10,... | collective-permute-start | bytes 884744 | tf_op jit(solution)/shard_map/ppermute | solution.py:350
  46.1 6.0 %collective-permute-done.10 = bf16[192,768]{1,0:T(8,128)(2,1)S(1)} collective-permute-done((bf16[192,768]{1,0:T(8,128)(2,1)S(1)}, bf16[192,768]{1,0:T(8,128)(2,1)S(1)}, u32[]{:S(2)}, u32[]{:S(2)}) %collective-permute-start.10) | collective-permute-done | bytes 294944 | tf_op jit(solution)/shard_map/ppermute | solution.py:350
  52.2 1.6 %collective-permute-start.11 = (bf16[192,384]{1,0:T(8,128)(2,1)S(1)}, bf16[192,384]{1,0:T(8,128)(2,1)S(1)}, u32[]{:S(2)}, u32[]{:S(2)}) collective-permute-start(bf16[192,384]{1,0:T(8,128)(2,1)S(1)} %slice.45), channel_id=1, source_target_pairs={{0,2},{1,3},{2,0},{3,1},{4,6},{5,7},{6,4},{7,5},{8,10},{9,11},{10,... | collective-permute-start | bytes 442376 | tf_op jit(solution)/shard_map/ppermute | solution.py:350
  53.9 1.5 %collective-permute-start.13 = (bf16[192,384]{1,0:T(8,128)(2,1)S(1)}, bf16[192,384]{1,0:T(8,128)(2,1)S(1)}, u32[]{:S(2)}, u32[]{:S(2)}) collective-permute-start(bf16[192,384]{1,0:T(8,128)(2,1)S(1)} %slice.44), channel_id=1, source_target_pairs={{0,1},{1,0},{2,3},{3,2},{4,5},{5,4},{6,7},{7,6},{8,9},{9,8},{10,11... | collective-permute-start | bytes 442376 | tf_op jit(solution)/shard_map/ppermute | solution.py:350
  55.4 2.0 %collective-permute-done.11 = bf16[192,384]{1,0:T(8,128)(2,1)S(1)} collective-permute-done((bf16[192,384]{1,0:T(8,128)(2,1)S(1)}, bf16[192,384]{1,0:T(8,128)(2,1)S(1)}, u32[]{:S(2)}, u32[]{:S(2)}) %collective-permute-start.11) | collective-permute-done | bytes 147488 | tf_op jit(solution)/shard_map/ppermute | solution.py:350
  57.5 1.6 %collective-permute-done.13 = bf16[192,384]{1,0:T(8,128)(2,1)S(1)} collective-permute-done((bf16[192,384]{1,0:T(8,128)(2,1)S(1)}, bf16[192,384]{1,0:T(8,128)(2,1)S(1)}, u32[]{:S(2)}, u32[]{:S(2)}) %collective-permute-start.13) | collective-permute-done | bytes 147488 | tf_op jit(solution)/shard_map/ppermute | solution.py:350
  (52 shorter events, 4.0 us)
Async XLA Ops:
  2.4 2.3 %copy-start.8 = (bf16[3072,768]{1,0:T(8,128)(2,1)S(1)}, bf16[3072,768]{1,0:T(8,128)(2,1)}, u32[]{:S(2)}) copy-start(bf16[3072,768]{1,0:T(8,128)(2,1)} %param.12) | copy-start | bytes 14155780
  2.4 8.9 %slice-start.2 = ((s8[4718592]{0:T(1024)(128)(4,1)}), s8[4194304]{0:T(1024)(128)(4,1)S(1)}, s32[]{:S(2)}) async-start(s8[4718592]{0:T(1024)(128)(4,1)} %bitcast.15), calls=%async_computation.2 | async-start | bytes 8388608
  4.8 6.6 %copy-start.2 = (bf16[384,3072]{1,0:T(8,128)(2,1)}, bf16[384,3072]{1,0:T(8,128)(2,1)S(1)}, u32[]{:S(2)}) copy-start(bf16[384,3072]{1,0:T(8,128)(2,1)S(1)} %norm.1) | copy-start | bytes 7077892
  4.8 6.6 %slice-start.3 = ((s8[4718592]{0:T(1024)(128)(4,1)}), s8[524288]{0:T(1024)(128)(4,1)S(1)}, s32[]{:S(2)}) async-start(s8[4718592]{0:T(1024)(128)(4,1)} %bitcast.15), calls=%async_computation.3 | async-start | bytes 1048576
  6.8 11.7 %copy-start.4 = (f32[1,3,3072]{2,0,1:T(1,128)S(1)}, f32[1,3,3072]{2,0,1:T(1,128)}, u32[]{:S(2)}) copy-start(f32[1,3,3072]{2,0,1:T(1,128)} %param.10) | copy-start | bytes 110596
  6.8 11.8 %copy-start.1 = (bf16[1,384,3072]{2,1,0:T(8,128)(2,1)S(1)}, bf16[1,384,3072]{2,1,0:T(8,128)(2,1)}, u32[]{:S(2)}) copy-start(bf16[1,384,3072]{2,1,0:T(8,128)(2,1)} %x_hbm.1) | copy-start | bytes 7077892
  6.8 19.8 %collective-permute-start.2 = (bf16[384,768]{1,0:T(8,128)(2,1)S(1)}, bf16[384,768]{1,0:T(8,128)(2,1)}, u32[]{:S(2)}, u32[]{:S(2)}) collective-permute-start(bf16[384,768]{1,0:T(8,128)(2,1)S(1)} %convolution_convert_fusion.2.refs_0_), channel_id=1, source_target_pairs={{0,8},{16,24},{8,0},{24,16},{1,9},{17,25},{9,1},{25,17},{2,10},{18... | collective-permute-start | bytes 1769480 | tf_op jit(solution)/shard_map/ppermute | solution.py:345
  9.9 17.6 %collective-permute-start.3 = (bf16[384,768]{1,0:T(8,128)(2,1)S(1)}, bf16[384,768]{1,0:T(8,128)(2,1)}, u32[]{:S(2)}, u32[]{:S(2)}) collective-permute-start(bf16[384,768]{1,0:T(8,128)(2,1)S(1)} %convolution_convert_fusion.2.refs_0_), channel_id=1, source_target_pairs={{8,16},{16,8},{9,17},{17,9},{10,18},{18,10},{11,19},{19,11},{12,20... | collective-permute-start | bytes 1769480 | tf_op jit(solution)/shard_map/ppermute | solution.py:345
  13.4 5.1 %copy-start.7 = (bf16[384,768]{1,0:T(8,128)(2,1)}, bf16[384,768]{1,0:T(8,128)(2,1)S(1)}, u32[]{:S(2)}) copy-start(bf16[384,768]{1,0:T(8,128)(2,1)S(1)} %convolution_convert_fusion.1) | copy-start | bytes 1769476
  13.4 21.4 %collective-permute-start.4 = (bf16[384,512]{1,0:T(8,128)(2,1)S(1)}, bf16[384,512]{1,0:T(8,128)(2,1)}, u32[]{:S(2)}, u32[]{:S(2)}) collective-permute-start(bf16[384,512]{1,0:T(8,128)(2,1)S(1)} %slice.25.refs_0_), channel_id=1, source_target_pairs={{0,8},{16,24},{8,0},{24,16},{1,9},{17,25},{9,1},{25,17},{2,10},{18... | collective-permute-start | bytes 1179656 | tf_op jit(solution)/shard_map/ppermute | solution.py:345
  17.1 17.8 %collective-permute-start.5 = (bf16[384,512]{1,0:T(8,128)(2,1)S(1)}, bf16[384,512]{1,0:T(8,128)(2,1)}, u32[]{:S(2)}, u32[]{:S(2)}) collective-permute-start(bf16[384,512]{1,0:T(8,128)(2,1)S(1)} %slice.25.refs_0_), channel_id=1, source_target_pairs={{8,16},{16,8},{9,17},{17,9},{10,18},{18,10},{11,19},{19,11},{12,20... | collective-permute-start | bytes 1179656 | tf_op jit(solution)/shard_map/ppermute | solution.py:345
  18.5 1.2 %collective-permute-start.1 = (f32[1,1,3072]{2,1,0:T(1,128)S(1)}, f32[1,1,3072]{2,1,0:T(1,128)S(1)}, u32[]{:S(2)}, u32[]{:S(2)}) collective-permute-start(f32[1,1,3072]{2,1,0:T(1,128)S(1)} %slice_bitcast_fusion), channel_id=1, source_target_pairs={{0,4},{4,0},{1,5},{5,1},{2,6},{6,2},{3,7},{7,3},{8,12},{12,8},{9,1... | collective-permute-start | bytes 36872 | tf_op jit(solution)/shard_map/ppermute | solution.py:350
  18.6 8.9 %copy-start.5 = (s32[3,7]{1,0:T(4,128)S(1)}, s32[3,7]{1,0:T(4,128)}, u32[]{:S(2)}) copy-start(s32[3,7]{1,0:T(4,128)} %ids_ref.1) | copy-start | bytes 256
  18.6 8.9 %copy-start.6 = (s32[3]{0:T(128)S(1)}, s32[3]{0:T(128)}, u32[]{:S(2)}) copy-start(s32[3]{0:T(128)} %count_ref.1) | copy-start | bytes 40
  19.7 6.2 %collective-permute-start = (bf16[384,384]{1,0:T(8,128)(2,1)S(1)}, bf16[384,384]{1,0:T(8,128)(2,1)S(1)}, u32[]{:S(2)}, u32[]{:S(2)}) collective-permute-start(bf16[384,384]{1,0:T(8,128)(2,1)S(1)} %dynamic-slice_bitcast_fusion), channel_id=1, source_target_pairs={{0,4},{4,0},{1,5},{5,1},{2,6},{6,2},{3,7},{7,3},{8,12},{12,8},{9,1... | collective-permute-start | bytes 884744 | tf_op jit(solution)/shard_map/ppermute | solution.py:350
  25.9 12.0 %collective-permute-start.7 = (bf16[384,256]{1,0:T(8,128)(2,1)S(1)}, bf16[384,256]{1,0:T(8,128)(2,1)S(1)}, u32[]{:S(2)}, u32[]{:S(2)}) collective-permute-start(bf16[384,256]{1,0:T(8,128)(2,1)S(1)} %slice.26.refs_0_), channel_id=1, source_target_pairs={{0,8},{16,24},{8,0},{24,16},{1,9},{17,25},{9,1},{25,17},{2,10},{18... | collective-permute-start | bytes 589832 | tf_op jit(solution)/shard_map/ppermute | solution.py:345
  26.6 11.2 %collective-permute-start.8 = (bf16[384,256]{1,0:T(8,128)(2,1)S(1)}, bf16[384,256]{1,0:T(8,128)(2,1)S(1)}, u32[]{:S(2)}, u32[]{:S(2)}) collective-permute-start(bf16[384,256]{1,0:T(8,128)(2,1)S(1)} %slice.26.refs_0_), channel_id=1, source_target_pairs={{8,16},{16,8},{9,17},{17,9},{10,18},{18,10},{11,19},{19,11},{12,20... | collective-permute-start | bytes 589832 | tf_op jit(solution)/shard_map/ppermute | solution.py:345
  34.9 5.1 %slice-start = ((s8[4718592]{0:T(1024)(128)(4,1)}), s8[524288]{0:T(1024)(128)(4,1)S(1)}, s32[]{:S(2)}) async-start(s8[4718592]{0:T(1024)(128)(4,1)} %bitcast.11), calls=%async_computation | async-start | bytes 1048576
  37.7 2.2 %collective-permute-start.6 = (bf16[384,512]{1,0:T(8,128)(2,1)S(1)}, bf16[384,512]{1,0:T(8,128)(2,1)S(1)}, u32[]{:S(2)}, u32[]{:S(2)}) collective-permute-start(bf16[384,512]{1,0:T(8,128)(2,1)S(1)} %gather.2.own_ref._), channel_id=1, source_target_pairs={{0,4},{4,0},{1,5},{5,1},{2,6},{6,2},{3,7},{7,3},{8,12},{12,8},{9,1... | collective-permute-start | bytes 1179656 | tf_op jit(solution)/shard_map/ppermute | solution.py:350
  38.8 3.2 %collective-permute-start.9 = (bf16[384,256]{1,0:T(8,128)(2,1)S(1)}, bf16[384,256]{1,0:T(8,128)(2,1)S(1)}, u32[]{:S(2)}, u32[]{:S(2)}) collective-permute-start(bf16[384,256]{1,0:T(8,128)(2,1)S(1)} %gather.3.own_ref), channel_id=1, source_target_pairs={{0,4},{4,0},{1,5},{5,1},{2,6},{6,2},{3,7},{7,3},{8,12},{12,8},{9,1... | collective-permute-start | bytes 589832 | tf_op jit(solution)/shard_map/ppermute | solution.py:350
  43.1 9.0 %collective-permute-start.10 = (bf16[192,768]{1,0:T(8,128)(2,1)S(1)}, bf16[192,768]{1,0:T(8,128)(2,1)S(1)}, u32[]{:S(2)}, u32[]{:S(2)}) collective-permute-start(bf16[192,768]{1,0:T(8,128)(2,1)S(1)} %get-tuple-element.32), channel_id=1, source_target_pairs={{0,1},{1,0},{2,3},{3,2},{4,5},{5,4},{6,7},{7,6},{8,9},{9,8},{10,11... | collective-permute-start | bytes 884744 | tf_op jit(solution)/shard_map/ppermute | solution.py:350
  44.6 9.2 %collective-permute-start.12 = (bf16[192,768]{1,0:T(8,128)(2,1)S(1)}, bf16[192,768]{1,0:T(8,128)(2,1)S(1)}, u32[]{:S(2)}, u32[]{:S(2)}) collective-permute-start(bf16[192,768]{1,0:T(8,128)(2,1)S(1)} %get-tuple-element.34), channel_id=1, source_target_pairs={{0,2},{1,3},{2,0},{3,1},{4,6},{5,7},{6,4},{7,5},{8,10},{9,11},{10,... | collective-permute-start | bytes 884744 | tf_op jit(solution)/shard_map/ppermute | solution.py:350
  52.2 5.2 %collective-permute-start.11 = (bf16[192,384]{1,0:T(8,128)(2,1)S(1)}, bf16[192,384]{1,0:T(8,128)(2,1)S(1)}, u32[]{:S(2)}, u32[]{:S(2)}) collective-permute-start(bf16[192,384]{1,0:T(8,128)(2,1)S(1)} %slice.45), channel_id=1, source_target_pairs={{0,2},{1,3},{2,0},{3,1},{4,6},{5,7},{6,4},{7,5},{8,10},{9,11},{10,... | collective-permute-start | bytes 442376 | tf_op jit(solution)/shard_map/ppermute | solution.py:350
  53.9 5.2 %collective-permute-start.13 = (bf16[192,384]{1,0:T(8,128)(2,1)S(1)}, bf16[192,384]{1,0:T(8,128)(2,1)S(1)}, u32[]{:S(2)}, u32[]{:S(2)}) collective-permute-start(bf16[192,384]{1,0:T(8,128)(2,1)S(1)} %slice.44), channel_id=1, source_target_pairs={{0,1},{1,0},{2,3},{3,2},{4,5},{5,4},{6,7},{7,6},{8,9},{9,8},{10,11... | collective-permute-start | bytes 442376 | tf_op jit(solution)/shard_map/ppermute | solution.py:350
  (3 other events, 4.7 us)

commit v4 on v3

--- a/solution.py
+++ b/solution.py
@@ -10,6 +10,7 @@
 HD = 64
 PAIR = 2 * HD
 FIRST_VALUES = 8 / 12
+NORM_ROWS = (1, 2, 3)
 MIB = 1024 * 1024
 
 
@@ -33,34 +34,60 @@
     return pl.ds(pl.multiple_of(start, 128), size)
 
 
-def norm_kernel(x_ref, mod_ref, h_ref):
-    rows = 64
-    shift = mod_ref[0]
-    scale = 1.0 + mod_ref[1]
-    for step in range(h_ref.shape[0] // rows):
+def norm_kernel(x_hbm, mod_hbm, h_ref, here_ref, there_ref, gate_ref, xb, mod_ref, sems):
+    ntok, width = h_ref.shape
+    rows = ntok // sum(NORM_ROWS)
+    copies, starts, first = [], {}, 0
+    for i, count in enumerate(NORM_ROWS):
+        at = pl.ds(first * rows, count * rows)
+        copies.append(pltpu.make_async_copy(x_hbm.at[0, at], xb.at[at], sems.at[i]))
+        starts[first] = copies[-1]
+        first += count
+    copies.insert(1, pltpu.make_async_copy(mod_hbm, mod_ref, sems.at[len(NORM_ROWS)]))
+    for copy in copies:
+        copy.start()
+    part = here_ref.shape[1]
+    own = lax.axis_index("guid") * (width // 2) + lax.axis_index("tp") * part
+    far = (1 - lax.axis_index("guid")) * (width // 2) + lax.axis_index("tp") * part
+    for step in range(ntok // rows):
+        if step in starts:
+            starts[step].wait()
         at = slice(step * rows, (step + 1) * rows)
-        xf = x_ref[0, at, :].astype(jnp.float32)
+        xf = xb[at, :].astype(jnp.float32)
         cent = xf - jnp.mean(xf, axis=1, keepdims=True)
         var = jnp.mean(cent * cent, axis=1, keepdims=True)
+        if step == 0:
+            copies[1].wait()
+            shift = mod_ref[0]
+            scale = 1.0 + mod_ref[1]
+            gate_ref[...] = mod_ref[2:3]
         h_ref[at, :] = (cent / jnp.sqrt(var + 1e-05) * scale + shift).astype(jnp.bfloat16)
-
-
-def norm(states, modul):
+    here_ref[...] = xb[:, aligned(own, part)]
+    there_ref[...] = xb[:, aligned(far, part)]
+
+
+def norm(states, modul, part):
     _, ntok, width = states.shape
-    block = 128
+    pinned = [pltpu.with_memory_space_constraint(one, pltpu.HBM) for one in (states, modul)]
     return pl.pallas_call(
         norm_kernel,
-        grid=(ntok // block,),
-        in_specs=[
-            pl.BlockSpec((1, block, width), lambda i: (0, i, 0)),
-            pl.BlockSpec((3, 1, width), lambda i: (0, 0, 0)),
+        in_specs=[pl.BlockSpec(memory_space=pl.ANY)] * 2,
+        out_specs=vmem(4),
+        out_shape=[
+            jax.ShapeDtypeStruct((ntok, width), jnp.bfloat16),
+            jax.ShapeDtypeStruct((ntok, part), jnp.bfloat16),
+            jax.ShapeDtypeStruct((ntok, part), jnp.bfloat16),
+            jax.ShapeDtypeStruct((1, 1, width), jnp.float32),
         ],
-        out_specs=pl.BlockSpec((block, width), lambda i: (i, 0)),
-        out_shape=jax.ShapeDtypeStruct((ntok, width), jnp.bfloat16),
+        scratch_shapes=[
+            pltpu.VMEM((ntok, width), jnp.bfloat16),
+            pltpu.VMEM((3, 1, width), jnp.float32),
+            pltpu.SemaphoreType.DMA((len(NORM_ROWS) + 1,)),
+        ],
         compiler_params=params(12),
-        cost_estimate=cost(10 * ntok * width, 4 * ntok * width, ntok),
+        cost_estimate=cost(1e10, 4 * ntok * width, ntok),
         name="norm",
-    )(states, modul)
+    )(*pinned)
 
 
 def ahead_here(distance):
@@ -184,7 +211,7 @@
             jax.ShapeDtypeStruct((items, tile_len, PAIR), jnp.float32),
         ],
         compiler_params=params(24),
-        cost_estimate=cost(4 * ntok * span * width, 2 * ntok * span * width / HD, ntok * span * width / HD),
+        cost_estimate=cost(0, 0),
         name="weigh",
     )(block_ids, block_count, query, *pieces)
 
@@ -203,7 +230,7 @@
         o_ref[rows, columns(pair)] = (by_head(acc, PAIR) * inv_ref[slot]).astype(jnp.bfloat16)
 
 
-def gather(p, inv, after, pieces, first_pair, tiles):
+def gather(p, inv, after, pieces, first_pair, tiles, flops):
     ntok, width = pieces[0].shape
     return pl.pallas_call(
         functools.partial(gather_kernel, tiles, first_pair),
@@ -211,7 +238,7 @@
         out_specs=vmem(1)[0],
         out_shape=jax.ShapeDtypeStruct((ntok, width), jnp.bfloat16),
         compiler_params=params(24),
-        cost_estimate=cost(2e10, 2 * ntok * p.shape[2] * width / HD),
+        cost_estimate=cost(flops, 0),
         name="gather",
     )(p, inv, after, *pieces)
 
@@ -251,50 +278,63 @@
     return [branch * (model // 2) + lax.bitwise_xor(here, p) * part for p in range(4)]
 
 
-def early_kernel(own_ref, oth_ref, w_ref, x_hbm, xo_ref, mod_ref, gate_ref, scale_ref, *refs):
-    y_ref, c_ref, xb, sem = refs
-    part = xb.shape[1]
-    done = own_ref.shape[1]
-    starts = partner_starts(x_hbm.shape[2], part)
-    copy = pltpu.make_async_copy(x_hbm.at[0, :, aligned(starts[0], part)], xb, sem)
-    copy.start()
+def early_kernel(own_ref, w_ref, x_ref, xo_ref, gate_ref, oth_gate_ref, scale_ref, y_ref, c_ref):
+    part = x_ref.shape[1]
+    starts = partner_starts(w_ref.shape[1], part)
     scale = scale_ref[0]
     branch = lax.axis_index("guid")
     mine = jnp.where(branch == 0, scale, 1.0 - scale)
     others = jnp.where(branch == 0, 1.0 - scale, scale)
-    for p in (3, 2, 1, 0):
+    for p in range(4):
         at = aligned(starts[p], part)
         spot = slice(p * part, (p + 1) * part)
-        own_gate = mine * mod_ref[2, :, at]
-        oth_gate = others * gate_ref[0, :, at]
-        c_ref[0:1, spot] = own_gate
-        c_ref[1:2, spot] = oth_gate
-        weight = w_ref[0:done, at]
-        y = own_gate * jnp.dot(own_ref[...], weight, preferred_element_type=jnp.float32)
-        y += oth_gate * jnp.dot(oth_ref[...], weight, preferred_element_type=jnp.float32)
+        gate = mine * gate_ref[0, :, at]
+        c_ref[0:1, spot] = gate
+        c_ref[1:2, spot] = others * oth_gate_ref[0, :, at]
+        weight = w_ref[0 : own_ref.shape[1], at]
+        y = gate * jnp.dot(own_ref[...], weight, preferred_element_type=jnp.float32)
         if p == 0:
-            copy.wait()
-            y += mine * xb[...].astype(jnp.float32) + others * xo_ref[...].astype(jnp.float32)
+            y += mine * x_ref[...].astype(jnp.float32) + others * xo_ref[...].astype(jnp.float32)
         y_ref[:, spot] = y
 
 
-def early(own, oth, w_out, states, x_other, modul, gate_other, scale):
+def early(own, w_out, x_own, x_other, gate_own, gate_other, scale):
     ntok, done = own.shape
     width, model = w_out.shape
-    part = x_other.shape[1]
     return pl.pallas_call(
         early_kernel,
-        in_specs=vmem(3) + [pl.BlockSpec(memory_space=pl.ANY)] + vmem(3) + smem(1),
+        in_specs=vmem(6) + smem(1),
         out_specs=vmem(2),
         out_shape=[
             jax.ShapeDtypeStruct((ntok, model // 2), jnp.float32),
             jax.ShapeDtypeStruct((2, model // 2), jnp.float32),
         ],
-        scratch_shapes=[pltpu.VMEM((ntok, part), jnp.bfloat16), pltpu.SemaphoreType.DMA],
         compiler_params=params(16),
-        cost_estimate=cost(2 * ntok * model * done, width * model + 4 * ntok * model),
+        cost_estimate=cost(0, 0),
         name="early",
-    )(own, oth, w_out, states, x_other, modul, gate_other, scale)
+    )(own, w_out, x_own, x_other, gate_own, gate_other, scale)
+
+
+def middle_kernel(early_ref, oth_ref, w_ref, c_ref, y_ref):
+    part = early_ref.shape[1] // 4
+    starts = partner_starts(w_ref.shape[1], part)
+    for p in range(4):
+        cols = slice(p * part, (p + 1) * part)
+        weight = w_ref[0 : oth_ref.shape[1], aligned(starts[p], part)]
+        added = jnp.dot(oth_ref[...], weight, preferred_element_type=jnp.float32)
+        y_ref[:, cols] = early_ref[:, cols] + c_ref[1:2, cols] * added
+
+
+def middle(sofar, oth, w_out, coef):
+    return pl.pallas_call(
+        middle_kernel,
+        in_specs=vmem(4),
+        out_specs=vmem(1)[0],
+        out_shape=jax.ShapeDtypeStruct(sofar.shape, jnp.float32),
+        compiler_params=params(16),
+        cost_estimate=cost(2 * sofar.shape[0] * sofar.shape[1] * oth.shape[1], 0),
+        name="middle",
+    )(sofar, oth, w_out, coef)
 
 
 def close_kernel(early_ref, own_ref, oth_ref, w_ref, c_ref, keep_a, keep_b, send_a, send_b):
@@ -356,14 +396,12 @@
     _, ntok, model = hidden_states.shape
     tiles = block_ids.shape[0]
     width = w_query.shape[1]
-    branch = lax.axis_index("guid")
-    tp_here = lax.axis_index("tp")
     reach_dev = min(4, (lax.axis_size("seq") - 1) // 2)
     part = model // (2 * lax.axis_size("tp"))
     cut = int(width * FIRST_VALUES) // PAIR * PAIR
     modul = jnp.transpose(modulation, (1, 0, 2))
 
-    h = norm(hidden_states, modul)
+    h, x_own, x_there, gate_own = norm(hidden_states, modul, part)
 
     def project(source, weight):
         return jnp.dot(source, weight, preferred_element_type=jnp.float32).astype(jnp.bfloat16)
@@ -376,28 +414,26 @@
 
     key, h = lax.optimization_barrier((project(h, w_key), h))
     keys = near(key)
-    value, h = lax.optimization_barrier((project(h, w_value), h))
+    value, query = lax.optimization_barrier((project(h, w_value), project(h, w_query)))
     values = [near(value[:, :cut]), near(value[:, cut:])]
-    query = project(h, w_query)
-
-    there = (1 - branch) * (model // 2) + tp_here * part
-    x_other = crossed(lax.dynamic_slice_in_dim(hidden_states[0], there, part, 1), "guid", 1)
-    gate_other = crossed(modul[2:3], "guid", 1)
+
+    value, x_there, gate_own = lax.optimization_barrier((value, x_there, gate_own))
+    x_other = crossed(x_there, "guid", 1)
+    gate_other = crossed(gate_own, "guid", 1)
     query, x_other, gate_other = lax.optimization_barrier((query, x_other, gate_other))
 
     def finish(at, group, after):
         if reach_dev == 1:
-            return gather(*weights, after, group, at.start // PAIR, tiles)
+            return gather(*weights, after, group, at.start // PAIR, tiles, 2e10 if at.start else 0)
         return attend(block_ids, block_count, query[:, at], [k[:, at] for k in keys], group)
 
     if reach_dev == 1:
         span = (2 * tiles + 1) * (ntok // tiles)
         weights = weigh(block_ids, block_count, query, keys, span)
     first = finish(slice(0, cut), values[0], query)
-    last = finish(slice(cut, width), values[1], first)
-    sofar, coef = early(
-        first, crossed(first, "guid", 1), w_out, hidden_states, x_other, modul, gate_other, guidance
-    )
+    sofar, coef = early(first, w_out, x_own, x_other, gate_own, gate_other, guidance)
+    last = finish(slice(cut, width), values[1], coef)
+    sofar = middle(sofar, crossed(first, "guid", 1), w_out, coef)
     keep_a, keep_b, send_a, send_b = close(sofar, last, crossed(last, "guid", 1), w_out, coef)
     got_a = crossed(send_a, "tp", 1)
     got_b = crossed(send_b, "tp", 2)

time: 60.4 us -> 57.1 us (0.945)
  the two profiles are of different devices: /device:TPU:0 before, /device:TPU:16 now
where the time goes in v4:
time: 57.1 us; the launch traced here: 56.9 us
  starting transfers between devices  17 us (30%)
  waiting for transfers between devices  15.9 us (28%)
  Pallas kernels  15.3 us (27%)
  matrix products  6.05 us (11%)
  between operations  0.94 us (2%)
  other arithmetic  0.9 us (2%)
  local copies, waits for them, and re-layouts  0.8 us (1%)
    ppermute x8, waiting for transfers between devices, crossed(): lax.ppermute(value, axis, [(i, i ^ bit) for i in range(lax.axis_size(axis...  11 us
    ppermute x6, starting transfers between devices, neighbours(): out.append(lax.ppermute(value, 'seq', route))  10.1 us
    ppermute x8, starting transfers between devices, crossed(): lax.ppermute(value, axis, [(i, i ^ bit) for i in range(lax.axis_size(axis...  6.9 us
    pallas_call x1, Pallas kernels, weigh(): pl.pallas_call(functools.partial(weigh_kernel, tiles, True), in_specs=sme...  6.78 us
    dot_general x3, matrix products, project(): jnp.dot(source, weight, preferred_element_type=jnp.float32)  6.05 us
    ppermute x6, waiting for transfers between devices, neighbours(): out.append(lax.ppermute(value, 'seq', route))  4.85 us
    pallas_call x1, Pallas kernels, norm(): pl.pallas_call(norm_kernel, in_specs=[pl.BlockSpec(memory_space=pl.ANY)]...  2.97 us
    pallas_call x2, Pallas kernels, gather(): pl.pallas_call(functools.partial(gather_kernel, tiles, first_pair), in_sp...  2.5 us
  transfers between devices with their start and end apart: 14, of which 8 were waited for; matrix products, arithmetic and copies ran while one was open for 7% of the time, Pallas kernels for 20%

profile of v4, /device:TPU:16, one launch (start us, length us, event | category | flops | bytes accessed | tf_op | source)
XLA Modules:
  0.0 56.9 jit_solution(13078377319157256691)
XLA Ops:
  0.0 3.0 %norm.1 = (bf16[384,3072]{1,0:T(8,128)(2,1)S(1)}, bf16[384,384]{1,0:T(8,128)(2,1)S(1)}, bf16[384,384]{1,0:T(8,128)(2,1)S(1)}, f32[1,1,3072]{2,1,0:T(1,128)S(1)}) custom-call(bf16[1,384,3072]{2,1,0:T(8,128)(2,1)} %x_hbm.1, f32[3,1,3072]{2,1,0:T(1,128)} %bitcast.11), custom_call_target="tpu_custom_call" | custom-call | flops 10000000000 | bytes 4718592 | tf_op jit(solution)/shard_map/norm/pallas_call | solution.py:72
  3.1 2.0 %convolution_convert_fusion.2.refs_0_ = bf16[384,768]{1,0:T(8,128)(2,1)S(1)} fusion(bf16[384,3072]{1,0:T(8,128)(2,1)S(1)} %get-tuple-element.27, bf16[3072,768]{1,0:T(8,128)(2,1)S(1)} %copy-done.2), kind=kOutput, calls=%fused_computation.2 | convolution fusion | flops 1812234240 | bytes 7667712 | tf_op jit(solution)/shard_map/dot_general | solution.py:407
  5.1 1.6 %collective-permute-start.2 = (bf16[384,768]{1,0:T(8,128)(2,1)S(1)}, bf16[384,768]{1,0:T(8,128)(2,1)S(1)}, u32[]{:S(2)}, u32[]{:S(2)}) collective-permute-start(bf16[384,768]{1,0:T(8,128)(2,1)S(1)} %convolution_convert_fusion.2.refs_0_), channel_id=1, source_target_pairs={{0,8},{16,24},{8,0},{24,16},{1,9},{17,25},{9,1},{25,17},{2,10},{18... | collective-permute-start | bytes 1769480 | tf_op jit(solution)/shard_map/ppermute | solution.py:385
  6.7 1.9 %collective-permute-start.3 = (bf16[384,768]{1,0:T(8,128)(2,1)S(1)}, bf16[384,768]{1,0:T(8,128)(2,1)S(1)}, u32[]{:S(2)}, u32[]{:S(2)}) collective-permute-start(bf16[384,768]{1,0:T(8,128)(2,1)S(1)} %convolution_convert_fusion.2.refs_0_), channel_id=1, source_target_pairs={{8,16},{16,8},{9,17},{17,9},{10,18},{18,10},{11,19},{19,11},{12,20... | collective-permute-start | bytes 1769480 | tf_op jit(solution)/shard_map/ppermute | solution.py:385
  8.7 2.0 %convolution_convert_fusion.q_ref._ = bf16[384,768]{1,0:T(8,128)(2,1)S(1)} fusion(bf16[384,3072]{1,0:T(8,128)(2,1)S(1)} %get-tuple-element.27, bf16[3072,768]{1,0:T(8,128)(2,1)S(1)} %copy-done.3), kind=kOutput, calls=%fused_computation | convolution fusion | flops 1812234240 | bytes 7667712 | tf_op jit(solution)/shard_map/dot_general | solution.py:407
  10.7 2.0 %convolution_convert_fusion.1 = bf16[384,768]{1,0:T(8,128)(2,1)S(1)} fusion(bf16[384,3072]{1,0:T(8,128)(2,1)S(1)} %get-tuple-element.27, bf16[3072,768]{1,0:T(8,128)(2,1)S(1)} %bitcast.10), kind=kOutput, calls=%fused_computation.1 | convolution fusion | flops 1812234240 | bytes 7667712 | tf_op jit(solution)/shard_map/dot_general | solution.py:407
  13.5 1.0 %collective-permute-done.1.oth_gate_ref = f32[1,1,3072]{2,1,0:T(1,128)S(1)} collective-permute-done((f32[1,1,3072]{2,1,0:T(1,128)S(1)}, f32[1,1,3072]{2,1,0:T(1,128)S(1)}, u32[]{:S(2)}, u32[]{:S(2)}) %collective-permute-start.1) | collective-permute-done | bytes 12320 | tf_op jit(solution)/shard_map/ppermute | solution.py:390
  14.4 3.9 %collective-permute-start.5 = (bf16[384,512]{1,0:T(8,128)(2,1)S(1)}, bf16[384,512]{1,0:T(8,128)(2,1)S(1)}, u32[]{:S(2)}, u32[]{:S(2)}) collective-permute-start(bf16[384,512]{1,0:T(8,128)(2,1)S(1)} %slice.20.refs_0_), channel_id=1, source_target_pairs={{8,16},{16,8},{9,17},{17,9},{10,18},{18,10},{11,19},{19,11},{12,20... | collective-permute-start | bytes 1179656 | tf_op jit(solution)/shard_map/ppermute | solution.py:385
  18.5 2.9 %collective-permute-done.2.refs_1_ = bf16[384,768]{1,0:T(8,128)(2,1)S(1)} collective-permute-done((bf16[384,768]{1,0:T(8,128)(2,1)S(1)}, bf16[384,768]{1,0:T(8,128)(2,1)S(1)}, u32[]{:S(2)}, u32[]{:S(2)}) %collective-permute-start.2) | collective-permute-done | bytes 589856 | tf_op jit(solution)/shard_map/ppermute | solution.py:385
  21.4 2.5 %collective-permute-start.8 = (bf16[384,256]{1,0:T(8,128)(2,1)S(1)}, bf16[384,256]{1,0:T(8,128)(2,1)S(1)}, u32[]{:S(2)}, u32[]{:S(2)}) collective-permute-start(bf16[384,256]{1,0:T(8,128)(2,1)S(1)} %slice.21.refs_0_), channel_id=1, source_target_pairs={{8,16},{16,8},{9,17},{17,9},{10,18},{18,10},{11,19},{19,11},{12,20... | collective-permute-start | bytes 589832 | tf_op jit(solution)/shard_map/ppermute | solution.py:385
  24.9 6.8 %weigh.1 = (bf16[18,256,896]{2,1,0:T(8,128)(2,1)S(1)}, f32[18,128,128]{2,1,0:T(8,128)S(1)}) custom-call(s32[3,7]{1,0:T(4,128)S(1)} %copy-done, s32[3]{0:T(128)S(1)} %copy-done.1, bf16[384,768]{1,0:T(8,128)(2,1)S(1)} %convolution_convert_fusion.q_ref._, bf16[384,768]{1,0:T(8,128)(2,1)S(1)} %convolution_convert_fusion.2.refs_0_, ...), custom_call_target="tpu_custom_call" | custom-call | tf_op jit(solution)/shard_map/weigh/pallas_call | solution.py:205
  31.7 1.6 %collective-permute-done.5.refs_2_ = bf16[384,512]{1,0:T(8,128)(2,1)S(1)} collective-permute-done((bf16[384,512]{1,0:T(8,128)(2,1)S(1)}, bf16[384,512]{1,0:T(8,128)(2,1)S(1)}, u32[]{:S(2)}, u32[]{:S(2)}) %collective-permute-start.5) | collective-permute-done | bytes 393248 | tf_op jit(solution)/shard_map/ppermute | solution.py:385
  33.3 1.6 %gather.2.own_ref = bf16[384,512]{1,0:T(8,128)(2,1)S(1)} custom-call(bf16[18,256,896]{2,1,0:T(8,128)(2,1)S(1)} %get-tuple-element.36.p_ref, f32[18,128,128]{2,1,0:T(8,128)S(1)} %get-tuple-element.37.inv_ref, bf16[384,768]{1,0:T(8,128)(2,1)S(1)} %convolution_convert_fusion.q_ref._, bf16[384,512]{1,0:T(8,128)(2,1)S(1)} %slice.20.refs_0_, ...), custom_call_target="tpu_custom_call" | custom-call | tf_op jit(solution)/shard_map/gather/pallas_call | solution.py:235
  35.6 1.0 %early.1 = (f32[384,1536]{1,0:T(8,128)S(1)}, f32[2,1536]{1,0:T(2,128)S(1)}) custom-call(bf16[384,512]{1,0:T(8,128)(2,1)S(1)} %gather.2.own_ref, bf16[768,3072]{1,0:T(8,128)(2,1)S(1)} %bitcast.8, bf16[384,384]{1,0:T(8,128)(2,1)S(1)} %get-tuple-element.38.x_ref, bf16[384,384]{1,0:T(8,128)(2,1)S(1)} %collective-permute-done.xo_ref, ...), custom_call_target="tpu_custom_call" | custom-call | tf_op jit(solution)/shard_map/early/pallas_call | solution.py:304
  36.6 0.9 %gather.3.own_ref = bf16[384,256]{1,0:T(8,128)(2,1)S(1)} custom-call(bf16[18,256,896]{2,1,0:T(8,128)(2,1)S(1)} %get-tuple-element.36.p_ref, f32[18,128,128]{2,1,0:T(8,128)S(1)} %get-tuple-element.37.inv_ref, f32[2,1536]{1,0:T(2,128)S(1)} %get-tuple-element.42.c_ref._, bf16[384,256]{1,0:T(8,128)(2,1)S(1)} %slice.21.refs_0_, ...), custom_call_target="tpu_custom_call" | custom-call | flops 20000000000 | tf_op jit(solution)/shard_map/gather/pallas_call | solution.py:235
  37.6 1.0 %middle.1.early_ref = f32[384,1536]{1,0:T(8,128)S(1)} custom-call(f32[384,1536]{1,0:T(8,128)S(1)} %get-tuple-element.41.early_ref, bf16[384,512]{1,0:T(8,128)(2,1)S(1)} %collective-permute-done.6.oth_ref, bf16[768,3072]{1,0:T(8,128)(2,1)S(1)} %bitcast.8, f32[2,1536]{1,0:T(2,128)S(1)} %get-tuple-element.42.c_ref._), custom_call_target="tpu_custom_call" | custom-call | flops 603979776 | tf_op jit(solution)/shard_map/middle/pallas_call | solution.py:329
  39.1 1.0 %close.1 = (f32[192,768]{1,0:T(8,128)S(1)}, f32[192,768]{1,0:T(8,128)S(1)}, bf16[192,768]{1,0:T(8,128)(2,1)S(1)}, bf16[192,768]{1,0:T(8,128)(2,1)S(1)}) custom-call(f32[384,1536]{1,0:T(8,128)S(1)} %middle.1.early_ref, bf16[384,256]{1,0:T(8,128)(2,1)S(1)} %gather.3.own_ref, bf16[384,256]{1,0:T(8,128)(2,1)S(1)} %collective-permute-done.9.oth_ref, ...), custom_call_target="tpu_custom_call" | custom-call | flops 603979776 | bytes 4718592 | tf_op jit(solution)/shard_map/close/pallas_call | solution.py:368
  40.1 1.5 %collective-permute-start.10 = (bf16[192,768]{1,0:T(8,128)(2,1)S(1)}, bf16[192,768]{1,0:T(8,128)(2,1)S(1)}, u32[]{:S(2)}, u32[]{:S(2)}) collective-permute-start(bf16[192,768]{1,0:T(8,128)(2,1)S(1)} %get-tuple-element.44), channel_id=1, source_target_pairs={{0,1},{1,0},{2,3},{3,2},{4,5},{5,4},{6,7},{7,6},{8,9},{9,8},{10,11... | collective-permute-start | bytes 884744 | tf_op jit(solution)/shard_map/ppermute | solution.py:390
  41.6 1.5 %collective-permute-start.12 = (bf16[192,768]{1,0:T(8,128)(2,1)S(1)}, bf16[192,768]{1,0:T(8,128)(2,1)S(1)}, u32[]{:S(2)}, u32[]{:S(2)}) collective-permute-start(bf16[192,768]{1,0:T(8,128)(2,1)S(1)} %get-tuple-element.46), channel_id=1, source_target_pairs={{0,2},{1,3},{2,0},{3,1},{4,6},{5,7},{6,4},{7,5},{8,10},{9,11},{10,... | collective-permute-start | bytes 884744 | tf_op jit(solution)/shard_map/ppermute | solution.py:390
  43.2 6.1 %collective-permute-done.10 = bf16[192,768]{1,0:T(8,128)(2,1)S(1)} collective-permute-done((bf16[192,768]{1,0:T(8,128)(2,1)S(1)}, bf16[192,768]{1,0:T(8,128)(2,1)S(1)}, u32[]{:S(2)}, u32[]{:S(2)}) %collective-permute-start.10) | collective-permute-done | bytes 294944 | tf_op jit(solution)/shard_map/ppermute | solution.py:390
  49.3 1.6 %collective-permute-start.11 = (bf16[192,384]{1,0:T(8,128)(2,1)S(1)}, bf16[192,384]{1,0:T(8,128)(2,1)S(1)}, u32[]{:S(2)}, u32[]{:S(2)}) collective-permute-start(bf16[192,384]{1,0:T(8,128)(2,1)S(1)} %slice.39), channel_id=1, source_target_pairs={{0,2},{1,3},{2,0},{3,1},{4,6},{5,7},{6,4},{7,5},{8,10},{9,11},{10,... | collective-permute-start | bytes 442376 | tf_op jit(solution)/shard_map/ppermute | solution.py:390
  50.9 1.6 %collective-permute-start.13 = (bf16[192,384]{1,0:T(8,128)(2,1)S(1)}, bf16[192,384]{1,0:T(8,128)(2,1)S(1)}, u32[]{:S(2)}, u32[]{:S(2)}) collective-permute-start(bf16[192,384]{1,0:T(8,128)(2,1)S(1)} %slice.38), channel_id=1, source_target_pairs={{0,1},{1,0},{2,3},{3,2},{4,5},{5,4},{6,7},{7,6},{8,9},{9,8},{10,11... | collective-permute-start | bytes 442376 | tf_op jit(solution)/shard_map/ppermute | solution.py:390
  52.5 2.0 %collective-permute-done.11 = bf16[192,384]{1,0:T(8,128)(2,1)S(1)} collective-permute-done((bf16[192,384]{1,0:T(8,128)(2,1)S(1)}, bf16[192,384]{1,0:T(8,128)(2,1)S(1)}, u32[]{:S(2)}, u32[]{:S(2)}) %collective-permute-start.11) | collective-permute-done | bytes 147488 | tf_op jit(solution)/shard_map/ppermute | solution.py:390
  54.5 1.6 %collective-permute-done.13 = bf16[192,384]{1,0:T(8,128)(2,1)S(1)} collective-permute-done((bf16[192,384]{1,0:T(8,128)(2,1)S(1)}, bf16[192,384]{1,0:T(8,128)(2,1)S(1)}, u32[]{:S(2)}, u32[]{:S(2)}) %collective-permute-start.13) | collective-permute-done | bytes 147488 | tf_op jit(solution)/shard_map/ppermute | solution.py:390
  (41 shorter events, 3.3 us)
Async XLA Ops:
  0.0 3.1 %copy-start.2 = (bf16[3072,768]{1,0:T(8,128)(2,1)S(1)}, bf16[3072,768]{1,0:T(8,128)(2,1)}, u32[]{:S(2)}) copy-start(bf16[3072,768]{1,0:T(8,128)(2,1)} %param.12) | copy-start | bytes 14155780
  3.1 5.6 %copy-start.3 = (bf16[3072,768]{1,0:T(8,128)(2,1)S(1)}, bf16[3072,768]{1,0:T(8,128)(2,1)}, u32[]{:S(2)}) copy-start(bf16[3072,768]{1,0:T(8,128)(2,1)} %param.11) | copy-start | bytes 14155780
  3.1 7.6 %slice-start.2 = ((s8[4718592]{0:T(1024)(128)(4,1)}), s8[4194304]{0:T(1024)(128)(4,1)S(1)}, s32[]{:S(2)}) async-start(s8[4718592]{0:T(1024)(128)(4,1)} %bitcast.9), calls=%async_computation.2 | async-start | bytes 8388608
  5.1 5.6 %slice-start.3 = ((s8[4718592]{0:T(1024)(128)(4,1)}), s8[524288]{0:T(1024)(128)(4,1)S(1)}, s32[]{:S(2)}) async-start(s8[4718592]{0:T(1024)(128)(4,1)} %bitcast.9), calls=%async_computation.3 | async-start | bytes 1048576
  5.1 16.3 %collective-permute-start.2 = (bf16[384,768]{1,0:T(8,128)(2,1)S(1)}, bf16[384,768]{1,0:T(8,128)(2,1)S(1)}, u32[]{:S(2)}, u32[]{:S(2)}) collective-permute-start(bf16[384,768]{1,0:T(8,128)(2,1)S(1)} %convolution_convert_fusion.2.refs_0_), channel_id=1, source_target_pairs={{0,8},{16,24},{8,0},{24,16},{1,9},{17,25},{9,1},{25,17},{2,10},{18... | collective-permute-start | bytes 1769480 | tf_op jit(solution)/shard_map/ppermute | solution.py:385
  6.7 18.1 %collective-permute-start.3 = (bf16[384,768]{1,0:T(8,128)(2,1)S(1)}, bf16[384,768]{1,0:T(8,128)(2,1)S(1)}, u32[]{:S(2)}, u32[]{:S(2)}) collective-permute-start(bf16[384,768]{1,0:T(8,128)(2,1)S(1)} %convolution_convert_fusion.2.refs_0_), channel_id=1, source_target_pairs={{8,16},{16,8},{9,17},{17,9},{10,18},{18,10},{11,19},{19,11},{12,20... | collective-permute-start | bytes 1769480 | tf_op jit(solution)/shard_map/ppermute | solution.py:385
  10.7 14.2 %copy-start = (s32[3,7]{1,0:T(4,128)S(1)}, s32[3,7]{1,0:T(4,128)}, u32[]{:S(2)}) copy-start(s32[3,7]{1,0:T(4,128)} %ids_ref.1) | copy-start | bytes 256
  10.7 14.1 %copy-start.1 = (s32[3]{0:T(128)S(1)}, s32[3]{0:T(128)}, u32[]{:S(2)}) copy-start(s32[3]{0:T(128)} %count_ref.1) | copy-start | bytes 40
  12.8 5.6 %collective-permute-start = (bf16[384,384]{1,0:T(8,128)(2,1)S(1)}, bf16[384,384]{1,0:T(8,128)(2,1)S(1)}, u32[]{:S(2)}, u32[]{:S(2)}) collective-permute-start(bf16[384,384]{1,0:T(8,128)(2,1)S(1)} %get-tuple-element.32), channel_id=1, source_target_pairs={{0,4},{4,0},{1,5},{5,1},{2,6},{6,2},{3,7},{7,3},{8,12},{12,8},{9,1... | collective-permute-start | bytes 884744 | tf_op jit(solution)/shard_map/ppermute | solution.py:390
  12.8 1.6 %collective-permute-start.1 = (f32[1,1,3072]{2,1,0:T(1,128)S(1)}, f32[1,1,3072]{2,1,0:T(1,128)S(1)}, u32[]{:S(2)}, u32[]{:S(2)}) collective-permute-start(f32[1,1,3072]{2,1,0:T(1,128)S(1)} %get-tuple-element.33.gate_ref), channel_id=1, source_target_pairs={{0,4},{4,0},{1,5},{5,1},{2,6},{6,2},{3,7},{7,3},{8,12},{12,8},{9,1... | collective-permute-start | bytes 36872 | tf_op jit(solution)/shard_map/ppermute | solution.py:390
  13.4 18.3 %collective-permute-start.4 = (bf16[384,512]{1,0:T(8,128)(2,1)S(1)}, bf16[384,512]{1,0:T(8,128)(2,1)S(1)}, u32[]{:S(2)}, u32[]{:S(2)}) collective-permute-start(bf16[384,512]{1,0:T(8,128)(2,1)S(1)} %slice.20.refs_0_), channel_id=1, source_target_pairs={{0,8},{16,24},{8,0},{24,16},{1,9},{17,25},{9,1},{25,17},{2,10},{18... | collective-permute-start | bytes 1179656 | tf_op jit(solution)/shard_map/ppermute | solution.py:385
  14.4 18.9 %collective-permute-start.5 = (bf16[384,512]{1,0:T(8,128)(2,1)S(1)}, bf16[384,512]{1,0:T(8,128)(2,1)S(1)}, u32[]{:S(2)}, u32[]{:S(2)}) collective-permute-start(bf16[384,512]{1,0:T(8,128)(2,1)S(1)} %slice.20.refs_0_), channel_id=1, source_target_pairs={{8,16},{16,8},{9,17},{17,9},{10,18},{18,10},{11,19},{19,11},{12,20... | collective-permute-start | bytes 1179656 | tf_op jit(solution)/shard_map/ppermute | solution.py:385
  18.4 18.2 %collective-permute-start.7 = (bf16[384,256]{1,0:T(8,128)(2,1)S(1)}, bf16[384,256]{1,0:T(8,128)(2,1)S(1)}, u32[]{:S(2)}, u32[]{:S(2)}) collective-permute-start(bf16[384,256]{1,0:T(8,128)(2,1)S(1)} %slice.21.refs_0_), channel_id=1, source_target_pairs={{0,8},{16,24},{8,0},{24,16},{1,9},{17,25},{9,1},{25,17},{2,10},{18... | collective-permute-start | bytes 589832 | tf_op jit(solution)/shard_map/ppermute | solution.py:385
  21.4 15.3 %collective-permute-start.8 = (bf16[384,256]{1,0:T(8,128)(2,1)S(1)}, bf16[384,256]{1,0:T(8,128)(2,1)S(1)}, u32[]{:S(2)}, u32[]{:S(2)}) collective-permute-start(bf16[384,256]{1,0:T(8,128)(2,1)S(1)} %slice.21.refs_0_), channel_id=1, source_target_pairs={{8,16},{16,8},{9,17},{17,9},{10,18},{18,10},{11,19},{19,11},{12,20... | collective-permute-start | bytes 589832 | tf_op jit(solution)/shard_map/ppermute | solution.py:385
  33.3 2.2 %slice-start = ((s8[4718592]{0:T(1024)(128)(4,1)}), s8[4194304]{0:T(1024)(128)(4,1)S(1)}, s32[]{:S(2)}) async-start(s8[4718592]{0:T(1024)(128)(4,1)} %bitcast.7), calls=%async_computation | async-start | bytes 8388608
  33.3 2.3 %slice-start.1 = ((s8[4718592]{0:T(1024)(128)(4,1)}), s8[524288]{0:T(1024)(128)(4,1)S(1)}, s32[]{:S(2)}) async-start(s8[4718592]{0:T(1024)(128)(4,1)} %bitcast.7), calls=%async_computation.1 | async-start | bytes 1048576
  34.9 2.7 %collective-permute-start.6 = (bf16[384,512]{1,0:T(8,128)(2,1)S(1)}, bf16[384,512]{1,0:T(8,128)(2,1)S(1)}, u32[]{:S(2)}, u32[]{:S(2)}) collective-permute-start(bf16[384,512]{1,0:T(8,128)(2,1)S(1)} %gather.2.own_ref), channel_id=1, source_target_pairs={{0,4},{4,0},{1,5},{5,1},{2,6},{6,2},{3,7},{7,3},{8,12},{12,8},{9,1... | collective-permute-start | bytes 1179656 | tf_op jit(solution)/shard_map/ppermute | solution.py:390
  37.5 1.5 %collective-permute-start.9 = (bf16[384,256]{1,0:T(8,128)(2,1)S(1)}, bf16[384,256]{1,0:T(8,128)(2,1)S(1)}, u32[]{:S(2)}, u32[]{:S(2)}) collective-permute-start(bf16[384,256]{1,0:T(8,128)(2,1)S(1)} %gather.3.own_ref), channel_id=1, source_target_pairs={{0,4},{4,0},{1,5},{5,1},{2,6},{6,2},{3,7},{7,3},{8,12},{12,8},{9,1... | collective-permute-start | bytes 589832 | tf_op jit(solution)/shard_map/ppermute | solution.py:390
  40.1 9.1 %collective-permute-start.10 = (bf16[192,768]{1,0:T(8,128)(2,1)S(1)}, bf16[192,768]{1,0:T(8,128)(2,1)S(1)}, u32[]{:S(2)}, u32[]{:S(2)}) collective-permute-start(bf16[192,768]{1,0:T(8,128)(2,1)S(1)} %get-tuple-element.44), channel_id=1, source_target_pairs={{0,1},{1,0},{2,3},{3,2},{4,5},{5,4},{6,7},{7,6},{8,9},{9,8},{10,11... | collective-permute-start | bytes 884744 | tf_op jit(solution)/shard_map/ppermute | solution.py:390
  41.6 9.2 %collective-permute-start.12 = (bf16[192,768]{1,0:T(8,128)(2,1)S(1)}, bf16[192,768]{1,0:T(8,128)(2,1)S(1)}, u32[]{:S(2)}, u32[]{:S(2)}) collective-permute-start(bf16[192,768]{1,0:T(8,128)(2,1)S(1)} %get-tuple-element.46), channel_id=1, source_target_pairs={{0,2},{1,3},{2,0},{3,1},{4,6},{5,7},{6,4},{7,5},{8,10},{9,11},{10,... | collective-permute-start | bytes 884744 | tf_op jit(solution)/shard_map/ppermute | solution.py:390
  49.3 5.2 %collective-permute-start.11 = (bf16[192,384]{1,0:T(8,128)(2,1)S(1)}, bf16[192,384]{1,0:T(8,128)(2,1)S(1)}, u32[]{:S(2)}, u32[]{:S(2)}) collective-permute-start(bf16[192,384]{1,0:T(8,128)(2,1)S(1)} %slice.39), channel_id=1, source_target_pairs={{0,2},{1,3},{2,0},{3,1},{4,6},{5,7},{6,4},{7,5},{8,10},{9,11},{10,... | collective-permute-start | bytes 442376 | tf_op jit(solution)/shard_map/ppermute | solution.py:390
  50.9 5.2 %collective-permute-start.13 = (bf16[192,384]{1,0:T(8,128)(2,1)S(1)}, bf16[192,384]{1,0:T(8,128)(2,1)S(1)}, u32[]{:S(2)}, u32[]{:S(2)}) collective-permute-start(bf16[192,384]{1,0:T(8,128)(2,1)S(1)} %slice.38), channel_id=1, source_target_pairs={{0,1},{1,0},{2,3},{3,2},{4,5},{5,4},{6,7},{7,6},{8,9},{9,8},{10,11... | collective-permute-start | bytes 442376 | tf_op jit(solution)/shard_map/ppermute | solution.py:390
